TPU v7x, 32 devices: a whole 2x2x4 slice. The times are simulated.
32 devices in a mesh: rows: 8 (over z, y), cols: 4 (over x, core).
Axes of the slice: x: 2, y: 2, z: 4, core: 2. Of those that a mesh axis runs over, the one named last changes fastest.
Arguments:
- features: float32 [8192, 4, 4, 256], P('rows', None, 'cols'), may hold values from -6 to 6
Outputs:
- factor_rows: float32 [512, 4, 4, 256], P(None, None, 'cols')
- basis: float32 [8192, 2, 256], P('rows')
- trailing: float32 [8192, 4, 4, 256], P('rows', None, 'cols')
All inputs are finite; a program needn't handle non-finite values.
Results may differ from a plain program's by a relative error of at most 0.0003.
Values sent between devices are 32-bit elements; how exact they have to be, the bound alone decides.
No kernel may reach another device: no remote copies, remote signals or barrier semaphores. Data moves between devices by JAX's collectives and lax.ppermute only.
A program may use at most 64 MiB of HBM per device.

v0:
```python
import jax
import jax.numpy as jnp
from jax import lax
from jax.sharding import PartitionSpec as P

HIGHEST = lax.Precision.HIGHEST


def broadcast(array, axis, root):
    mine = lax.axis_index(axis) == root
    return lax.psum(jnp.where(mine, array, jnp.zeros_like(array)), axis)


def product(left, right):
    return jnp.dot(left, right, precision=HIGHEST)


def lower_solve(gram, panel):
    lower = jnp.linalg.cholesky(gram)
    solved = lax.linalg.triangular_solve(lower, panel.T, left_side=True, lower=True).T
    return (solved, lower)


def single_pass(panel):
    gram = lax.psum(product(panel.T, panel), "rows")
    return lower_solve(gram, panel)[0]


def send_basis(basis, owner):
    return broadcast(basis, "cols", owner)


def panel_basis(panel, owner):
    return send_basis(single_pass(panel), owner)


def factor_project(panel, owner, block):
    basis = panel_basis(panel, owner)
    return (basis, lax.psum(product(basis.T, block), "rows"))


def on_device(features):
    rows_dev = features.shape[0]
    pan_dev = features.shape[1]
    width = features.shape[3]
    local = features.reshape(rows_dev, pan_dev * width)
    first_cols = local[:, :width]
    basis_a, proj_a = factor_project(first_cols, 0, local)
    updated = local - product(basis_a, proj_a)
    basis_b, proj_b = factor_project(updated[:, :width], 1, updated)
    final = updated - product(basis_b, proj_b)
    factor_rows = jnp.concatenate([proj_a, proj_b], axis=0).reshape(2 * width, pan_dev, 1, width)
    basis = jnp.stack([basis_a, basis_b], axis=1)
    return (factor_rows, basis, final.reshape(rows_dev, pan_dev, 1, width))


def solution(mesh):
    placed = (P("rows", None, "cols", None),)
    return jax.shard_map(
        on_device,
        mesh=mesh,
        in_specs=placed,
        out_specs=(
            P(None, None, "cols", None),
            P("rows", None, None),
            P("rows", None, "cols", None),
        ),
        check_vma=False,
    )
```

profile of v0, /device:TPU:0, one launch (start us, length us, event | category | flops | bytes accessed | tf_op | source)
XLA Modules:
  0.0 582.0 jit_solution(5204747491281987344)
XLA Ops:
  7.2 10.9 %copy.4 = f32[1024,4,1,256]{0,3,1,2:T(8,128)} copy(f32[1024,4,1,256]{3,2,1,0:T(1,128)} %param.4) | data formatting | bytes 8388608 | tf_op args[0]
  18.1 3.3 fusion.4
  22.8 72.0 %all-reduce.8.cloned.1.call-done = f32[256,256]{0,1:T(8,128)} async-done(((f32[256,256]{0,1:T(8,128)}), f32[256,256]{0,1:T(8,128)}) %all-reduce.8.cloned.1.call-update) | async-done | bytes 262160 | tf_op jit(solution)/shard_map/psum | solution.py:25
  96.9 11.7 %cholesky.130 = f32[128,128]{1,0:T(8,128)S(1)} custom-call(f32[128,128]{1,0:T(8,128)S(1)} %cholesky.194), custom_call_target="Cholesky" | custom-call | tf_op jit(solution)/shard_map/jit(cholesky)/cholesky | solution.py:19
  108.6 9.8 %custom-call.13 = f32[1,128,128]{1,2,0:T(8,128)S(1)} custom-call(f32[1,128,128]{2,1,0:T(8,128)S(1)} %get-tuple-element.51), custom_call_target="InvertDiagBlocksLowerTriangular" | custom-call | tf_op jit(solution)/shard_map/jit(cholesky)/cholesky | solution.py:19
  119.0 11.7 %cholesky.147 = f32[128,128]{1,0:T(8,128)S(1)} custom-call(f32[128,128]{1,0:T(8,128)S(1)} %convolution_subtract_fusion.5), custom_call_target="Cholesky" | custom-call | tf_op jit(solution)/shard_map/jit(cholesky)/cholesky | solution.py:19
  132.9 4.3 while.4
  133.7 1.4 bitcast_dynamic-update-slice_fusion.4
  137.2 19.7 %custom-call.14 = f32[2,128,128]{1,2,0:T(8,128)S(1)} custom-call(f32[2,128,128]{2,1,0:T(8,128)S(1)} %get-tuple-element.19), custom_call_target="InvertDiagBlocksLowerTriangular" | custom-call | tf_op jit(solution)/shard_map/triangular_solve/custom-call.0 | solution.py:20
  159.9 35.5 %all-reduce.10.cloned.1.call-done = f32[1024,256]{0,1:T(8,128)} async-done(((f32[1024,256]{0,1:T(8,128)}), f32[1024,256]{0,1:T(8,128)}) %all-reduce.10.cloned.1.call-update) | async-done | bytes 1048592 | tf_op jit(solution)/shard_map/psum | solution.py:11
  195.3 7.2 %fusion.24 = f32[256,1024]{1,0:T(8,128)} fusion(f32[1024,256]{0,1:T(8,128)} %all-reduce.10.cloned.1.call-done, f32[1024,1024]{0,1:T(8,128)} %bitcast.84), kind=kOutput, calls=%fused_computation.66 | convolution fusion | flops 3221225472 | bytes 6291456 | tf_op jit(solution)/shard_map/dot_general | solution.py:15
  202.7 78.5 %all-reduce.12.cloned.1.call-done = f32[256,1024]{1,0:T(8,128)} async-done(((f32[256,1024]{1,0:T(8,128)}), f32[256,1024]{1,0:T(8,128)}) %all-reduce.12.cloned.1.call-update) | async-done | bytes 1048592 | tf_op jit(solution)/shard_map/psum | solution.py:39
  281.1 7.2 %convolution_subtract_fusion.1 = f32[1024,1024]{0,1:T(8,128)S(1)} fusion(f32[1024,1024]{0,1:T(8,128)} %bitcast.85, f32[1024,256]{0,1:T(8,128)S(1)} %copy-done.1, f32[256,1024]{1,0:T(8,128)} %all-reduce.12.cloned.1.call-done), kind=kOutput, calls=%fused_computation.5 | convolution fusion | flops 3222274048 | bytes 10485760 | tf_op jit(solution)/shard_map/dot_general | solution.py:15
  288.3 2.0 copy-done
  290.3 1.7 fusion.2
  293.7 68.8 %all-reduce.14.cloned.1.call-done = f32[256,256]{0,1:T(8,128)} async-done(((f32[256,256]{0,1:T(8,128)}), f32[256,256]{0,1:T(8,128)}) %all-reduce.14.cloned.1.call-update) | async-done | bytes 262160 | tf_op jit(solution)/shard_map/psum | solution.py:25
  364.5 11.7 %cholesky.164 = f32[128,128]{1,0:T(8,128)S(1)} custom-call(f32[128,128]{1,0:T(8,128)S(1)} %cholesky.197), custom_call_target="Cholesky" | custom-call | tf_op jit(solution)/shard_map/jit(cholesky)/cholesky | solution.py:19
  376.9 9.8 %custom-call.15 = f32[1,128,128]{1,2,0:T(8,128)S(1)} custom-call(f32[1,128,128]{2,1,0:T(8,128)S(1)} %get-tuple-element.47), custom_call_target="InvertDiagBlocksLowerTriangular" | custom-call | tf_op jit(solution)/shard_map/jit(cholesky)/cholesky | solution.py:19
  387.2 11.7 %cholesky.181 = f32[128,128]{1,0:T(8,128)S(1)} custom-call(f32[128,128]{1,0:T(8,128)S(1)} %convolution_subtract_fusion.4), custom_call_target="Cholesky" | custom-call | tf_op jit(solution)/shard_map/jit(cholesky)/cholesky | solution.py:19
  401.1 4.4 while.5
  401.9 1.4 bitcast_dynamic-update-slice_fusion.5
  404.0 1.4 bitcast_dynamic-update-slice_fusion.5
  405.4 19.7 %custom-call.16 = f32[2,128,128]{1,2,0:T(8,128)S(1)} custom-call(f32[2,128,128]{2,1,0:T(8,128)S(1)} %get-tuple-element.20), custom_call_target="InvertDiagBlocksLowerTriangular" | custom-call | tf_op jit(solution)/shard_map/triangular_solve/custom-call.0 | solution.py:20
  428.1 35.5 %all-reduce.16.cloned.1.call-done = f32[1024,256]{0,1:T(8,128)} async-done(((f32[1024,256]{0,1:T(8,128)}), f32[1024,256]{0,1:T(8,128)}) %all-reduce.16.cloned.1.call-update) | async-done | bytes 1048592 | tf_op jit(solution)/shard_map/psum | solution.py:11
  463.6 7.3 %fusion.25 = f32[256,1024]{1,0:T(8,128)} fusion(f32[1024,256]{0,1:T(8,128)} %all-reduce.16.cloned.1.call-done, f32[1024,1024]{0,1:T(8,128)} %copy-done), kind=kOutput, calls=%fused_computation.67 | convolution fusion | flops 3221225472 | bytes 6291456 | tf_op jit(solution)/shard_map/dot_general | solution.py:15
  470.9 1.5 pad_maximum_fusion.1
  472.4 4.1 copy.10
  476.5 73.1 %all-reduce.18.cloned.1.call-done = f32[256,1024]{1,0:T(8,128)} async-done(((f32[256,1024]{1,0:T(8,128)}), f32[256,1024]{1,0:T(8,128)}) %all-reduce.18.cloned.1.call-update) | async-done | bytes 1048592 | tf_op jit(solution)/shard_map/psum | solution.py:39
  549.6 2.9 pad_maximum_fusion
  552.5 4.7 reshape.63
  557.2 6.7 %convolution_subtract_fusion = f32[1024,1024]{0,1:T(8,128)} fusion(f32[1024,1024]{0,1:T(8,128)} %copy-done, f32[1024,256]{0,1:T(8,128)S(1)} %copy-done.2, f32[256,1024]{1,0:T(8,128)S(1)} %copy-done.4), kind=kOutput, calls=%fused_computation.4 | convolution fusion | flops 3222274048 | bytes 10485760 | tf_op jit(solution)/shard_map/dot_general | solution.py:15
  563.9 10.9 %copy.11 = f32[1024,4,1,256]{3,2,1,0:T(1,128)} copy(f32[1024,4,1,256]{0,3,1,2:T(8,128)} %bitcast.86) | data formatting | bytes 8388608
  (65 shorter events, 20.3 us)
Async XLA Ops:
  7.2 87.6 %all-reduce.8.cloned.1.call-start = ((), (), s32[]{:S(2)}) async-start(), calls=%async_computation | async-start | bytes 524288 | tf_op jit(solution)/shard_map/psum | solution.py:25
  21.4 173.9 %all-reduce.10.cloned.1.call-start = ((), (), s32[]{:S(2)}) async-start(), calls=%async_computation.1 | async-start | bytes 2097152 | tf_op jit(solution)/shard_map/psum | solution.py:11
  159.8 121.3 %all-reduce.12.cloned.1.call-start = ((), (), s32[]{:S(2)}) async-start(), calls=%async_computation.2 | async-start | bytes 2097152 | tf_op jit(solution)/shard_map/psum | solution.py:39
  195.3 85.8 %copy-start.1 = (f32[1024,256]{0,1:T(8,128)S(1)}, f32[1024,256]{0,1:T(8,128)}, u32[]{:S(2)}) copy-start(f32[1024,256]{0,1:T(8,128)} %all-reduce.10.cloned.1.call-done) | copy-start | bytes 3145732
  202.6 159.8 %all-reduce.14.cloned.1.call-start = ((), (), s32[]{:S(2)}) async-start(), calls=%async_computation.3 | async-start | bytes 524288 | tf_op jit(solution)/shard_map/psum | solution.py:25
  288.3 2.0 copy-start
  292.1 171.5 %all-reduce.16.cloned.1.call-start = ((), (), s32[]{:S(2)}) async-start(), calls=%async_computation.4 | async-start | bytes 2097152 | tf_op jit(solution)/shard_map/psum | solution.py:11
  428.1 121.5 %all-reduce.18.cloned.1.call-start = ((), (), s32[]{:S(2)}) async-start(), calls=%async_computation.5 | async-start | bytes 2097152 | tf_op jit(solution)/shard_map/psum | solution.py:39
  463.6 7.3 %copy-start.2 = (f32[1024,256]{0,1:T(8,128)S(1)}, f32[1024,256]{0,1:T(8,128)}, u32[]{:S(2)}) copy-start(f32[1024,256]{0,1:T(8,128)} %all-reduce.16.cloned.1.call-done) | copy-start | bytes 3145732
  470.9 78.7 %copy-start.3 = (f32[256,1024]{1,0:T(8,128)S(1)}, f32[256,1024]{1,0:T(8,128)}, u32[]{:S(2)}) copy-start(f32[256,1024]{1,0:T(8,128)} %all-reduce.12.cloned.1.call-done) | copy-start | bytes 3145732
  549.6 7.6 %copy-start.4 = (f32[256,1024]{1,0:T(8,128)S(1)}, f32[256,1024]{1,0:T(8,128)}, u32[]{:S(2)}) copy-start(f32[256,1024]{1,0:T(8,128)} %all-reduce.18.cloned.1.call-done) | copy-start | bytes 3145732
Sparse Core Ops, SparseCore 0:
  21.5 73.2 all-reduce.7
  159.9 35.3 all-reduce.9
  202.7 78.3 all-reduce.11
  292.2 70.1 all-reduce.13
  428.2 35.3 all-reduce.15
  471.0 78.5 all-reduce.17
where the time goes:
time: 591 us; the launch traced here: 582 us
  waiting for transfers between devices  363 us (61%)
  other arithmetic  116 us (20%)
  local copies, waits for them, and re-layouts  45.6 us (8%)
  matrix products  38 us (6%)
  between operations  17.5 us (3%)
    psum x2, waiting for transfers between devices, factor_project(): return (basis, lax.psum(product(basis.T, block), 'rows'))  152 us
    psum x2, waiting for transfers between devices, single_pass(): gram = lax.psum(product(panel.T, panel), 'rows')  141 us
    psum x2, waiting for transfers between devices, broadcast(): return lax.psum(jnp.where(mine, array, jnp.zeros_like(array)), axis)  70.9 us
    another operation x13, other arithmetic, lower_solve(): lower = jnp.linalg.cholesky(gram)  68.7 us
    another operation x5, other arithmetic, lower_solve(): lax.linalg.triangular_solve(lower, panel.T, left_side=True, lower=True)  39.4 us
    dot_general x6, matrix products, product(): return jnp.dot(left, right, precision=HIGHEST)  33.4 us
    unnamed x13, local copies, waits for them, and re-layouts  27.9 us
  transfers between devices with their start and end apart: 6, of which 6 were waited for; matrix products, arithmetic and copies ran while one was open for 1% of the time, Pallas kernels for 0%

commit v1 on v0

v1 whole, which is shorter than its diff:
```python
import jax
import jax.numpy as jnp
from jax import lax
from jax.experimental import pallas as pl
from jax.experimental.pallas import tpu as pltpu
from jax.sharding import PartitionSpec as P

HIGHEST = lax.Precision.HIGHEST
LANES = 128
SUB = 8
F32 = jnp.float32
BF16 = jnp.bfloat16


def params(mib):
    return pltpu.CompilerParams(vmem_limit_bytes=mib * 1024 * 1024)


def vmem_spec():
    return pl.BlockSpec(memory_space=pltpu.VMEM)


def smem_spec():
    return pl.BlockSpec(memory_space=pltpu.SMEM)


def split(value):
    high = value.astype(BF16)
    return high, (value - high.astype(F32)).astype(BF16)


NN = (((1,), (0,)), ((), ()))
NT = (((1,), (1,)), ((), ()))


def dot3(left, right, dims=NN):
    def one(a, b):
        return lax.dot_general(a, b, dims, preferred_element_type=F32)

    return one(left[0], right[0]) + (one(left[0], right[1]) + one(left[1], right[0]))


def panel_kernel(x_ref, out_ref):
    rows = out_ref.shape[1]
    blocks = x_ref.shape[0] // rows
    for half in range(out_ref.shape[0]):
        out_ref[half] = x_ref[pl.ds(half, rows, stride=blocks), :]


def own_panel(lines, rows, blocks, halves):
    step = 256
    return pl.pallas_call(
        panel_kernel,
        grid=(rows // step,),
        in_specs=[pl.BlockSpec((step * blocks, LANES), lambda i: (i, 0))],
        out_specs=pl.BlockSpec((halves, step, LANES), lambda i: (0, i, 0)),
        out_shape=jax.ShapeDtypeStruct((halves, rows, LANES), F32),
        name="own_panel",
    )(lines)


def gram_kernel(core_ref, a_ref, b_ref, out_ref):
    core = core_ref[0]

    def pick(zero, one):
        return jnp.where(core == 0, zero, one)

    own = jnp.concatenate([a_ref[0], a_ref[1]], axis=1)
    other = jnp.concatenate([b_ref[0], b_ref[1]], axis=1)
    first = pick(own, other)
    cross = pick(b_ref[0], a_ref[1])
    left = split(jnp.concatenate([own.T, cross.T], axis=0))
    right_own = split(own)
    right_first = split(first)
    width = own.shape[1]
    left_own = tuple(part[:width] for part in left)
    left_cross = tuple(part[width:] for part in left)
    mine = dot3(left_own, right_own)
    mixed = dot3(left_cross, right_first)
    out_ref[0] = mine[:LANES, :LANES]
    out_ref[1] = mine[LANES:, :LANES]
    out_ref[2] = mine[LANES:, LANES:]
    out_ref[3] = mixed[:, :LANES]
    out_ref[4] = mixed[:, LANES:]


def panel_gram(core, own, other):
    return pl.pallas_call(
        gram_kernel,
        in_specs=[smem_spec(), vmem_spec(), vmem_spec()],
        out_specs=vmem_spec(),
        out_shape=jax.ShapeDtypeStruct((5, LANES, LANES), F32),
        compiler_params=params(48),
        name="panel_gram",
    )(core, own, other)


def product_kernel(base_ref, x_ref, p0_ref, p1_ref, out_ref):
    rows = p0_ref.shape[0]
    blocks = x_ref.shape[0] // rows
    count = out_ref.shape[0]
    base = base_ref[0]
    left = split(jnp.concatenate([p0_ref[...].T, p1_ref[...].T], axis=0))
    parts = [x_ref[pl.ds(base + i, rows, stride=blocks), :] for i in range(count)]
    result = dot3(left, split(jnp.concatenate(parts, axis=1)))
    for i in range(count):
        out_ref[i] = result[:, i * LANES:(i + 1) * LANES]


def panel_products(base, lines, p0, p1, count):
    return pl.pallas_call(
        product_kernel,
        in_specs=[smem_spec(), vmem_spec(), vmem_spec(), vmem_spec()],
        out_specs=vmem_spec(),
        out_shape=jax.ShapeDtypeStruct((count, 2 * LANES, LANES), F32),
        compiler_params=params(48),
        name="panel_products",
    )(base, lines, p0, p1)


def lane_copy(value, lane):
    return jnp.broadcast_to(value[:, lane:lane + 1], value.shape)


def row_copy(value, row):
    return jnp.broadcast_to(value[row:row + 1, :], value.shape)


def inverse_factor(block):
    groups = LANES // SUB
    lane = lax.broadcasted_iota(jnp.int32, (SUB, LANES), 1)
    sub = lax.broadcasted_iota(jnp.int32, (SUB, LANES), 0)
    work = [block[SUB * g:SUB * (g + 1), :] for g in range(groups)]
    result = []
    for g in range(groups):
        start = SUB * g
        panel = work[g]
        inside = (lane >= start) & (lane < start + SUB)
        cols = [lane_copy(panel, start + j) for j in range(SUB)]
        c = {(s, j): row_copy(cols[j], s) for j in range(SUB) for s in range(j, SUB)}
        mult, recip = {}, []
        for i in range(SUB):
            recip.append(1.0 / c[i, i])
            for s in range(i + 1, SUB):
                mult[s, i] = c[s, i] * recip[i]
                for t in range(i + 1, s + 1):
                    c[s, t] = c[s, t] - mult[s, i] * c[t, i]
        unit = jnp.where(inside, jnp.where(lane == start + sub, 1.0, 0.0), panel)
        upper = []
        for s in range(SUB):
            row = row_copy(unit, s)
            for i in range(s):
                row = row - mult[s, i] * upper[i]
            upper.append(row)
        solved = [None] * SUB
        for s in reversed(range(SUB)):
            row = upper[s] * recip[s]
            for t in range(s + 1, SUB):
                row = row - mult[t, s] * solved[t]
            solved[s] = row
        for later in range(g + 1, groups):
            old = work[later]
            new = jnp.where(inside, 0.0, old)
            for j in range(SUB):
                new = new - lane_copy(old, start + j) * solved[j]
            work[later] = new
        rows = upper[0]
        diag = c[0, 0]
        for s in range(1, SUB):
            rows = jnp.where(sub == s, upper[s], rows)
            diag = jnp.where(sub == s, c[s, s], diag)
        result.append(jnp.where(lane < start + SUB, rows * lax.rsqrt(diag), 0.0))
    return jnp.concatenate(result, axis=0)


def dot6(a, b, dims=NN):
    return lax.dot_general(a, b, dims, precision=HIGHEST, preferred_element_type=F32)


def factor_kernel(g0_ref, g1_ref, out_ref):
    s = {
        (0, 0): g0_ref[0], (1, 0): g0_ref[1], (1, 1): g0_ref[2],
        (2, 0): g0_ref[3], (2, 1): g0_ref[4],
        (2, 2): g1_ref[0], (3, 2): g1_ref[1], (3, 3): g1_ref[2],
        (3, 0): g1_ref[3], (3, 1): g1_ref[4],
    }
    n = 4
    e = {}
    for k in range(n):
        m = inverse_factor(s[k, k])
        x = {j: dot6(m, e[k, j]) for j in range(k)}
        x[k] = m
        for j in range(n):
            value = x[j] if j <= k else jnp.zeros((LANES, LANES), F32)
            out_ref[k * LANES:(k + 1) * LANES, j * LANES:(j + 1) * LANES] = value
        low = {i: dot6(s[i, k], m, NT) for i in range(k + 1, n)}
        for i in range(k + 1, n):
            for j in range(k + 1, i + 1):
                s[i, j] = s[i, j] - dot6(low[i], low[j], NT)
            for j in range(k + 1):
                term = dot6(low[i], x[j])
                e[i, j] = e[i, j] - term if (i, j) in e else -term


def inverse_of_factor(g0, g1):
    size = 4 * LANES
    return pl.pallas_call(
        factor_kernel,
        in_specs=[vmem_spec(), vmem_spec()],
        out_specs=vmem_spec(),
        out_shape=jax.ShapeDtypeStruct((size, size), F32),
        compiler_params=params(48),
        name="inverse_of_factor",
    )(g0, g1)


def basis_kernel(a0_ref, a1_ref, x_ref, lines_ref, high_ref, low_ref):
    rows = a0_ref.shape[1]
    panels = jnp.concatenate([a0_ref[0], a0_ref[1], a1_ref[0], a1_ref[1]], axis=1)
    q = dot3(split(panels), split(x_ref[...]), NT)
    high, low = split(q)
    high_ref[...] = high
    low_ref[...] = low
    for panel in range(2):
        for half in range(2):
            k = 2 * panel + half
            lines_ref[pl.ds(2 * half + panel, rows, stride=4), :] = q[:, k * LANES:(k + 1) * LANES]


def panel_bases(a0, a1, inverse):
    halves, rows, lanes = a0.shape
    size = inverse.shape[0]
    step = 256
    return pl.pallas_call(
        basis_kernel,
        grid=(rows // step,),
        in_specs=[
            pl.BlockSpec((halves, step, lanes), lambda i: (0, i, 0)),
            pl.BlockSpec((halves, step, lanes), lambda i: (0, i, 0)),
            pl.BlockSpec((size, size), lambda i: (0, 0)),
        ],
        out_specs=[
            pl.BlockSpec((4 * step, lanes), lambda i: (i, 0)),
            pl.BlockSpec((step, size), lambda i: (i, 0)),
            pl.BlockSpec((step, size), lambda i: (i, 0)),
        ],
        out_shape=[
            jax.ShapeDtypeStruct((4 * rows, lanes), F32),
            jax.ShapeDtypeStruct((rows, size), BF16),
            jax.ShapeDtypeStruct((rows, size), BF16),
        ],
        compiler_params=params(48),
        name="panel_bases",
    )(a0, a1, inverse)


def trailing_kernel(bases_ref, x_ref, qh_ref, ql_ref, inv_ref, m0_ref, m1_ref, r0_ref, r1_ref,
                    factor_ref, out_ref, wh_ref, wl_ref):
    rows = qh_ref.shape[0]
    blocks = x_ref.shape[0] // rows
    count = m0_ref.shape[0]
    size = inv_ref.shape[0]

    @pl.when(pl.program_id(0) == 0)
    def _():
        inverse = split(inv_ref[...])
        for side, (h0, h1) in enumerate(((m0_ref, m1_ref), (r0_ref, r1_ref))):
            columns = []
            for i in range(count):
                columns.append(jnp.concatenate(
                    [h0[i, :LANES], h1[i, :LANES], h0[i, LANES:], h1[i, LANES:]], axis=0))
            w = dot3(inverse, split(jnp.concatenate(columns, axis=1)))
            for i in range(count):
                factor_ref[pl.ds(bases_ref[side] + i, size, stride=blocks), :] = (
                    w[:, i * LANES:(i + 1) * LANES])
            high, low = split(w)
            wh_ref[side] = high
            wl_ref[side] = low

    q = (qh_ref[...], ql_ref[...])
    for side in range(2):
        term = dot3(q, (wh_ref[side], wl_ref[side]))
        for i in range(count):
            where = pl.ds(bases_ref[side] + i, rows, stride=blocks)
            out_ref[where, :] = x_ref[where, :] - term[:, i * LANES:(i + 1) * LANES]


def finish(bases, lines, q_high, q_low, inverse, mine, received):
    rows, size = q_high.shape
    blocks = lines.shape[0] // rows
    count = mine[0].shape[0]
    step = 256
    whole = pl.BlockSpec((count, 2 * LANES, LANES), lambda i: (0, 0, 0))
    return pl.pallas_call(
        trailing_kernel,
        grid=(rows // step,),
        in_specs=[
            smem_spec(),
            pl.BlockSpec((step * blocks, LANES), lambda i: (i, 0)),
            pl.BlockSpec((step, size), lambda i: (i, 0)),
            pl.BlockSpec((step, size), lambda i: (i, 0)),
            pl.BlockSpec((size, size), lambda i: (0, 0)),
            whole, whole, whole, whole,
        ],
        out_specs=[
            pl.BlockSpec((size * blocks, LANES), lambda i: (0, 0)),
            pl.BlockSpec((step * blocks, LANES), lambda i: (i, 0)),
        ],
        out_shape=[
            jax.ShapeDtypeStruct((size * blocks, LANES), F32),
            jax.ShapeDtypeStruct(lines.shape, F32),
        ],
        scratch_shapes=[
            pltpu.VMEM((2, size, count * LANES), BF16),
            pltpu.VMEM((2, size, count * LANES), BF16),
        ],
        compiler_params=params(56),
        name="finish",
    )(bases, lines, q_high, q_low, inverse, mine[0], mine[1], received[0], received[1])


def swap(value, axis, size, bit):
    return lax.ppermute(value, axis, [(i, i ^ bit) for i in range(size)])


def spread(value, col, cols):
    span = 2
    while span < cols:
        got = lax.ppermute(value, "cols", [(i, i + span) for i in range(min(span, cols - span))])
        value = jnp.where(col < span, value, got)
        span *= 2
    return value


def bits_of(size):
    bits, bit = [], 1
    while bit < size:
        bits.append(bit)
        bit *= 2
    return bits


def halves_of(value, flag):
    half = value.shape[0] // 2
    keep = lax.dynamic_slice_in_dim(value, flag * half, half, 0)
    give = lax.dynamic_slice_in_dim(value, (1 - flag) * half, half, 0)
    return keep, give


def join(mine, got, flag):
    return jnp.where(flag == 0, jnp.concatenate([mine, got], 0), jnp.concatenate([got, mine], 0))


def sum_rows(mine, got, row, rows):
    shape = mine.shape
    value = (mine + got).reshape(-1, shape[-1])
    bits = bits_of(rows)[1:]
    for bit in bits:
        keep, give = halves_of(value, (row // bit) % 2)
        value = keep + swap(give, "rows", rows, bit)
    for bit in reversed(bits):
        value = join(value, swap(value, "rows", rows, bit), (row // bit) % 2)
    return value.reshape(shape)


def program(rows_n, cols_n):
    def on_device(features):
        rows, panels, _, width = features.shape
        halves = width // LANES
        blocks = panels * halves
        lines = features.reshape(rows * blocks, LANES)
        row, col = lax.axis_index("rows"), lax.axis_index("cols")
        core = col % 2
        own = own_panel(lines, rows, blocks, halves)

        other = swap(own, "cols", cols_n, 1)
        gram = panel_gram(core.reshape(1), own, other)
        gram = gram.reshape(-1, LANES)
        keep, give = halves_of(gram, row % 2)
        gram = keep + swap(give, "rows", rows_n, 1)
        for bit in bits_of(rows_n)[1:]:
            gram = gram + swap(gram, "rows", rows_n, bit)
        gram = join(gram, swap(gram, "rows", rows_n, 1), row % 2)
        gram = spread(gram, col, cols_n)
        got = swap(gram, "cols", cols_n, 1)
        shape = (5, LANES, LANES)
        first = jnp.where(core == 0, gram, got).reshape(shape)
        second = jnp.where(core == 0, got, gram).reshape(shape)
        inverse = inverse_of_factor(first, second)

        count = blocks // 2
        near = (row % 2) * count
        far = count - near
        mine, received, p0, p1 = [], [], [], []
        for half in range(halves):
            piece = spread(own[half], col, cols_n)
            twin = swap(piece, "cols", cols_n, 1)
            zero = jnp.where(core == 0, piece, twin)
            one = jnp.where(core == 0, twin, piece)
            p0.append(zero)
            p1.append(one)
            give = panel_products(far.reshape(1), lines, zero, one, count)
            keep = panel_products(near.reshape(1), lines, zero, one, count)
            total = sum_rows(keep, swap(give, "rows", rows_n, 1), row, rows_n)
            mine.append(total)
            received.append(swap(total, "rows", rows_n, 1))

        a0, a1 = jnp.stack(p0), jnp.stack(p1)
        basis, q_high, q_low = panel_bases(a0, a1, inverse)
        factor, trailing = finish(jnp.stack([near, far]), lines, q_high, q_low, inverse, mine, received)
        basis = basis.reshape(rows, halves, 2, LANES).transpose(0, 2, 1, 3).reshape(rows, 2, width)
        return (factor.reshape(2 * width, panels, 1, width), basis, trailing.reshape(features.shape))

    return on_device


def solution(mesh):
    placed = (P("rows", None, "cols", None),)
    return jax.shard_map(
        program(mesh.shape["rows"], mesh.shape["cols"]),
        mesh=mesh,
        in_specs=placed,
        out_specs=(
            P(None, None, "cols", None),
            P("rows", None, None),
            P("rows", None, "cols", None),
        ),
        check_vma=False,
    )
```

time: 591 us -> 172 us (0.29); the launches traced: 582 us -> 171 us
  waiting for transfers between devices: 363 us -> 60.9 us
  other arithmetic: 116 us -> 8.95 us
  Pallas kernels: 0 us -> 53.4 us
  matrix products: 38 us -> 0 us
  starting transfers between devices: 0.46 us -> 35 us
  local copies, waits for them, and re-layouts: 45.6 us -> 11.9 us
  between operations: 17.5 us -> 0.94 us
    psum x6 -> x0, waiting for transfers between devices: 363 us -> none  [the longest x2 152 us: factor_project(): return (basis, lax.psum(product(basis.T, block), 'rows'))]
    another operation x19 -> x2, other arithmetic: 110 us -> 0.8 us  [the longest x1 0.66 us: on_device(): jnp.stack([near, far])]
    ppermute x0 -> x23, waiting for transfers between devices: none -> 60.9 us  [the longest x20 40 us: swap(): return lax.ppermute(value, axis, [(i, i ^ bit) for i in range(size)])]
    pallas_call x0 -> x9, Pallas kernels: none -> 53.4 us  [the longest x1 27.1 us: inverse_of_factor(): pl.pallas_call(factor_kernel, in_specs=[vmem_spec(), vmem_spec()], out_sp...]
    ppermute x0 -> x23, starting transfers between devices: none -> 35 us  [the longest x20 24.2 us: swap(): return lax.ppermute(value, axis, [(i, i ^ bit) for i in range(size)])]
    dot_general x6 -> x0, matrix products: 33.4 us -> none  [product(): return jnp.dot(left, right, precision=HIGHEST)]
    unnamed x13 -> x26, local copies, waits for them, and re-layouts: 27.9 us -> 9.79 us
    another operation x19 -> x0, local copies, waits for them, and re-layouts: 8.25 us -> none  [the longest x15 8.2 us: lower_solve(): lax.linalg.triangular_solve(lower, panel.T, left_side=True, lower=True)]
  transfers between devices with their start and end apart: 6 -> 23, of which waited for: 6 -> 11; matrix products, arithmetic and copies ran while one was open for 1% -> 6% of each run, Pallas kernels for 0% -> 22%
where the time goes in v1:
time: 172 us; the launch traced here: 171 us
  waiting for transfers between devices  60.9 us (35%)
  Pallas kernels  53.4 us (31%)
  starting transfers between devices  35 us (20%)
  local copies, waits for them, and re-layouts  11.9 us (7%)
  other arithmetic  8.95 us (5%)
    ppermute x20, waiting for transfers between devices, swap(): return lax.ppermute(value, axis, [(i, i ^ bit) for i in range(size)])  40 us
    pallas_call x1, Pallas kernels, inverse_of_factor(): pl.pallas_call(factor_kernel, in_specs=[vmem_spec(), vmem_spec()], out_sp...  27.1 us
    ppermute x20, starting transfers between devices, swap(): return lax.ppermute(value, axis, [(i, i ^ bit) for i in range(size)])  24.2 us
    ppermute x3, waiting for transfers between devices, spread(): lax.ppermute(value, 'cols', [(i, i + span) for i in range(min(span, cols...  21 us
    pallas_call x1, Pallas kernels, finish(): pl.pallas_call(trailing_kernel, grid=(rows // step,), in_specs=[smem_spec...  11.9 us
    ppermute x3, starting transfers between devices, spread(): lax.ppermute(value, 'cols', [(i, i + span) for i in range(min(span, cols...  10.8 us
    unnamed x26, local copies, waits for them, and re-layouts  9.79 us
    pallas_call x4, Pallas kernels, panel_products(): pl.pallas_call(product_kernel, in_specs=[smem_spec(), vmem_spec(), vmem_s...  5.88 us
  transfers between devices with their start and end apart: 23, of which 11 were waited for; matrix products, arithmetic and copies ran while one was open for 6% of the time, Pallas kernels for 22%

profile of v1, /device:TPU:0, one launch (start us, length us, event | category | flops | bytes accessed | tf_op | source)
XLA Modules:
  0.0 171.1 jit_solution(10552360463684265647)
XLA Ops:
  0.6 4.1 %own_panel.1.a_ref = f32[2,1024,128]{2,1,0:T(8,128)} custom-call(f32[8192,128]{1,0:T(8,128)} %bitcast.30), custom_call_target="tpu_custom_call" | custom-call | tf_op jit(solution)/shard_map/own_panel/pallas_call | solution.py:52
  6.0 4.9 %collective-permute-start = (f32[1024,128]{1,0:T(8,128)S(1)}, f32[1024,128]{1,0:T(8,128)S(1)}, u32[]{:S(2)}, u32[]{:S(2)}) collective-permute-start(f32[1024,128]{1,0:T(8,128)S(1)} %get-tuple-element.22), channel_id=1, source_target_pairs={{0,2},{1,3},{4,6},{5,7},{8,10},{9,11},{12,14},{13,15},{16,18},{17,... | collective-permute-start | bytes 1572872 | tf_op jit(solution)/shard_map/ppermute | solution.py:329
  10.8 1.3 collective-permute-start.2
  12.3 10.9 %collective-permute-done = f32[1024,128]{1,0:T(8,128)S(1)} collective-permute-done((f32[1024,128]{1,0:T(8,128)S(1)}, f32[1024,128]{1,0:T(8,128)S(1)}, u32[]{:S(2)}, u32[]{:S(2)}) %collective-permute-start) | collective-permute-done | bytes 524320 | tf_op jit(solution)/shard_map/ppermute | solution.py:329
  23.1 10.1 %collective-permute-done.2 = f32[1024,128]{1,0:T(8,128)S(1)} collective-permute-done((f32[1024,128]{1,0:T(8,128)S(1)}, f32[1024,128]{1,0:T(8,128)S(1)}, u32[]{:S(2)}, u32[]{:S(2)}) %collective-permute-start.2) | collective-permute-done | bytes 524320 | tf_op jit(solution)/shard_map/ppermute | solution.py:329
  33.2 2.1 %broadcast_select_fusion.1 = (f32[1024,128]{1,0:T(8,128)S(1)}, f32[1024,128]{1,0:T(8,128)}) fusion(f32[1024,128]{1,0:T(8,128)S(1)} %collective-permute-done, pred[]{:T(512)S(6)} %lt.63, f32[2,1024,128]{2,1,0:T(8,128)} %own_panel.1.a_ref, f32[1024,128]{1,0:T(8,128)S(1)} %collective-permute-done.2), kind=kLoop, calls=%fused_computation.12 | loop fusion | flops 262144 | bytes 3145729 | tf_op jit(solution)/shard_map/jit(_where)/select_n | solution.py:330
  36.1 1.3 collective-permute-done.1
  38.7 2.2 %copy-done = f32[1024,4,1,256]{3,2,1,0:T(1,128)S(1)} copy-done((f32[1024,4,1,256]{3,2,1,0:T(1,128)S(1)}, f32[1024,4,1,256]{3,2,1,0:T(1,128)}, u32[]{:S(2)}) %copy-start) | copy-done | bytes 4194328
  40.9 2.1 %panel_products.5 = f32[4,256,128]{2,1,0:T(8,128)} custom-call(s32[1]{0:T(128)} %bitcast.1.base_ref, f32[8192,128]{1,0:T(8,128)S(1)} %bitcast.32, f32[1024,128]{1,0:T(8,128)S(1)} %get-tuple-element.17.p0_ref, f32[1024,128]{1,0:T(8,128)S(1)} %get-tuple-element.16.p1_ref), custom_call_target="tpu_custom_call" | custom-call | tf_op jit(solution)/shard_map/panel_products/pallas_call | solution.py:111
  42.9 1.5 collective-permute-start.11
  48.5 1.6 collective-permute-start.16
  50.1 11.3 %collective-permute-done.5 = f32[320,128]{1,0:T(8,128)S(1)} collective-permute-done((f32[320,128]{1,0:T(8,128)S(1)}, f32[320,128]{1,0:T(8,128)S(1)}, u32[]{:S(2)}, u32[]{:S(2)}) %collective-permute-start.5) | collective-permute-done | bytes 163872 | tf_op jit(solution)/shard_map/ppermute | solution.py:323
  61.4 1.6 collective-permute-start.6
  63.1 3.7 %collective-permute-done.6 = f32[320,128]{1,0:T(8,128)S(1)} collective-permute-done((f32[320,128]{1,0:T(8,128)S(1)}, f32[320,128]{1,0:T(8,128)S(1)}, u32[]{:S(2)}, u32[]{:S(2)}) %collective-permute-start.6) | collective-permute-done | bytes 163872 | tf_op jit(solution)/shard_map/ppermute | solution.py:323
  66.8 2.7 %collective-permute-start.7 = (f32[320,128]{1,0:T(8,128)S(1)}, f32[320,128]{1,0:T(8,128)S(1)}, u32[]{:S(2)}, u32[]{:S(2)}) collective-permute-start(f32[320,128]{1,0:T(8,128)S(1)} %add.77), channel_id=1, source_target_pairs={{0,16},{4,20},{8,24},{12,28},{16,0},{20,4},{24,8},{28,12},{1,17},{... | collective-permute-start | bytes 491528 | tf_op jit(solution)/shard_map/ppermute | solution.py:323
  69.5 2.2 %copy-done.2 = f32[1024,4,1,256]{3,2,1,0:T(1,128)S(1)} copy-done((f32[1024,4,1,256]{3,2,1,0:T(1,128)S(1)}, f32[1024,4,1,256]{3,2,1,0:T(1,128)}, u32[]{:S(2)}) %copy-start.2) | copy-done | bytes 4194328
  73.0 2.2 %collective-permute-done.7 = f32[320,128]{1,0:T(8,128)S(1)} collective-permute-done((f32[320,128]{1,0:T(8,128)S(1)}, f32[320,128]{1,0:T(8,128)S(1)}, u32[]{:S(2)}, u32[]{:S(2)}) %collective-permute-start.7) | collective-permute-done | bytes 163872 | tf_op jit(solution)/shard_map/ppermute | solution.py:323
  75.2 1.6 collective-permute-start.8
  79.3 2.2 %copy-done.3 = f32[1024,4,1,256]{3,2,1,0:T(1,128)S(1)} copy-done((f32[1024,4,1,256]{3,2,1,0:T(1,128)S(1)}, f32[1024,4,1,256]{3,2,1,0:T(1,128)}, u32[]{:S(2)}) %copy-start.3) | copy-done | bytes 4194328
  83.9 1.4 collective-permute-start.17
  85.3 4.6 %collective-permute-start.9 = (f32[640,128]{1,0:T(8,128)S(1)}, f32[640,128]{1,0:T(8,128)S(1)}, u32[]{:S(2)}, u32[]{:S(2)}) collective-permute-start(f32[640,128]{1,0:T(8,128)S(1)} %maximum_select_fusion.2), channel_id=1, source_target_pairs={{0,2},{1,3},{4,6},{5,7},{8,10},{9,11},{12,14},{13,15},{16,18},{17,... | collective-permute-start | bytes 983048 | tf_op jit(solution)/shard_map/ppermute | solution.py:329
  91.0 2.1 %collective-permute-start.13 = (f32[256,128]{1,0:T(8,128)S(1)}, f32[256,128]{1,0:T(8,128)S(1)}, u32[]{:S(2)}, u32[]{:S(2)}) collective-permute-start(f32[256,128]{1,0:T(8,128)S(1)} %constant_dynamic-slice_fusion.2), channel_id=1, source_target_pairs={{0,16},{4,20},{8,24},{12,28},{16,0},{20,4},{24,8},{28,12},{1,17},{... | collective-permute-start | bytes 393224 | tf_op jit(solution)/shard_map/ppermute | solution.py:323
  94.2 8.3 %collective-permute-done.13 = f32[256,128]{1,0:T(8,128)S(1)} collective-permute-done((f32[256,128]{1,0:T(8,128)S(1)}, f32[256,128]{1,0:T(8,128)S(1)}, u32[]{:S(2)}, u32[]{:S(2)}) %collective-permute-start.13) | collective-permute-done | bytes 131104 | tf_op jit(solution)/shard_map/ppermute | solution.py:323
  102.5 1.9 %collective-permute-done.18 = f32[256,128]{1,0:T(8,128)S(1)} collective-permute-done((f32[256,128]{1,0:T(8,128)S(1)}, f32[256,128]{1,0:T(8,128)S(1)}, u32[]{:S(2)}, u32[]{:S(2)}) %collective-permute-start.18) | collective-permute-done | bytes 131104 | tf_op jit(solution)/shard_map/ppermute | solution.py:323
  105.5 4.5 %collective-permute-done.14 = f32[256,128]{1,0:T(8,128)S(1)} collective-permute-done((f32[256,128]{1,0:T(8,128)S(1)}, f32[256,128]{1,0:T(8,128)S(1)}, u32[]{:S(2)}, u32[]{:S(2)}) %collective-permute-start.14) | collective-permute-done | bytes 131104 | tf_op jit(solution)/shard_map/ppermute | solution.py:323
  110.1 3.2 %collective-permute-start.15 = (f32[512,128]{1,0:T(8,128)S(1)}, f32[512,128]{1,0:T(8,128)S(1)}, u32[]{:S(2)}, u32[]{:S(2)}) collective-permute-start(f32[512,128]{1,0:T(8,128)S(1)} %maximum_select_fusion.3), channel_id=1, source_target_pairs={{0,8},{4,12},{8,0},{12,4},{16,24},{20,28},{24,16},{28,20},{1,9},{5... | collective-permute-start | bytes 786440 | tf_op jit(solution)/shard_map/ppermute | solution.py:323
  113.3 3.2 %collective-permute-start.20 = (f32[512,128]{1,0:T(8,128)S(1)}, f32[512,128]{1,0:T(8,128)S(1)}, u32[]{:S(2)}, u32[]{:S(2)}) collective-permute-start(f32[512,128]{1,0:T(8,128)S(1)} %maximum_select_fusion.4), channel_id=1, source_target_pairs={{0,8},{4,12},{8,0},{12,4},{16,24},{20,28},{24,16},{28,20},{1,9},{5... | collective-permute-start | bytes 786440 | tf_op jit(solution)/shard_map/ppermute | solution.py:323
  116.6 3.9 %collective-permute-done.15 = f32[512,128]{1,0:T(8,128)S(1)} collective-permute-done((f32[512,128]{1,0:T(8,128)S(1)}, f32[512,128]{1,0:T(8,128)S(1)}, u32[]{:S(2)}, u32[]{:S(2)}) %collective-permute-start.15) | collective-permute-done | bytes 262176 | tf_op jit(solution)/shard_map/ppermute | solution.py:323
  121.1 2.8 %collective-permute-done.20 = f32[512,128]{1,0:T(8,128)S(1)} collective-permute-done((f32[512,128]{1,0:T(8,128)S(1)}, f32[512,128]{1,0:T(8,128)S(1)}, u32[]{:S(2)}, u32[]{:S(2)}) %collective-permute-start.20) | collective-permute-done | bytes 262176 | tf_op jit(solution)/shard_map/ppermute | solution.py:323
  125.5 27.1 %inverse_of_factor.1.x_ref.inv_ref = f32[512,512]{1,0:T(8,128)S(1)} custom-call(f32[5,128,128]{2,1,0:T(8,128)S(1)} %bitcast.41, f32[5,128,128]{2,1,0:T(8,128)S(1)} %bitcast.40), custom_call_target="tpu_custom_call" | custom-call | tf_op jit(solution)/shard_map/inverse_of_factor/pallas_call | solution.py:207
  152.6 3.6 %panel_bases.1 = (f32[4096,128]{1,0:T(8,128)}, bf16[1024,512]{1,0:T(8,128)(2,1)S(1)}, bf16[1024,512]{1,0:T(8,128)(2,1)S(1)}) custom-call(f32[2,1024,128]{2,1,0:T(8,128)S(1)} %get-tuple-element.26.a0_ref, f32[2,1024,128]{2,1,0:T(8,128)S(1)} %get-tuple-element.27.a1_ref, f32[512,512]{1,0:T(8,128)S(1)} %inverse_of_factor.1.x_ref.inv_ref), custom_call_target="tpu_custom_call" | custom-call | tf_op jit(solution)/shard_map/panel_bases/pallas_call | solution.py:234
  159.2 11.9 %finish.1 = (f32[4096,128]{1,0:T(8,128)}, f32[8192,128]{1,0:T(8,128)}) custom-call(s32[2]{0:T(128)} %pad_add_fusion.bases_ref, f32[8192,128]{1,0:T(8,128)} %bitcast.31, bf16[1024,512]{1,0:T(8,128)(2,1)} %copy-done.6, bf16[1024,512]{1,0:T(8,128)(2,1)} %copy-done.7, f32[512,512]{1,0:T(8,128)} %copy-done.5, f32[4,256,128]{2,1,0:T(8,128)} %bitcast.49, ...), custom_call_target="tpu_custom_call" | custom-call | tf_op jit(solution)/shard_map/finish/pallas_call | solution.py:294
  (76 shorter events, 22.2 us)
Async XLA Ops:
  6.0 17.2 %collective-permute-start = (f32[1024,128]{1,0:T(8,128)S(1)}, f32[1024,128]{1,0:T(8,128)S(1)}, u32[]{:S(2)}, u32[]{:S(2)}) collective-permute-start(f32[1024,128]{1,0:T(8,128)S(1)} %get-tuple-element.22), channel_id=1, source_target_pairs={{0,2},{1,3},{4,6},{5,7},{8,10},{9,11},{12,14},{13,15},{16,18},{17,... | collective-permute-start | bytes 1572872 | tf_op jit(solution)/shard_map/ppermute | solution.py:329
  10.8 22.4 %collective-permute-start.2 = (f32[1024,128]{1,0:T(8,128)S(1)}, f32[1024,128]{1,0:T(8,128)S(1)}, u32[]{:S(2)}, u32[]{:S(2)}) collective-permute-start(f32[1024,128]{1,0:T(8,128)S(1)} %get-tuple-element.23), channel_id=1, source_target_pairs={{0,2},{1,3},{4,6},{5,7},{8,10},{9,11},{12,14},{13,15},{16,18},{17,... | collective-permute-start | bytes 1572872 | tf_op jit(solution)/shard_map/ppermute | solution.py:329
  12.2 32.3 %collective-permute-start.4 = (f32[2,1024,128]{2,1,0:T(8,128)}, f32[2,1024,128]{2,1,0:T(8,128)S(1)}, u32[]{:S(2)}, u32[]{:S(2)}) collective-permute-start(f32[2,1024,128]{2,1,0:T(8,128)} %own_panel.1.a_ref), channel_id=1, source_target_pairs={{0,1},{1,0},{2,3},{3,2},{4,5},{5,4},{6,7},{7,6},{8,9},{9,8},{10,11... | collective-permute-start | bytes 3145736 | tf_op jit(solution)/shard_map/ppermute | solution.py:323
  35.3 9.1 %copy-start.4 = (f32[2,1024,128]{2,1,0:T(8,128)S(1)}, f32[2,1024,128]{2,1,0:T(8,128)}, u32[]{:S(2)}) copy-start(f32[2,1024,128]{2,1,0:T(8,128)} %own_panel.1.a_ref) | copy-start | bytes 3145732
  35.3 2.1 %collective-permute-start.1 = (f32[1024,128]{1,0:T(8,128)S(1)}, f32[1024,128]{1,0:T(8,128)}, u32[]{:S(2)}, u32[]{:S(2)}) collective-permute-start(f32[1024,128]{1,0:T(8,128)S(1)} %get-tuple-element.20), channel_id=1, source_target_pairs={{0,1},{1,0},{2,3},{3,2},{4,5},{5,4},{6,7},{7,6},{8,9},{9,8},{10,11... | collective-permute-start | bytes 1572872 | tf_op jit(solution)/shard_map/ppermute | solution.py:323
  35.3 10.6 %collective-permute-start.3 = (f32[1024,128]{1,0:T(8,128)}, f32[1024,128]{1,0:T(8,128)}, u32[]{:S(2)}, u32[]{:S(2)}) collective-permute-start(f32[1024,128]{1,0:T(8,128)} %get-tuple-element.21), channel_id=1, source_target_pairs={{0,1},{1,0},{2,3},{3,2},{4,5},{5,4},{6,7},{7,6},{8,9},{9,8},{10,11... | collective-permute-start | bytes 1572872 | tf_op jit(solution)/shard_map/ppermute | solution.py:323
  38.7 2.2 %copy-start = (f32[1024,4,1,256]{3,2,1,0:T(1,128)S(1)}, f32[1024,4,1,256]{3,2,1,0:T(1,128)}, u32[]{:S(2)}) copy-start(f32[1024,4,1,256]{3,2,1,0:T(1,128)} %param.1) | copy-start | bytes 12582916
  40.9 6.4 %copy-start.1 = (f32[1024,4,1,256]{3,2,1,0:T(1,128)S(1)}, f32[1024,4,1,256]{3,2,1,0:T(1,128)}, u32[]{:S(2)}) copy-start(f32[1024,4,1,256]{3,2,1,0:T(1,128)} %param.1) | copy-start | bytes 12582916
  42.9 33.9 %collective-permute-start.11 = (f32[4,256,128]{2,1,0:T(8,128)}, f32[4,256,128]{2,1,0:T(8,128)}, u32[]{:S(2)}, u32[]{:S(2)}) collective-permute-start(f32[4,256,128]{2,1,0:T(8,128)} %panel_products.5), channel_id=1, source_target_pairs={{0,4},{4,0},{8,12},{12,8},{16,20},{20,16},{24,28},{28,24},{1,5},{5... | collective-permute-start | bytes 1572872 | tf_op jit(solution)/shard_map/ppermute | solution.py:323
  45.4 16.0 %collective-permute-start.5 = (f32[320,128]{1,0:T(8,128)S(1)}, f32[320,128]{1,0:T(8,128)S(1)}, u32[]{:S(2)}, u32[]{:S(2)}) collective-permute-start(f32[320,128]{1,0:T(8,128)S(1)} %constant_dynamic-slice_fusion.4), channel_id=1, source_target_pairs={{0,4},{4,0},{8,12},{12,8},{16,20},{20,16},{24,28},{28,24},{1,5},{5... | collective-permute-start | bytes 491528 | tf_op jit(solution)/shard_map/ppermute | solution.py:323
  48.5 34.2 %collective-permute-start.16 = (f32[4,256,128]{2,1,0:T(8,128)S(1)}, f32[4,256,128]{2,1,0:T(8,128)}, u32[]{:S(2)}, u32[]{:S(2)}) collective-permute-start(f32[4,256,128]{2,1,0:T(8,128)S(1)} %panel_products.7), channel_id=1, source_target_pairs={{0,4},{4,0},{8,12},{12,8},{16,20},{20,16},{24,28},{28,24},{1,5},{5... | collective-permute-start | bytes 1572872 | tf_op jit(solution)/shard_map/ppermute | solution.py:323
  61.4 5.4 %collective-permute-start.6 = (f32[320,128]{1,0:T(8,128)S(1)}, f32[320,128]{1,0:T(8,128)S(1)}, u32[]{:S(2)}, u32[]{:S(2)}) collective-permute-start(f32[320,128]{1,0:T(8,128)S(1)} %dynamic-slice_add_fusion.2), channel_id=1, source_target_pairs={{0,8},{4,12},{8,0},{12,4},{16,24},{20,28},{24,16},{28,20},{1,9},{5... | collective-permute-start | bytes 491528 | tf_op jit(solution)/shard_map/ppermute | solution.py:323
  66.8 8.3 %collective-permute-start.7 = (f32[320,128]{1,0:T(8,128)S(1)}, f32[320,128]{1,0:T(8,128)S(1)}, u32[]{:S(2)}, u32[]{:S(2)}) collective-permute-start(f32[320,128]{1,0:T(8,128)S(1)} %add.77), channel_id=1, source_target_pairs={{0,16},{4,20},{8,24},{12,28},{16,0},{20,4},{24,8},{28,12},{1,17},{... | collective-permute-start | bytes 491528 | tf_op jit(solution)/shard_map/ppermute | solution.py:323
  69.5 2.2 %copy-start.2 = (f32[1024,4,1,256]{3,2,1,0:T(1,128)S(1)}, f32[1024,4,1,256]{3,2,1,0:T(1,128)}, u32[]{:S(2)}) copy-start(f32[1024,4,1,256]{3,2,1,0:T(1,128)} %param.1) | copy-start | bytes 12582916
  75.2 10.1 %collective-permute-start.8 = (f32[320,128]{1,0:T(8,128)S(1)}, f32[320,128]{1,0:T(8,128)S(1)}, u32[]{:S(2)}, u32[]{:S(2)}) collective-permute-start(f32[320,128]{1,0:T(8,128)S(1)} %add.78), channel_id=1, source_target_pairs={{0,4},{4,0},{8,12},{12,8},{16,20},{20,16},{24,28},{28,24},{1,5},{5... | collective-permute-start | bytes 491528 | tf_op jit(solution)/shard_map/ppermute | solution.py:323
  78.6 11.3 %collective-permute-start.12 = (f32[512,128]{1,0:T(8,128)}, f32[512,128]{1,0:T(8,128)}, u32[]{:S(2)}, u32[]{:S(2)}) collective-permute-start(f32[512,128]{1,0:T(8,128)} %constant_dynamic-slice_fusion.3), channel_id=1, source_target_pairs={{0,8},{4,12},{8,0},{12,4},{16,24},{20,28},{24,16},{28,20},{1,9},{5... | collective-permute-start | bytes 786440 | tf_op jit(solution)/shard_map/ppermute | solution.py:323
  79.3 2.2 %copy-start.3 = (f32[1024,4,1,256]{3,2,1,0:T(1,128)S(1)}, f32[1024,4,1,256]{3,2,1,0:T(1,128)}, u32[]{:S(2)}) copy-start(f32[1024,4,1,256]{3,2,1,0:T(1,128)} %param.1) | copy-start | bytes 12582916
  83.9 9.2 %collective-permute-start.17 = (f32[512,128]{1,0:T(8,128)S(1)}, f32[512,128]{1,0:T(8,128)S(1)}, u32[]{:S(2)}, u32[]{:S(2)}) collective-permute-start(f32[512,128]{1,0:T(8,128)S(1)} %constant_dynamic-slice_fusion.1), channel_id=1, source_target_pairs={{0,8},{4,12},{8,0},{12,4},{16,24},{20,28},{24,16},{28,20},{1,9},{5... | collective-permute-start | bytes 786440 | tf_op jit(solution)/shard_map/ppermute | solution.py:323
  85.3 31.2 %collective-permute-start.9 = (f32[640,128]{1,0:T(8,128)S(1)}, f32[640,128]{1,0:T(8,128)S(1)}, u32[]{:S(2)}, u32[]{:S(2)}) collective-permute-start(f32[640,128]{1,0:T(8,128)S(1)} %maximum_select_fusion.2), channel_id=1, source_target_pairs={{0,2},{1,3},{4,6},{5,7},{8,10},{9,11},{12,14},{13,15},{16,18},{17,... | collective-permute-start | bytes 983048 | tf_op jit(solution)/shard_map/ppermute | solution.py:329
  91.0 11.5 %collective-permute-start.13 = (f32[256,128]{1,0:T(8,128)S(1)}, f32[256,128]{1,0:T(8,128)S(1)}, u32[]{:S(2)}, u32[]{:S(2)}) collective-permute-start(f32[256,128]{1,0:T(8,128)S(1)} %constant_dynamic-slice_fusion.2), channel_id=1, source_target_pairs={{0,16},{4,20},{8,24},{12,28},{16,0},{20,4},{24,8},{28,12},{1,17},{... | collective-permute-start | bytes 393224 | tf_op jit(solution)/shard_map/ppermute | solution.py:323
  93.2 11.2 %collective-permute-start.18 = (f32[256,128]{1,0:T(8,128)S(1)}, f32[256,128]{1,0:T(8,128)S(1)}, u32[]{:S(2)}, u32[]{:S(2)}) collective-permute-start(f32[256,128]{1,0:T(8,128)S(1)} %constant_dynamic-slice_fusion), channel_id=1, source_target_pairs={{0,16},{4,20},{8,24},{12,28},{16,0},{20,4},{24,8},{28,12},{1,17},{... | collective-permute-start | bytes 393224 | tf_op jit(solution)/shard_map/ppermute | solution.py:323
  102.4 7.6 %collective-permute-start.14 = (f32[256,128]{1,0:T(8,128)S(1)}, f32[256,128]{1,0:T(8,128)S(1)}, u32[]{:S(2)}, u32[]{:S(2)}) collective-permute-start(f32[256,128]{1,0:T(8,128)S(1)} %dynamic-slice_add_fusion.4), channel_id=1, source_target_pairs={{0,16},{4,20},{8,24},{12,28},{16,0},{20,4},{24,8},{28,12},{1,17},{... | collective-permute-start | bytes 393224 | tf_op jit(solution)/shard_map/ppermute | solution.py:323
  104.4 8.9 %collective-permute-start.19 = (f32[256,128]{1,0:T(8,128)S(1)}, f32[256,128]{1,0:T(8,128)S(1)}, u32[]{:S(2)}, u32[]{:S(2)}) collective-permute-start(f32[256,128]{1,0:T(8,128)S(1)} %dynamic-slice_add_fusion.3), channel_id=1, source_target_pairs={{0,16},{4,20},{8,24},{12,28},{16,0},{20,4},{24,8},{28,12},{1,17},{... | collective-permute-start | bytes 393224 | tf_op jit(solution)/shard_map/ppermute | solution.py:323
  110.1 10.5 %collective-permute-start.15 = (f32[512,128]{1,0:T(8,128)S(1)}, f32[512,128]{1,0:T(8,128)S(1)}, u32[]{:S(2)}, u32[]{:S(2)}) collective-permute-start(f32[512,128]{1,0:T(8,128)S(1)} %maximum_select_fusion.3), channel_id=1, source_target_pairs={{0,8},{4,12},{8,0},{12,4},{16,24},{20,28},{24,16},{28,20},{1,9},{5... | collective-permute-start | bytes 786440 | tf_op jit(solution)/shard_map/ppermute | solution.py:323
  113.3 10.7 %collective-permute-start.20 = (f32[512,128]{1,0:T(8,128)S(1)}, f32[512,128]{1,0:T(8,128)S(1)}, u32[]{:S(2)}, u32[]{:S(2)}) collective-permute-start(f32[512,128]{1,0:T(8,128)S(1)} %maximum_select_fusion.4), channel_id=1, source_target_pairs={{0,8},{4,12},{8,0},{12,4},{16,24},{20,28},{24,16},{28,20},{1,9},{5... | collective-permute-start | bytes 786440 | tf_op jit(solution)/shard_map/ppermute | solution.py:323
  116.6 8.9 %collective-permute-start.10 = (f32[640,128]{1,0:T(8,128)S(1)}, f32[640,128]{1,0:T(8,128)S(1)}, u32[]{:S(2)}, u32[]{:S(2)}) collective-permute-start(f32[640,128]{1,0:T(8,128)S(1)} %broadcast_select_fusion.6), channel_id=1, source_target_pairs={{0,1},{1,0},{2,3},{3,2},{4,5},{5,4},{6,7},{7,6},{8,9},{9,8},{10,11... | collective-permute-start | bytes 983048 | tf_op jit(solution)/shard_map/ppermute | solution.py:323
  120.6 35.6 %copy-start.8 = (f32[1024,128]{1,0:T(8,128)}, f32[1024,128]{1,0:T(8,128)S(1)}, u32[]{:S(2)}) copy-start(f32[1024,128]{1,0:T(8,128)S(1)} %maximum_select_fusion) | copy-start | bytes 1572868
  120.6 37.6 %collective-permute-start.21 = (f32[4,256,128]{2,1,0:T(8,128)S(1)}, f32[4,256,128]{2,1,0:T(8,128)S(1)}, u32[]{:S(2)}, u32[]{:S(2)}) collective-permute-start(f32[4,256,128]{2,1,0:T(8,128)S(1)} %bitcast.48), channel_id=1, source_target_pairs={{0,4},{4,0},{8,12},{12,8},{16,20},{20,16},{24,28},{28,24},{1,5},{5... | collective-permute-start | bytes 1572872 | tf_op jit(solution)/shard_map/ppermute | solution.py:323
  124.0 32.2 %copy-start.9 = (f32[1024,128]{1,0:T(8,128)}, f32[1024,128]{1,0:T(8,128)S(1)}, u32[]{:S(2)}) copy-start(f32[1024,128]{1,0:T(8,128)S(1)} %maximum_select_fusion.1) | copy-start | bytes 1572868
  124.0 34.1 %collective-permute-start.22 = (f32[4,256,128]{2,1,0:T(8,128)S(1)}, f32[4,256,128]{2,1,0:T(8,128)S(1)}, u32[]{:S(2)}, u32[]{:S(2)}) collective-permute-start(f32[4,256,128]{2,1,0:T(8,128)S(1)} %bitcast.50), channel_id=1, source_target_pairs={{0,4},{4,0},{8,12},{12,8},{16,20},{20,16},{24,28},{28,24},{1,5},{5... | collective-permute-start | bytes 1572872 | tf_op jit(solution)/shard_map/ppermute | solution.py:323
  152.6 5.6 %copy-start.5 = (f32[512,512]{1,0:T(8,128)}, f32[512,512]{1,0:T(8,128)S(1)}, u32[]{:S(2)}) copy-start(f32[512,512]{1,0:T(8,128)S(1)} %inverse_of_factor.1.x_ref.inv_ref) | copy-start | bytes 3145732
  156.2 1.0 copy-start.6
  (4 other events, 3.6 us)

commit v2 on v0

v2 whole, which is shorter than its diff:
```python
import functools

import jax
import jax.numpy as jnp
from jax import lax
from jax.experimental import pallas as pl
from jax.experimental.pallas import tpu as pltpu
from jax.sharding import PartitionSpec as P

HIGHEST = lax.Precision.HIGHEST
LANES = 128
SUB = 8
F32 = jnp.float32
BF16 = jnp.bfloat16


def params():
    return pltpu.CompilerParams(vmem_limit_bytes=48 * 1024 * 1024)


def vmem_spec():
    return pl.BlockSpec(memory_space=pltpu.VMEM)


def smem_spec():
    return pl.BlockSpec(memory_space=pltpu.SMEM)


def split(value):
    high = value.astype(BF16)
    return high, (value - high.astype(F32)).astype(BF16)


NN = (((1,), (0,)), ((), ()))
NT = (((1,), (1,)), ((), ()))


def dot3(left, right, dims=NN):
    def one(a, b):
        return lax.dot_general(a, b, dims, preferred_element_type=F32)

    return one(left[0], right[0]) + (one(left[0], right[1]) + one(left[1], right[0]))


def panel_kernel(x_ref, *refs):
    slabs, both, sems = refs[:-2], refs[-2], refs[-1]
    copies = [
        pltpu.make_async_copy(x_ref.at[:, 0, half], both.at[half], sems.at[half])
        for half in range(len(slabs))
    ]
    for copy in copies:
        copy.start()
    for half, slab in enumerate(slabs):
        copies[half].wait()
        slab[...] = both[half]


def own_panel(features):
    rows, panels, _, width = features.shape
    halves = width // LANES
    slab = jax.ShapeDtypeStruct((rows, LANES), F32)
    *slabs, both = pl.pallas_call(
        panel_kernel,
        in_specs=[pl.BlockSpec(memory_space=pltpu.HBM)],
        out_specs=[vmem_spec()] * (halves + 1),
        out_shape=[slab] * halves + [jax.ShapeDtypeStruct((halves, rows, LANES), F32)],
        scratch_shapes=[pltpu.SemaphoreType.DMA((halves,))],
        compiler_params=params(),
        cost_estimate=cost(2),
        name="own_panel",
    )(features.reshape(rows, panels, halves, LANES))
    return slabs, both


def any_spec():
    return pl.BlockSpec(memory_space=pl.ANY)


def cost(micros=0):
    return pl.CostEstimate(flops=1 + micros * 10 ** 9, bytes_accessed=1, transcendentals=0)


def held_kernel(value_ref, *refs):
    del value_ref, refs


def held(value, *after):
    return pl.pallas_call(
        held_kernel,
        in_specs=[any_spec()] * (1 + len(after)),
        out_specs=any_spec(),
        out_shape=jax.ShapeDtypeStruct(value.shape, value.dtype),
        input_output_aliases={0: 0},
        compiler_params=params(),
        cost_estimate=cost(),
        name="held",
    )(value, *after)


def halve_kernel(flag_ref, mine_ref, got_ref, *refs):
    keep_ref, give_ref = refs[-2:]
    half = keep_ref.shape[0]
    near = pl.multiple_of(flag_ref[0] * half, half)
    far = pl.multiple_of((1 - flag_ref[0]) * half, half)
    give_ref[...] = mine_ref[pl.ds(far, half), :] + got_ref[pl.ds(far, half), :]
    keep_ref[...] = mine_ref[pl.ds(near, half), :] + got_ref[pl.ds(near, half), :]


def halve(mine, got, flag, *after):
    rows, lanes = mine.shape
    half = jax.ShapeDtypeStruct((rows // 2, lanes), F32)
    return pl.pallas_call(
        halve_kernel,
        in_specs=[smem_spec()] + [vmem_spec()] * 2 + [any_spec()] * len(after),
        out_specs=[vmem_spec()] * 2,
        out_shape=[half, half],
        compiler_params=params(),
        cost_estimate=cost(),
        name="halve",
    )(flag.reshape(1), mine, got, *after)


def add_kernel(mine_ref, got_ref, *refs):
    refs[-1][...] = mine_ref[...] + got_ref[...]


def add(mine, got, *after):
    return pl.pallas_call(
        add_kernel,
        in_specs=[vmem_spec()] * 2 + [any_spec()] * len(after),
        out_specs=vmem_spec(),
        out_shape=jax.ShapeDtypeStruct(mine.shape, F32),
        compiler_params=params(),
        cost_estimate=cost(),
        name="add",
    )(mine, got, *after)


def join_kernel(flag_ref, mine_ref, got_ref, *refs):
    out_ref = refs[-1]
    half = mine_ref.shape[0]
    out_ref[pl.ds(pl.multiple_of(flag_ref[0] * half, half), half), :] = mine_ref[...]
    out_ref[pl.ds(pl.multiple_of((1 - flag_ref[0]) * half, half), half), :] = got_ref[...]


def join(mine, got, flag, *after):
    rows, lanes = mine.shape
    return pl.pallas_call(
        join_kernel,
        in_specs=[smem_spec()] + [vmem_spec()] * 2 + [any_spec()] * len(after),
        out_specs=vmem_spec(),
        out_shape=jax.ShapeDtypeStruct((2 * rows, lanes), F32),
        compiler_params=params(),
        cost_estimate=cost(),
        name="join",
    )(flag.reshape(1), mine, got, *after)


def gram_kernel(flags_ref, a_ref, b_ref, keep_ref, give_ref, work_ref):
    flag, core = flags_ref[0], flags_ref[1]

    def pick(zero, one):
        return jnp.where(core == 0, zero, one)

    own = jnp.concatenate([a_ref[0], a_ref[1]], axis=1)
    other = jnp.concatenate([b_ref[0], b_ref[1]], axis=1)
    first = pick(own, other)
    cross = pick(b_ref[0], a_ref[1])
    left = split(jnp.concatenate([own.T, cross.T], axis=0))
    width = own.shape[1]
    mine = dot3(tuple(part[:width] for part in left), split(own))
    mixed = dot3(tuple(part[width:] for part in left), split(first))
    parts = [mine[:LANES, :LANES], mine[LANES:, :LANES], mine[LANES:, LANES:],
             mixed[:, :LANES], mixed[:, LANES:]]
    for i, part in enumerate(parts):
        work_ref[i * LANES:(i + 1) * LANES, :] = part
    half = keep_ref.shape[0]
    keep_ref[...] = work_ref[pl.ds(pl.multiple_of(flag * half, half), half), :]
    give_ref[...] = work_ref[pl.ds(pl.multiple_of((1 - flag) * half, half), half), :]


def panel_gram(flags, own, other):
    half = jax.ShapeDtypeStruct((5 * LANES // 2, LANES), F32)
    return pl.pallas_call(
        gram_kernel,
        in_specs=[smem_spec(), vmem_spec(), vmem_spec()],
        out_specs=[vmem_spec()] * 2,
        out_shape=[half, half],
        scratch_shapes=[pltpu.VMEM((5 * LANES, LANES), F32)],
        compiler_params=params(),
        cost_estimate=cost(1),
        name="panel_gram",
    )(flags, own, other)


def fetch(x_ref, first, slabs_ref, sems):
    copies = []
    for i in range(slabs_ref.shape[0]):
        halves = x_ref.shape[2]
        source = x_ref.at[:, first + i // halves, i % halves]
        copies.append(pltpu.make_async_copy(source, slabs_ref.at[i], sems.at[i]))
    for copy in copies:
        copy.start()
    return copies


def times_columns(left, copies, slabs_ref, out_ref):
    for copy in copies:
        copy.wait()
    right = jnp.concatenate([slabs_ref[i] for i in range(slabs_ref.shape[0])], axis=1)
    value = dot3(left, split(right))
    height = value.shape[0]
    for i in range(slabs_ref.shape[0]):
        out_ref[i * height:(i + 1) * height, :] = value[:, i * LANES:(i + 1) * LANES]


def choose(flags_ref, own, other, got, twin):
    mine = jnp.where(flags_ref[2] == 1, own, got)
    paired = jnp.where(flags_ref[2] == 1, other, twin)
    zero = jnp.where(flags_ref[1] == 0, mine, paired)
    one = jnp.where(flags_ref[1] == 0, paired, mine)
    return zero, one


def product_kernel(flags_ref, x_ref, own_ref, other_ref, got_ref, twin_ref, *refs):
    give_ref, keep_ref, far_ref, near_ref, sems = refs[-5:]
    panels = x_ref.shape[1] // 2
    far = fetch(x_ref, (1 - flags_ref[0]) * panels, far_ref, sems.at[0])
    near = fetch(x_ref, flags_ref[0] * panels, near_ref, sems.at[1])
    zero, one = choose(flags_ref, own_ref[...], other_ref[...], got_ref[...], twin_ref[...])
    left = split(jnp.concatenate([zero, one], axis=1).T)
    times_columns(left, far, far_ref, give_ref)
    times_columns(left, near, near_ref, keep_ref)


def panel_products(flags, features, own, other, got, twin, *after):
    rows, panels, _, width = features.shape
    count = panels * width // LANES // 2
    x = features.reshape(rows, panels, width // LANES, LANES)
    out = jax.ShapeDtypeStruct((count * 2 * LANES, LANES), F32)
    return pl.pallas_call(
        product_kernel,
        in_specs=[smem_spec(), pl.BlockSpec(memory_space=pltpu.HBM)]
        + [vmem_spec()] * 4 + [any_spec()] * len(after),
        out_specs=[vmem_spec()] * 2,
        out_shape=[out, out],
        scratch_shapes=[pltpu.VMEM((count, rows, LANES), F32)] * 2
        + [pltpu.SemaphoreType.DMA((2, count))],
        compiler_params=params(),
        cost_estimate=cost(4),
        name="panel_products",
    )(flags, x, own, other, got, twin, *after)


def lane_copy(value, lane):
    return jnp.broadcast_to(value[:, lane:lane + 1], value.shape)


def row_copy(value, row):
    return jnp.broadcast_to(value[row:row + 1, :], value.shape)


def inverse_factor(block):
    groups = LANES // SUB
    lane = lax.broadcasted_iota(jnp.int32, (SUB, LANES), 1)
    sub = lax.broadcasted_iota(jnp.int32, (SUB, LANES), 0)
    work = [block[SUB * g:SUB * (g + 1), :] for g in range(groups)]
    result = []
    for g in range(groups):
        start = SUB * g
        panel = work[g]
        inside = (lane >= start) & (lane < start + SUB)
        cols = [lane_copy(panel, start + j) for j in range(SUB)]
        c = {(s, j): row_copy(cols[j], s) for j in range(SUB) for s in range(j, SUB)}
        mult, recip, diag = {}, [], []
        for i in range(0, SUB, 2):
            a, b, d = c[i, i], c[i + 1, i], c[i + 1, i + 1]
            det = a * d - b * b
            ra, rdet = 1.0 / a, 1.0 / det
            f = b * ra
            mult[i + 1, i] = f
            rb = a * rdet
            recip += [ra, rb]
            diag += [a, det * ra]
            for s in range(i + 2, SUB):
                mult[s, i] = c[s, i] * ra
                c[s, i + 1] = c[s, i + 1] - f * c[s, i]
                mult[s, i + 1] = c[s, i + 1] * rb
            for s in range(i + 2, SUB):
                for t in range(i + 2, s + 1):
                    c[s, t] = (c[s, t] - mult[s, i] * c[t, i]) - mult[s, i + 1] * c[t, i + 1]
        unit = jnp.where(inside, jnp.where(lane == start + sub, 1.0, 0.0), panel)
        upper = []
        for s in range(SUB):
            row = row_copy(unit, s)
            for i in range(s):
                row = row - mult[s, i] * upper[i]
            upper.append(row)
        scaled = [upper[s] * recip[s] for s in range(SUB)]
        nxt = g + 1
        if nxt < groups:
            old = work[nxt]
            new = jnp.where(inside, 0.0, old)
            v = []
            for j in range(SUB):
                e = lane_copy(old, start + j)
                for i in range(j):
                    e = e - mult[j, i] * v[i]
                v.append(e)
                new = new - e * scaled[j]
            work[nxt] = new
            nxt += 1
        if nxt < groups:
            solved = [None] * SUB
            for s in reversed(range(SUB)):
                row = scaled[s]
                for t in reversed(range(s + 1, SUB)):
                    row = row - mult[t, s] * solved[t]
                solved[s] = row
        for later in range(nxt, groups):
            old = work[later]
            new = jnp.where(inside, 0.0, old)
            for j in range(SUB):
                new = new - lane_copy(old, start + j) * solved[j]
            work[later] = new
        rows, dg = upper[0], diag[0]
        for s in range(1, SUB):
            rows = jnp.where(sub == s, upper[s], rows)
            dg = jnp.where(sub == s, diag[s], dg)
        result.append(jnp.where(lane < start + SUB, rows * lax.rsqrt(dg), 0.0))
    return jnp.concatenate(result, axis=0)


def dot6(a, b, dims=NN):
    return lax.dot_general(a, b, dims, precision=HIGHEST, preferred_element_type=F32)


STAGES = 4


def place(i, j):
    return i * (i + 1) // 2 + j


def stage(k, s):
    m = inverse_factor(s[k, k])
    for j in range(k):
        s[k, j] = dot6(m, s[k, j])
    low = {i: dot6(s[i, k], m, NT) for i in range(k + 1, STAGES)}
    s[k, k] = m
    for i in range(k + 1, STAGES):
        for j in range(k + 1, i + 1):
            s[i, j] = s[i, j] - dot6(low[i], low[j], NT)
        for j in range(k):
            s[i, j] = s[i, j] - dot6(low[i], s[k, j])
        s[i, k] = -dot6(low[i], m)


def first_stage_kernel(core_ref, mine_ref, twin_ref, *refs):
    out_ref = refs[-1]
    zero = jnp.where(core_ref[0] == 0, mine_ref[...], twin_ref[...])
    one = jnp.where(core_ref[0] == 0, twin_ref[...], mine_ref[...])

    def block(value, i):
        return value[i * LANES:(i + 1) * LANES]

    s = {
        (0, 0): block(zero, 0), (1, 0): block(zero, 1), (1, 1): block(zero, 2),
        (2, 0): block(zero, 3), (2, 1): block(zero, 4),
        (2, 2): block(one, 0), (3, 2): block(one, 1), (3, 3): block(one, 2),
        (3, 0): block(one, 3), (3, 1): block(one, 4),
    }
    stage(0, s)
    for (i, j), value in s.items():
        out_ref[place(i, j)] = value


def later_stage_kernel(k, in_ref, *refs):
    s = {(i, j): in_ref[place(i, j)] for i in range(STAGES) for j in range(i + 1)}
    stage(k, s)
    for (i, j), value in s.items():
        refs[-1][place(i, j)] = value


def stage_call(kernel, name, operands, scalars, after):
    return pl.pallas_call(
        kernel,
        in_specs=[smem_spec()] * scalars + [vmem_spec()] * (len(operands) - scalars)
        + [any_spec()] * len(after),
        out_specs=vmem_spec(),
        out_shape=jax.ShapeDtypeStruct((place(STAGES, 0), LANES, LANES), F32),
        compiler_params=params(),
        cost_estimate=cost(5),
        name=name,
    )(*operands, *after)


def first_stage(core, mine, twin, *after):
    return stage_call(first_stage_kernel, "factor_0", [core.reshape(1), mine, twin], 1, after)


def later_stage(k, state, *after):
    return stage_call(functools.partial(later_stage_kernel, k), "factor_%d" % k, [state], 0, after)


def packed(ref):
    zero = jnp.zeros((LANES, LANES), F32)
    rows = [
        jnp.concatenate([ref[place(i, j)] if j <= i else zero for j in range(STAGES)], axis=1)
        for i in range(STAGES)
    ]
    return jnp.concatenate(rows, axis=0)


def basis_kernel(flags_ref, *refs):
    halves = (len(refs) - 4) // 4
    x_ref, lines_ref, high_ref, low_ref = refs[-4:]
    zeros, ones = [], []
    for half in range(halves):
        zero, one = choose(flags_ref, *(ref[...] for ref in refs[4 * half:4 * half + 4]))
        zeros.append(zero)
        ones.append(one)
    rows = zeros[0].shape[0]
    panels = jnp.concatenate(zeros + ones, axis=1)
    q = dot3(split(panels), split(packed(x_ref)), NT)
    high, low = split(q)
    high_ref[...] = high
    low_ref[...] = low
    for panel in range(2):
        for half in range(2):
            k = 2 * panel + half
            lines_ref[pl.ds(2 * half + panel, rows, stride=4), :] = q[:, k * LANES:(k + 1) * LANES]


def panel_bases(flags, slabs, inverse):
    rows = slabs[0].shape[0]
    size = STAGES * LANES
    step = 256
    piece = pl.BlockSpec((step, LANES), lambda i: (i, 0))
    wide = pl.BlockSpec((step, size), lambda i: (i, 0))
    return pl.pallas_call(
        basis_kernel,
        grid=(rows // step,),
        in_specs=[smem_spec()] + [piece] * len(slabs) + [vmem_spec()],
        out_specs=[pl.BlockSpec((4 * step, LANES), lambda i: (i, 0)), wide, wide],
        out_shape=[
            jax.ShapeDtypeStruct((4 * rows, LANES), F32),
            jax.ShapeDtypeStruct((rows, size), BF16),
            jax.ShapeDtypeStruct((rows, size), BF16),
        ],
        compiler_params=params(),
        cost_estimate=cost(5),
        name="panel_bases",
    )(flags, *slabs, inverse)


def trailing_kernel(flags_ref, x_ref, qh_ref, ql_ref, inv_ref, h0_ref, h1_ref, *refs):
    factor_ref, out_ref, x_slabs, w_slabs, out_slabs, x_sems, w_sems, out_sems = refs[-8:]
    count, rows = x_slabs.shape[0], x_slabs.shape[1]
    halves = x_ref.shape[2]
    first = flags_ref[0] * x_ref.shape[1] // 2
    fetched = fetch(x_ref, first, x_slabs, x_sems)
    columns = []
    for i in range(count):
        at = [(2 * i + p) * LANES for p in range(2)]
        columns.append(jnp.concatenate([ref[a:a + LANES] for a in at for ref in (h0_ref, h1_ref)], axis=0))
    w = dot3(split(packed(inv_ref)), split(jnp.concatenate(columns, axis=1)))
    sent = []
    for i in range(count):
        w_slabs[i] = w[:, i * LANES:(i + 1) * LANES]
        target = factor_ref.at[:, first + i // halves, i % halves]
        sent.append(pltpu.make_async_copy(w_slabs.at[i], target, w_sems.at[i]))
        sent[-1].start()
    right = split(w)
    for copy in fetched:
        copy.wait()
    chunks = out_sems.shape[0]
    step = rows // chunks
    for chunk in range(chunks):
        here = pl.ds(chunk * step, step)
        term = dot3((qh_ref[here, :], ql_ref[here, :]), right)
        for i in range(count):
            out_slabs[i, here, :] = x_slabs[i, here, :] - term[:, i * LANES:(i + 1) * LANES]
            target = out_ref.at[here, first + i // halves, i % halves]
            sent.append(pltpu.make_async_copy(out_slabs.at[i, here], target, out_sems.at[chunk, i]))
            sent[-1].start()
    for copy in sent:
        copy.wait()


def finish(side, features, q_high, q_low, inverse, pieces, outs, *after):
    rows, panels, _, width = features.shape
    halves = width // LANES
    size = q_high.shape[1]
    count = panels * halves // 2
    x = features.reshape(rows, panels, halves, LANES)
    hbm = pl.BlockSpec(memory_space=pltpu.HBM)
    chunks = 4
    extra = len(outs)
    return pl.pallas_call(
        trailing_kernel,
        in_specs=[smem_spec(), hbm] + [vmem_spec()] * 5 + [hbm] * extra + [any_spec()] * len(after),
        out_specs=[hbm, hbm],
        out_shape=[
            jax.ShapeDtypeStruct((size, panels, halves, LANES), F32),
            jax.ShapeDtypeStruct(x.shape, F32),
        ],
        scratch_shapes=[
            pltpu.VMEM((count, rows, LANES), F32),
            pltpu.VMEM((count, size, LANES), F32),
            pltpu.VMEM((count, rows, LANES), F32),
            pltpu.SemaphoreType.DMA((count,)),
            pltpu.SemaphoreType.DMA((count,)),
            pltpu.SemaphoreType.DMA((chunks, count)),
        ],
        input_output_aliases={7 + i: i for i in range(extra)},
        compiler_params=params(),
        cost_estimate=cost(5),
        name="finish",
    )(side.reshape(1), x, q_high, q_low, inverse, *pieces, *outs, *after)


def swap(value, axis, size, bit):
    return lax.ppermute(value, axis, [(i, i ^ bit) for i in range(size)])


def spread(value, col, cols):
    got, span = None, 2
    while span < cols:
        new = lax.ppermute(value, "cols", [(i, i + span) for i in range(min(span, cols - span))])
        got = new if got is None else jnp.where(col < span, got, new)
        span *= 2
        if span < cols:
            value = jnp.where(col < 2, value, got)
    return got


def bits_of(size):
    bits, bit = [], 1
    while bit < size:
        bits.append(bit)
        bit *= 2
    return bits


def sum_steps(mine, got, row, rows):
    bits = bits_of(rows)[1:]
    after = yield
    for bit in bits:
        mine, give = halve(mine, got, (row // bit) % 2, after)
        got = swap(give, "rows", rows, bit)
        after = yield mine
    value = add(mine, got, after)
    for bit in reversed(bits):
        got = swap(value, "rows", rows, bit)
        after = yield value
        value = join(value, got, (row // bit) % 2, after)
    yield value


def program(rows_n, cols_n):
    bits = bits_of(rows_n)[1:]

    def on_device(features):
        rows, panels, _, width = features.shape
        halves = width // LANES
        row, col = lax.axis_index("rows"), lax.axis_index("cols")
        side, core, owner = row % 2, col % 2, (col < 2).astype(jnp.int32)
        slabs, own = own_panel(features)
        pieces = [spread(slab, col, cols_n) for slab in slabs]

        other = swap(own, "cols", cols_n, 1)
        gram, give = panel_gram(jnp.stack([side, core]), own, other)
        gram = add(gram, swap(give, "rows", rows_n, 1))

        flags = jnp.stack([side, core, owner])
        sums, shares = [], []
        for half in range(halves):
            piece = held(pieces[half], gram)
            twin = swap(piece, "cols", cols_n, 1)
            share = [slabs[half], other[half], piece, twin]
            give, keep = panel_products(flags, features, *share, gram)
            shares += share
            steps = sum_steps(keep, swap(give, "rows", rows_n, 1), row, rows_n)
            next(steps)
            sums.append(steps)
            if half < halves - 1:
                gram = add(gram, swap(gram, "rows", rows_n, bits[0]), give)

        lead, trail = sums
        last = lead.send(give)
        last = lead.send(last)
        for bit in bits[1:]:
            last = gram = add(gram, swap(gram, "rows", rows_n, bit), last)
        last = trail.send(last)
        gram = join(gram, swap(gram, "rows", rows_n, 1), side, last)
        last = lead.send(gram)
        arrived = spread(gram, col, cols_n)
        last = trail.send(last)
        gram = jnp.where(col < 2, gram, held(arrived, last))
        state = first_stage(core, gram, swap(gram, "cols", cols_n, 1), last)
        for k in range(1, STAGES - 1):
            near = lead.send(state)
            last = trail.send(near)
            state = later_stage(k, state, last)
        for _ in range(2 * len(bits) - 4):
            near = lead.send(state)
            last = trail.send(near)
        inverse = later_stage(STAGES - 1, state, last)
        far = trail.send(inverse)

        mine = [near, far]
        received = [swap(total, "rows", rows_n, 1) for total in mine]
        basis, q_high, q_low = panel_bases(flags, shares, inverse)
        outs = finish(side, features, q_high, q_low, inverse, mine, ())
        factor, trailing = finish(1 - side, features, q_high, q_low, inverse, received, outs)
        basis = basis.reshape(rows, halves, 2, LANES).transpose(0, 2, 1, 3).reshape(rows, 2, width)
        return (factor.reshape(2 * width, panels, 1, width), basis, trailing.reshape(features.shape))

    return on_device


def solution(mesh):
    placed = (P("rows", None, "cols", None),)
    return jax.shard_map(
        program(mesh.shape["rows"], mesh.shape["cols"]),
        mesh=mesh,
        in_specs=placed,
        out_specs=(
            P(None, None, "cols", None),
            P("rows", None, None),
            P("rows", None, "cols", None),
        ),
        check_vma=False,
    )
```

time: 591 us -> 145 us (0.25); the launches traced: 582 us -> 144 us
  waiting for transfers between devices: 363 us -> 49.3 us
  other arithmetic: 116 us -> 0.19 us
  Pallas kernels: 0 us -> 50.2 us
  local copies, waits for them, and re-layouts: 45.6 us -> 3.18 us
  starting transfers between devices: 0.46 us -> 40.3 us
  matrix products: 38 us -> 0 us
  between operations: 17.5 us -> 1.17 us
    psum x6 -> x0, waiting for transfers between devices: 363 us -> none  [the longest x2 152 us: factor_project(): return (basis, lax.psum(product(basis.T, block), 'rows'))]
    another operation x19 -> x2, other arithmetic: 110 us -> 0.15 us  [the longest x1 0.08 us: on_device(): flags = jnp.stack([side, core, owner])]
    pallas_call x0 -> x28, Pallas kernels: none -> 50.2 us  [the longest x4 19.8 us: stage_call(): pl.pallas_call(kernel, in_specs=[smem_spec()] * scalars + [vmem_spec()] *...]
    ppermute x0 -> x23, waiting for transfers between devices: none -> 49.3 us  [the longest x20 40.9 us: swap(): return lax.ppermute(value, axis, [(i, i ^ bit) for i in range(size)])]
    ppermute x0 -> x23, starting transfers between devices: none -> 40.3 us  [the longest x20 27 us: swap(): return lax.ppermute(value, axis, [(i, i ^ bit) for i in range(size)])]
    dot_general x6 -> x0, matrix products: 33.4 us -> none  [product(): return jnp.dot(left, right, precision=HIGHEST)]
    unnamed x13 -> x22, local copies, waits for them, and re-layouts: 27.9 us -> 3.11 us
    another operation x19 -> x0, local copies, waits for them, and re-layouts: 8.25 us -> none  [the longest x15 8.2 us: lower_solve(): lax.linalg.triangular_solve(lower, panel.T, left_side=True, lower=True)]
  transfers between devices with their start and end apart: 6 -> 23, of which waited for: 6 -> 13; matrix products, arithmetic and copies ran while one was open for 1% -> 0% of each run, Pallas kernels for 0% -> 26%
where the time goes in v2:
time: 145 us; the launch traced here: 144 us
  Pallas kernels  50.2 us (35%)
  waiting for transfers between devices  49.3 us (34%)
  starting transfers between devices  40.3 us (28%)
  local copies, waits for them, and re-layouts  3.18 us (2%)
    ppermute x20, waiting for transfers between devices, swap(): return lax.ppermute(value, axis, [(i, i ^ bit) for i in range(size)])  40.9 us
    ppermute x20, starting transfers between devices, swap(): return lax.ppermute(value, axis, [(i, i ^ bit) for i in range(size)])  27 us
    pallas_call x4, Pallas kernels, stage_call(): pl.pallas_call(kernel, in_specs=[smem_spec()] * scalars + [vmem_spec()] *...  19.8 us
    ppermute x3, starting transfers between devices, spread(): lax.ppermute(value, 'cols', [(i, i + span) for i in range(min(span, cols...  13.3 us
    pallas_call x2, Pallas kernels, panel_products(): pl.pallas_call(product_kernel, in_specs=[smem_spec(), pl.BlockSpec(memory...  9.97 us
    pallas_call x2, Pallas kernels, finish(): pl.pallas_call(trailing_kernel, in_specs=[smem_spec(), hbm] + [vmem_spec(...  9.7 us
    ppermute x3, waiting for transfers between devices, spread(): lax.ppermute(value, 'cols', [(i, i + span) for i in range(min(span, cols...  8.35 us
    pallas_call x1, Pallas kernels, panel_bases(): pl.pallas_call(basis_kernel, grid=(rows // step,), in_specs=[smem_spec()]...  5.13 us
  transfers between devices with their start and end apart: 23, of which 13 were waited for; matrix products, arithmetic and copies ran while one was open for 0% of the time, Pallas kernels for 26%

profile of v2, /device:TPU:0, one launch (start us, length us, event | category | flops | bytes accessed | tf_op | source)
XLA Modules:
  0.0 144.3 jit_solution(6221584749447240096)
XLA Ops:
  0.6 2.0 %own_panel.1 = (f32[1024,128]{1,0:T(8,128)S(1)}, f32[1024,128]{1,0:T(8,128)}, f32[2,1024,128]{2,1,0:T(8,128)S(1)}) custom-call(f32[1024,4,2,128]{3,2,1,0:T(2,128)} %bitcast.18), custom_call_target="tpu_custom_call" | custom-call | flops 2000000000 | bytes 1 | tf_op jit(solution)/shard_map/own_panel/pallas_call | solution.py:62
  3.2 4.4 %collective-permute-start.1 = (f32[1024,128]{1,0:T(8,128)S(1)}, f32[1024,128]{1,0:T(8,128)S(1)}, u32[]{:S(2)}, u32[]{:S(2)}) collective-permute-start(f32[1024,128]{1,0:T(8,128)S(1)} %get-tuple-element.27.own_ref.refs_0_), channel_id=1, source_target_pairs={{0,2},{1,3},{4,6},{5,7},{8,10},{9,11},{12,14},{13,15},{16,18},{17,... | collective-permute-start | bytes 1572872 | tf_op jit(solution)/shard_map/ppermute | solution.py:530
  9.2 1.6 %collective-permute-start.2 = (f32[320,128]{1,0:T(8,128)S(1)}, f32[320,128]{1,0:T(8,128)S(1)}, u32[]{:S(2)}, u32[]{:S(2)}) collective-permute-start(f32[320,128]{1,0:T(8,128)S(1)} %get-tuple-element.30), channel_id=1, source_target_pairs={{0,4},{4,0},{8,12},{12,8},{16,20},{20,16},{24,28},{28,24},{1,5},{5... | collective-permute-start | bytes 491528 | tf_op jit(solution)/shard_map/ppermute | solution.py:524
  10.8 4.8 %collective-permute-done.2.got_ref = f32[320,128]{1,0:T(8,128)S(1)} collective-permute-done((f32[320,128]{1,0:T(8,128)S(1)}, f32[320,128]{1,0:T(8,128)S(1)}, u32[]{:S(2)}, u32[]{:S(2)}) %collective-permute-start.2) | collective-permute-done | bytes 163872 | tf_op jit(solution)/shard_map/ppermute | solution.py:524
  15.6 3.8 %collective-permute-done.1.value_ref = f32[1024,128]{1,0:T(8,128)S(1)} collective-permute-done((f32[1024,128]{1,0:T(8,128)S(1)}, f32[1024,128]{1,0:T(8,128)S(1)}, u32[]{:S(2)}, u32[]{:S(2)}) %collective-permute-start.1) | collective-permute-done | bytes 524320 | tf_op jit(solution)/shard_map/ppermute | solution.py:530
  19.4 4.4 %collective-permute-start.4 = (f32[1024,128]{1,0:T(8,128)}, f32[1024,128]{1,0:T(8,128)S(1)}, u32[]{:S(2)}, u32[]{:S(2)}) collective-permute-start(f32[1024,128]{1,0:T(8,128)} %get-tuple-element.31.own_ref.refs_4_), channel_id=1, source_target_pairs={{0,2},{1,3},{4,6},{5,7},{8,10},{9,11},{12,14},{13,15},{16,18},{17,... | collective-permute-start | bytes 1572872 | tf_op jit(solution)/shard_map/ppermute | solution.py:530
  24.0 1.6 %collective-permute-start.5 = (f32[320,128]{1,0:T(8,128)S(1)}, f32[320,128]{1,0:T(8,128)S(1)}, u32[]{:S(2)}, u32[]{:S(2)}) collective-permute-start(f32[320,128]{1,0:T(8,128)S(1)} %add.36.refs_0_.mine_ref), channel_id=1, source_target_pairs={{0,8},{4,12},{8,0},{12,4},{16,24},{20,28},{24,16},{28,20},{1,9},{5... | collective-permute-start | bytes 491528 | tf_op jit(solution)/shard_map/ppermute | solution.py:524
  25.7 4.9 %panel_products.2 = (f32[1024,128]{1,0:T(8,128)}, f32[1024,128]{1,0:T(8,128)S(1)}) custom-call(s32[3]{0:T(128)S(1)} %pad_add_fusion.flags_ref, f32[1024,4,2,128]{3,2,1,0:T(2,128)} %bitcast.19, f32[1024,128]{1,0:T(8,128)S(1)} %get-tuple-element.27.own_ref.refs_0_, f32[1024,128]{1,0:T(8,128)S(1)} %get-tuple-element.55.other_ref.refs_1_, ...), custom_call_target="tpu_custom_call" | custom-call | flops 4000000000 | bytes 1 | tf_op jit(solution)/shard_map/panel_products/pallas_call | solution.py:241
  31.4 4.5 %collective-permute-done.4.value_ref = f32[1024,128]{1,0:T(8,128)S(1)} collective-permute-done((f32[1024,128]{1,0:T(8,128)}, f32[1024,128]{1,0:T(8,128)S(1)}, u32[]{:S(2)}, u32[]{:S(2)}) %collective-permute-start.4) | collective-permute-done | bytes 524320 | tf_op jit(solution)/shard_map/ppermute | solution.py:530
  37.9 5.1 %panel_products.3 = (f32[1024,128]{1,0:T(8,128)S(1)}, f32[1024,128]{1,0:T(8,128)S(1)}) custom-call(s32[3]{0:T(128)S(1)} %pad_add_fusion.flags_ref, f32[1024,4,2,128]{3,2,1,0:T(2,128)} %bitcast.20, f32[1024,128]{1,0:T(8,128)} %get-tuple-element.31.own_ref.refs_4_, f32[1024,128]{1,0:T(8,128)S(1)} %get-tuple-element.54.other_ref.refs_5_, ...), custom_call_target="tpu_custom_call" | custom-call | flops 4000000000 | bytes 1 | tf_op jit(solution)/shard_map/panel_products/pallas_call | solution.py:241
  44.6 6.4 %collective-permute-done.8.got_ref = f32[1024,128]{1,0:T(8,128)} collective-permute-done((f32[1024,128]{1,0:T(8,128)}, f32[1024,128]{1,0:T(8,128)}, u32[]{:S(2)}, u32[]{:S(2)}) %collective-permute-start.8) | collective-permute-done | bytes 524320 | tf_op jit(solution)/shard_map/ppermute | solution.py:524
  52.1 1.8 %halve.4 = (f32[512,128]{1,0:T(8,128)S(1)}, f32[512,128]{1,0:T(8,128)}) custom-call(s32[1]{0:T(128)} %bitcast.8.flag_ref, f32[1024,128]{1,0:T(8,128)S(1)} %copy-done.1, f32[1024,128]{1,0:T(8,128)} %collective-permute-done.8.got_ref, f32[1024,128]{1,0:T(8,128)S(1)} %get-tuple-element.34.refs_0_), custom_call_target="tpu_custom_call" | custom-call | flops 1 | bytes 1 | tf_op jit(solution)/shard_map/halve/pallas_call | solution.py:112
  55.4 2.6 %collective-permute-start.7 = (f32[320,128]{1,0:T(8,128)S(1)}, f32[320,128]{1,0:T(8,128)S(1)}, u32[]{:S(2)}, u32[]{:S(2)}) collective-permute-start(f32[320,128]{1,0:T(8,128)S(1)} %add.37.refs_0_.mine_ref), channel_id=1, source_target_pairs={{0,16},{4,20},{8,24},{12,28},{16,0},{20,4},{24,8},{28,12},{1,17},{... | collective-permute-start | bytes 491528 | tf_op jit(solution)/shard_map/ppermute | solution.py:524
  58.0 7.1 %collective-permute-done.9.got_ref = f32[512,128]{1,0:T(8,128)S(1)} collective-permute-done((f32[512,128]{1,0:T(8,128)}, f32[512,128]{1,0:T(8,128)S(1)}, u32[]{:S(2)}, u32[]{:S(2)}) %collective-permute-start.9) | collective-permute-done | bytes 262176 | tf_op jit(solution)/shard_map/ppermute | solution.py:524
  66.9 3.7 %collective-permute-done.10.got_ref = f32[320,128]{1,0:T(8,128)S(1)} collective-permute-done((f32[320,128]{1,0:T(8,128)S(1)}, f32[320,128]{1,0:T(8,128)S(1)}, u32[]{:S(2)}, u32[]{:S(2)}) %collective-permute-start.10) | collective-permute-done | bytes 163872 | tf_op jit(solution)/shard_map/ppermute | solution.py:524
  70.6 4.5 %collective-permute-start.12 = (f32[640,128]{1,0:T(8,128)S(1)}, f32[640,128]{1,0:T(8,128)S(1)}, u32[]{:S(2)}, u32[]{:S(2)}) collective-permute-start(f32[640,128]{1,0:T(8,128)S(1)} %join.5.refs_0_), channel_id=1, source_target_pairs={{0,2},{1,3},{4,6},{5,7},{8,10},{9,11},{12,14},{13,15},{16,18},{17,... | collective-permute-start | bytes 983048 | tf_op jit(solution)/shard_map/ppermute | solution.py:530
  75.1 2.6 %collective-permute-start.13 = (f32[512,128]{1,0:T(8,128)S(1)}, f32[512,128]{1,0:T(8,128)S(1)}, u32[]{:S(2)}, u32[]{:S(2)}) collective-permute-start(f32[512,128]{1,0:T(8,128)S(1)} %get-tuple-element.40), channel_id=1, source_target_pairs={{0,8},{4,12},{8,0},{12,4},{16,24},{20,28},{24,16},{28,20},{1,9},{5... | collective-permute-start | bytes 786440 | tf_op jit(solution)/shard_map/ppermute | solution.py:524
  77.7 1.6 %collective-permute-start.14 = (f32[256,128]{1,0:T(8,128)S(1)}, f32[256,128]{1,0:T(8,128)S(1)}, u32[]{:S(2)}, u32[]{:S(2)}) collective-permute-start(f32[256,128]{1,0:T(8,128)S(1)} %get-tuple-element.41), channel_id=1, source_target_pairs={{0,16},{4,20},{8,24},{12,28},{16,0},{20,4},{24,8},{28,12},{1,17},{... | collective-permute-start | bytes 393224 | tf_op jit(solution)/shard_map/ppermute | solution.py:524
  79.3 4.4 %collective-permute-done.14.got_ref = f32[256,128]{1,0:T(8,128)S(1)} collective-permute-done((f32[256,128]{1,0:T(8,128)S(1)}, f32[256,128]{1,0:T(8,128)S(1)}, u32[]{:S(2)}, u32[]{:S(2)}) %collective-permute-start.14) | collective-permute-done | bytes 131104 | tf_op jit(solution)/shard_map/ppermute | solution.py:524
  84.2 2.7 %collective-permute-start.17 = (f32[256,128]{1,0:T(8,128)S(1)}, f32[256,128]{1,0:T(8,128)S(1)}, u32[]{:S(2)}, u32[]{:S(2)}) collective-permute-start(f32[256,128]{1,0:T(8,128)S(1)} %add.39.refs_0_.mine_ref), channel_id=1, source_target_pairs={{0,16},{4,20},{8,24},{12,28},{16,0},{20,4},{24,8},{28,12},{1,17},{... | collective-permute-start | bytes 393224 | tf_op jit(solution)/shard_map/ppermute | solution.py:524
  87.2 5.4 %factor_0.1.refs_0_.in_ref = f32[10,128,128]{2,1,0:T(8,128)S(1)} custom-call(s32[1]{0:T(128)} %bitcast.3.core_ref, f32[640,128]{1,0:T(8,128)S(1)} %broadcast_select_fusion.mine_ref, f32[640,128]{1,0:T(8,128)S(1)} %collective-permute-done.15.twin_ref, f32[256,128]{1,0:T(8,128)S(1)} %get-tuple-element.42.refs_0_.mine_ref), custom_call_target="tpu_custom_call" | custom-call | flops 5000000000 | bytes 1 | tf_op jit(solution)/shard_map/factor_0/pallas_call | solution.py:386
  92.6 4.4 %collective-permute-done.17.got_ref = f32[256,128]{1,0:T(8,128)S(1)} collective-permute-done((f32[256,128]{1,0:T(8,128)S(1)}, f32[256,128]{1,0:T(8,128)S(1)}, u32[]{:S(2)}, u32[]{:S(2)}) %collective-permute-start.17) | collective-permute-done | bytes 131104 | tf_op jit(solution)/shard_map/ppermute | solution.py:524
  97.5 1.9 %collective-permute-done.16.got_ref = f32[256,128]{1,0:T(8,128)S(1)} collective-permute-done((f32[256,128]{1,0:T(8,128)S(1)}, f32[256,128]{1,0:T(8,128)S(1)}, u32[]{:S(2)}, u32[]{:S(2)}) %collective-permute-start.16) | collective-permute-done | bytes 131104 | tf_op jit(solution)/shard_map/ppermute | solution.py:524
  101.0 4.9 %factor_1.1.refs_0_.in_ref = f32[10,128,128]{2,1,0:T(8,128)S(1)} custom-call(f32[10,128,128]{2,1,0:T(8,128)S(1)} %factor_0.1.refs_0_.in_ref, f32[256,128]{1,0:T(8,128)S(1)} %add.40.refs_0_.mine_ref), custom_call_target="tpu_custom_call" | custom-call | flops 5000000000 | bytes 1 | tf_op jit(solution)/shard_map/factor_1/pallas_call | solution.py:386
  105.9 2.0 %collective-permute-done.19.got_ref = f32[512,128]{1,0:T(8,128)S(1)} collective-permute-done((f32[512,128]{1,0:T(8,128)S(1)}, f32[512,128]{1,0:T(8,128)S(1)}, u32[]{:S(2)}, u32[]{:S(2)}) %collective-permute-start.19) | collective-permute-done | bytes 262176 | tf_op jit(solution)/shard_map/ppermute | solution.py:524
  107.9 5.3 %factor_2.1.in_ref = f32[10,128,128]{2,1,0:T(8,128)S(1)} custom-call(f32[10,128,128]{2,1,0:T(8,128)S(1)} %factor_1.1.refs_0_.in_ref, f32[512,128]{1,0:T(8,128)S(1)} %join.8.refs_0_.mine_ref), custom_call_target="tpu_custom_call" | custom-call | flops 5000000000 | bytes 1 | tf_op jit(solution)/shard_map/factor_2/pallas_call | solution.py:386
  113.3 2.1 %collective-permute-start.21 = (f32[512,128]{1,0:T(8,128)S(1)}, f32[512,128]{1,0:T(8,128)S(1)}, u32[]{:S(2)}, u32[]{:S(2)}) collective-permute-start(f32[512,128]{1,0:T(8,128)S(1)} %join.8.refs_0_.mine_ref), channel_id=1, source_target_pairs={{0,8},{4,12},{8,0},{12,4},{16,24},{20,28},{24,16},{28,20},{1,9},{5... | collective-permute-start | bytes 786440 | tf_op jit(solution)/shard_map/ppermute | solution.py:524
  116.9 4.2 %factor_3.1.refs_8_.refs_0_.inv_ref = f32[10,128,128]{2,1,0:T(8,128)S(1)} custom-call(f32[10,128,128]{2,1,0:T(8,128)S(1)} %factor_2.1.in_ref, f32[512,128]{1,0:T(8,128)S(1)} %join.8.refs_0_.mine_ref), custom_call_target="tpu_custom_call" | custom-call | flops 5000000000 | bytes 1 | tf_op jit(solution)/shard_map/factor_3/pallas_call | solution.py:386
  122.6 5.1 %panel_bases.1 = (f32[4096,128]{1,0:T(8,128)}, bf16[1024,512]{1,0:T(8,128)(2,1)S(1)}, bf16[1024,512]{1,0:T(8,128)(2,1)}) custom-call(s32[3]{0:T(128)S(1)} %pad_add_fusion.flags_ref, f32[1024,128]{1,0:T(8,128)S(1)} %copy-done.7, f32[1024,128]{1,0:T(8,128)S(1)} %copy-done.5, f32[1024,128]{1,0:T(8,128)S(1)} %held.3.got_ref.refs_2_, ...), custom_call_target="tpu_custom_call" | custom-call | flops 5000000000 | bytes 1 | tf_op jit(solution)/shard_map/panel_bases/pallas_call | solution.py:441
  128.9 4.8 %finish.2 = (f32[512,4,2,128]{3,2,1,0:T(2,128)}, f32[1024,4,2,128]{3,2,1,0:T(2,128)}) custom-call(s32[1]{0:T(128)} %bitcast.2.flag_ref.flags_ref, f32[1024,4,2,128]{3,2,1,0:T(2,128)} %bitcast.21, bf16[1024,512]{1,0:T(8,128)(2,1)S(1)} %get-tuple-element.44.qh_ref, bf16[1024,512]{1,0:T(8,128)(2,1)S(1)} %copy-done.10, ...), custom_call_target="tpu_custom_call" | custom-call | flops 5000000000 | bytes 1 | tf_op jit(solution)/shard_map/finish/pallas_call | solution.py:500
  133.8 5.5 %collective-permute-done.22.h1_ref = f32[1024,128]{1,0:T(8,128)S(1)} collective-permute-done((f32[1024,128]{1,0:T(8,128)S(1)}, f32[1024,128]{1,0:T(8,128)S(1)}, u32[]{:S(2)}, u32[]{:S(2)}) %collective-permute-start.22) | collective-permute-done | bytes 524320 | tf_op jit(solution)/shard_map/ppermute | solution.py:524
  139.3 4.9 %finish.3 = (f32[512,4,2,128]{3,2,1,0:T(2,128)}, f32[1024,4,2,128]{3,2,1,0:T(2,128)}) custom-call(s32[1]{0:T(128)} %bitcast.flags_ref, f32[1024,4,2,128]{3,2,1,0:T(2,128)} %bitcast.22, bf16[1024,512]{1,0:T(8,128)(2,1)S(1)} %get-tuple-element.44.qh_ref, bf16[1024,512]{1,0:T(8,128)(2,1)S(1)} %copy-done.10, ...), custom_call_target="tpu_custom_call", output_to_operand_aliasing={{0}: (7, {}), {1}: (8, {})} | custom-call | flops 5000000000 | bytes 1 | tf_op jit(solution)/shard_map/finish/pallas_call | solution.py:500
  (68 shorter events, 17.9 us)
Async XLA Ops:
  2.7 27.9 %copy-start.6 = (f32[1024,128]{1,0:T(8,128)}, f32[1024,128]{1,0:T(8,128)S(1)}, u32[]{:S(2)}) copy-start(f32[1024,128]{1,0:T(8,128)S(1)} %get-tuple-element.27.own_ref.refs_0_) | copy-start | bytes 1572868
  2.7 5.1 %collective-permute-start = (f32[2,1024,128]{2,1,0:T(8,128)S(1)}, f32[2,1024,128]{2,1,0:T(8,128)S(1)}, u32[]{:S(2)}, u32[]{:S(2)}) collective-permute-start(f32[2,1024,128]{2,1,0:T(8,128)S(1)} %get-tuple-element.28.a_ref), channel_id=1, source_target_pairs={{0,1},{1,0},{2,3},{3,2},{4,5},{5,4},{6,7},{7,6},{8,9},{9,8},{10,11... | collective-permute-start | bytes 3145736 | tf_op jit(solution)/shard_map/ppermute | solution.py:524
  3.2 16.2 %collective-permute-start.1 = (f32[1024,128]{1,0:T(8,128)S(1)}, f32[1024,128]{1,0:T(8,128)S(1)}, u32[]{:S(2)}, u32[]{:S(2)}) collective-permute-start(f32[1024,128]{1,0:T(8,128)S(1)} %get-tuple-element.27.own_ref.refs_0_), channel_id=1, source_target_pairs={{0,2},{1,3},{4,6},{5,7},{8,10},{9,11},{12,14},{13,15},{16,18},{17,... | collective-permute-start | bytes 1572872 | tf_op jit(solution)/shard_map/ppermute | solution.py:530
  9.2 6.4 %collective-permute-start.2 = (f32[320,128]{1,0:T(8,128)S(1)}, f32[320,128]{1,0:T(8,128)S(1)}, u32[]{:S(2)}, u32[]{:S(2)}) collective-permute-start(f32[320,128]{1,0:T(8,128)S(1)} %get-tuple-element.30), channel_id=1, source_target_pairs={{0,4},{4,0},{8,12},{12,8},{16,20},{20,16},{24,28},{28,24},{1,5},{5... | collective-permute-start | bytes 491528 | tf_op jit(solution)/shard_map/ppermute | solution.py:524
  19.4 6.2 %collective-permute-start.3 = (f32[1024,128]{1,0:T(8,128)S(1)}, f32[1024,128]{1,0:T(8,128)}, u32[]{:S(2)}, u32[]{:S(2)}) collective-permute-start(f32[1024,128]{1,0:T(8,128)S(1)} %held.3.got_ref.refs_2_), channel_id=1, source_target_pairs={{0,1},{1,0},{2,3},{3,2},{4,5},{5,4},{6,7},{7,6},{8,9},{9,8},{10,11... | collective-permute-start | bytes 1572872 | tf_op jit(solution)/shard_map/ppermute | solution.py:524
  19.4 16.5 %collective-permute-start.4 = (f32[1024,128]{1,0:T(8,128)}, f32[1024,128]{1,0:T(8,128)S(1)}, u32[]{:S(2)}, u32[]{:S(2)}) collective-permute-start(f32[1024,128]{1,0:T(8,128)} %get-tuple-element.31.own_ref.refs_4_), channel_id=1, source_target_pairs={{0,2},{1,3},{4,6},{5,7},{8,10},{9,11},{12,14},{13,15},{16,18},{17,... | collective-permute-start | bytes 1572872 | tf_op jit(solution)/shard_map/ppermute | solution.py:530
  24.0 6.6 %copy-start.4 = (f32[1024,128]{1,0:T(8,128)}, f32[1024,128]{1,0:T(8,128)S(1)}, u32[]{:S(2)}) copy-start(f32[1024,128]{1,0:T(8,128)S(1)} %get-tuple-element.55.other_ref.refs_1_) | copy-start | bytes 1572868
  24.0 13.9 %copy-start.2 = (f32[1024,128]{1,0:T(8,128)}, f32[1024,128]{1,0:T(8,128)S(1)}, u32[]{:S(2)}) copy-start(f32[1024,128]{1,0:T(8,128)S(1)} %get-tuple-element.54.other_ref.refs_5_) | copy-start | bytes 1572868
  24.0 7.4 %collective-permute-start.5 = (f32[320,128]{1,0:T(8,128)S(1)}, f32[320,128]{1,0:T(8,128)S(1)}, u32[]{:S(2)}, u32[]{:S(2)}) collective-permute-start(f32[320,128]{1,0:T(8,128)S(1)} %add.36.refs_0_.mine_ref), channel_id=1, source_target_pairs={{0,8},{4,12},{8,0},{12,4},{16,24},{20,28},{24,16},{28,20},{1,9},{5... | collective-permute-start | bytes 491528 | tf_op jit(solution)/shard_map/ppermute | solution.py:524
  36.0 1.9 %collective-permute-start.6 = (f32[1024,128]{1,0:T(8,128)S(1)}, f32[1024,128]{1,0:T(8,128)S(1)}, u32[]{:S(2)}, u32[]{:S(2)}) collective-permute-start(f32[1024,128]{1,0:T(8,128)S(1)} %held.4.got_ref.refs_6_), channel_id=1, source_target_pairs={{0,1},{1,0},{2,3},{3,2},{4,5},{5,4},{6,7},{7,6},{8,9},{9,8},{10,11... | collective-permute-start | bytes 1572872 | tf_op jit(solution)/shard_map/ppermute | solution.py:524
  36.0 15.0 %collective-permute-start.8 = (f32[1024,128]{1,0:T(8,128)}, f32[1024,128]{1,0:T(8,128)}, u32[]{:S(2)}, u32[]{:S(2)}) collective-permute-start(f32[1024,128]{1,0:T(8,128)} %get-tuple-element.32.refs_0_), channel_id=1, source_target_pairs={{0,4},{4,0},{8,12},{12,8},{16,20},{20,16},{24,28},{28,24},{1,5},{5... | collective-permute-start | bytes 1572872 | tf_op jit(solution)/shard_map/ppermute | solution.py:524
  37.9 5.1 %copy-start.8 = (f32[1024,128]{1,0:T(8,128)}, f32[1024,128]{1,0:T(8,128)S(1)}, u32[]{:S(2)}) copy-start(f32[1024,128]{1,0:T(8,128)S(1)} %collective-permute-done.6.twin_ref.refs_7_) | copy-start | bytes 1572868
  43.0 23.8 %collective-permute-start.11 = (f32[1024,128]{1,0:T(8,128)S(1)}, f32[1024,128]{1,0:T(8,128)S(1)}, u32[]{:S(2)}, u32[]{:S(2)}) collective-permute-start(f32[1024,128]{1,0:T(8,128)S(1)} %get-tuple-element.34.refs_0_), channel_id=1, source_target_pairs={{0,4},{4,0},{8,12},{12,8},{16,20},{20,16},{24,28},{28,24},{1,5},{5... | collective-permute-start | bytes 1572872 | tf_op jit(solution)/shard_map/ppermute | solution.py:524
  53.9 11.3 %collective-permute-start.9 = (f32[512,128]{1,0:T(8,128)}, f32[512,128]{1,0:T(8,128)S(1)}, u32[]{:S(2)}, u32[]{:S(2)}) collective-permute-start(f32[512,128]{1,0:T(8,128)} %get-tuple-element.36), channel_id=1, source_target_pairs={{0,8},{4,12},{8,0},{12,4},{16,24},{20,28},{24,16},{28,20},{1,9},{5... | collective-permute-start | bytes 786440 | tf_op jit(solution)/shard_map/ppermute | solution.py:524
  55.4 9.7 %collective-permute-start.7 = (f32[320,128]{1,0:T(8,128)S(1)}, f32[320,128]{1,0:T(8,128)S(1)}, u32[]{:S(2)}, u32[]{:S(2)}) collective-permute-start(f32[320,128]{1,0:T(8,128)S(1)} %add.37.refs_0_.mine_ref), channel_id=1, source_target_pairs={{0,16},{4,20},{8,24},{12,28},{16,0},{20,4},{24,8},{28,12},{1,17},{... | collective-permute-start | bytes 491528 | tf_op jit(solution)/shard_map/ppermute | solution.py:524
  65.2 5.4 %collective-permute-start.10 = (f32[320,128]{1,0:T(8,128)S(1)}, f32[320,128]{1,0:T(8,128)S(1)}, u32[]{:S(2)}, u32[]{:S(2)}) collective-permute-start(f32[320,128]{1,0:T(8,128)S(1)} %add.38.refs_0_.mine_ref), channel_id=1, source_target_pairs={{0,4},{4,0},{8,12},{12,8},{16,20},{20,16},{24,28},{28,24},{1,5},{5... | collective-permute-start | bytes 491528 | tf_op jit(solution)/shard_map/ppermute | solution.py:524
  70.6 13.4 %collective-permute-start.12 = (f32[640,128]{1,0:T(8,128)S(1)}, f32[640,128]{1,0:T(8,128)S(1)}, u32[]{:S(2)}, u32[]{:S(2)}) collective-permute-start(f32[640,128]{1,0:T(8,128)S(1)} %join.5.refs_0_), channel_id=1, source_target_pairs={{0,2},{1,3},{4,6},{5,7},{8,10},{9,11},{12,14},{13,15},{16,18},{17,... | collective-permute-start | bytes 983048 | tf_op jit(solution)/shard_map/ppermute | solution.py:530
  75.1 8.9 %collective-permute-start.13 = (f32[512,128]{1,0:T(8,128)S(1)}, f32[512,128]{1,0:T(8,128)S(1)}, u32[]{:S(2)}, u32[]{:S(2)}) collective-permute-start(f32[512,128]{1,0:T(8,128)S(1)} %get-tuple-element.40), channel_id=1, source_target_pairs={{0,8},{4,12},{8,0},{12,4},{16,24},{20,28},{24,16},{28,20},{1,9},{5... | collective-permute-start | bytes 786440 | tf_op jit(solution)/shard_map/ppermute | solution.py:524
  77.7 6.1 %collective-permute-start.14 = (f32[256,128]{1,0:T(8,128)S(1)}, f32[256,128]{1,0:T(8,128)S(1)}, u32[]{:S(2)}, u32[]{:S(2)}) collective-permute-start(f32[256,128]{1,0:T(8,128)S(1)} %get-tuple-element.41), channel_id=1, source_target_pairs={{0,16},{4,20},{8,24},{12,28},{16,0},{20,4},{24,8},{28,12},{1,17},{... | collective-permute-start | bytes 393224 | tf_op jit(solution)/shard_map/ppermute | solution.py:524
  84.1 3.1 %collective-permute-start.15 = (f32[640,128]{1,0:T(8,128)S(1)}, f32[640,128]{1,0:T(8,128)S(1)}, u32[]{:S(2)}, u32[]{:S(2)}) collective-permute-start(f32[640,128]{1,0:T(8,128)S(1)} %broadcast_select_fusion.mine_ref), channel_id=1, source_target_pairs={{0,1},{1,0},{2,3},{3,2},{4,5},{5,4},{6,7},{7,6},{8,9},{9,8},{10,11... | collective-permute-start | bytes 983048 | tf_op jit(solution)/shard_map/ppermute | solution.py:524
  84.2 12.9 %collective-permute-start.17 = (f32[256,128]{1,0:T(8,128)S(1)}, f32[256,128]{1,0:T(8,128)S(1)}, u32[]{:S(2)}, u32[]{:S(2)}) collective-permute-start(f32[256,128]{1,0:T(8,128)S(1)} %add.39.refs_0_.mine_ref), channel_id=1, source_target_pairs={{0,16},{4,20},{8,24},{12,28},{16,0},{20,4},{24,8},{28,12},{1,17},{... | collective-permute-start | bytes 393224 | tf_op jit(solution)/shard_map/ppermute | solution.py:524
  86.9 12.6 %collective-permute-start.16 = (f32[256,128]{1,0:T(8,128)S(1)}, f32[256,128]{1,0:T(8,128)S(1)}, u32[]{:S(2)}, u32[]{:S(2)}) collective-permute-start(f32[256,128]{1,0:T(8,128)S(1)} %get-tuple-element.43), channel_id=1, source_target_pairs={{0,16},{4,20},{8,24},{12,28},{16,0},{20,4},{24,8},{28,12},{1,17},{... | collective-permute-start | bytes 393224 | tf_op jit(solution)/shard_map/ppermute | solution.py:524
  97.1 10.8 %collective-permute-start.19 = (f32[512,128]{1,0:T(8,128)S(1)}, f32[512,128]{1,0:T(8,128)S(1)}, u32[]{:S(2)}, u32[]{:S(2)}) collective-permute-start(f32[512,128]{1,0:T(8,128)S(1)} %join.6.refs_0_.mine_ref), channel_id=1, source_target_pairs={{0,8},{4,12},{8,0},{12,4},{16,24},{20,28},{24,16},{28,20},{1,9},{5... | collective-permute-start | bytes 786440 | tf_op jit(solution)/shard_map/ppermute | solution.py:524
  99.5 8.4 %collective-permute-start.18 = (f32[256,128]{1,0:T(8,128)S(1)}, f32[256,128]{1,0:T(8,128)S(1)}, u32[]{:S(2)}, u32[]{:S(2)}) collective-permute-start(f32[256,128]{1,0:T(8,128)S(1)} %add.40.refs_0_.mine_ref), channel_id=1, source_target_pairs={{0,16},{4,20},{8,24},{12,28},{16,0},{20,4},{24,8},{28,12},{1,17},{... | collective-permute-start | bytes 393224 | tf_op jit(solution)/shard_map/ppermute | solution.py:524
  113.2 9.3 %copy-start.3 = (f32[1024,128]{1,0:T(8,128)S(1)}, f32[1024,128]{1,0:T(8,128)}, u32[]{:S(2)}) copy-start(f32[1024,128]{1,0:T(8,128)} %copy-done.2) | copy-start | bytes 1572868
  113.2 9.3 %copy-start.5 = (f32[1024,128]{1,0:T(8,128)S(1)}, f32[1024,128]{1,0:T(8,128)}, u32[]{:S(2)}) copy-start(f32[1024,128]{1,0:T(8,128)} %copy-done.4) | copy-start | bytes 1572868
  113.3 9.3 %copy-start.7 = (f32[1024,128]{1,0:T(8,128)S(1)}, f32[1024,128]{1,0:T(8,128)}, u32[]{:S(2)}) copy-start(f32[1024,128]{1,0:T(8,128)} %copy-done.6) | copy-start | bytes 1572868
  113.3 9.3 %copy-start.9 = (f32[1024,128]{1,0:T(8,128)S(1)}, f32[1024,128]{1,0:T(8,128)}, u32[]{:S(2)}) copy-start(f32[1024,128]{1,0:T(8,128)} %copy-done.8) | copy-start | bytes 1572868
  113.3 7.7 %collective-permute-start.21 = (f32[512,128]{1,0:T(8,128)S(1)}, f32[512,128]{1,0:T(8,128)S(1)}, u32[]{:S(2)}, u32[]{:S(2)}) collective-permute-start(f32[512,128]{1,0:T(8,128)S(1)} %join.8.refs_0_.mine_ref), channel_id=1, source_target_pairs={{0,8},{4,12},{8,0},{12,4},{16,24},{20,28},{24,16},{28,20},{1,9},{5... | collective-permute-start | bytes 786440 | tf_op jit(solution)/shard_map/ppermute | solution.py:524
  115.3 18.4 %collective-permute-start.20 = (f32[1024,128]{1,0:T(8,128)S(1)}, f32[1024,128]{1,0:T(8,128)S(1)}, u32[]{:S(2)}, u32[]{:S(2)}) collective-permute-start(f32[1024,128]{1,0:T(8,128)S(1)} %join.7.refs_0_.h0_ref), channel_id=1, source_target_pairs={{0,4},{4,0},{8,12},{12,8},{16,20},{20,16},{24,28},{28,24},{1,5},{5... | collective-permute-start | bytes 1572872 | tf_op jit(solution)/shard_map/ppermute | solution.py:524
  121.1 18.2 %collective-permute-start.22 = (f32[1024,128]{1,0:T(8,128)S(1)}, f32[1024,128]{1,0:T(8,128)S(1)}, u32[]{:S(2)}, u32[]{:S(2)}) collective-permute-start(f32[1024,128]{1,0:T(8,128)S(1)} %join.9.h1_ref), channel_id=1, source_target_pairs={{0,4},{4,0},{8,12},{12,8},{16,20},{20,16},{24,28},{28,24},{1,5},{5... | collective-permute-start | bytes 1572872 | tf_op jit(solution)/shard_map/ppermute | solution.py:524
  127.7 1.2 copy-start.10
  (2 other events, 1.9 us)

commit v3 on v2

--- a/solution.py
+++ b/solution.py
@@ -390,7 +390,7 @@
         out_specs=vmem_spec(),
         out_shape=jax.ShapeDtypeStruct((place(STAGES, 0), LANES, LANES), F32),
         compiler_params=params(),
-        cost_estimate=cost(5),
+        cost_estimate=cost(),
         name=name,
     )(*operands, *after)
 
@@ -413,8 +413,8 @@
 
 
 def basis_kernel(flags_ref, *refs):
-    halves = (len(refs) - 4) // 4
-    x_ref, lines_ref, high_ref, low_ref = refs[-4:]
+    halves = (len(refs) - 5) // 4
+    x_ref, lines_ref, high_ref, low_ref = refs[4 * halves], *refs[-3:]
     zeros, ones = [], []
     for half in range(halves):
         zero, one = choose(flags_ref, *(ref[...] for ref in refs[4 * half:4 * half + 4]))
@@ -432,7 +432,7 @@
             lines_ref[pl.ds(2 * half + panel, rows, stride=4), :] = q[:, k * LANES:(k + 1) * LANES]
 
 
-def panel_bases(flags, slabs, inverse):
+def panel_bases(flags, slabs, inverse, after):
     rows = slabs[0].shape[0]
     size = STAGES * LANES
     step = 256
@@ -441,7 +441,7 @@
     return pl.pallas_call(
         basis_kernel,
         grid=(rows // step,),
-        in_specs=[smem_spec()] + [piece] * len(slabs) + [vmem_spec()],
+        in_specs=[smem_spec()] + [piece] * len(slabs) + [vmem_spec(), any_spec()],
         out_specs=[pl.BlockSpec((4 * step, LANES), lambda i: (i, 0)), wide, wide],
         out_shape=[
             jax.ShapeDtypeStruct((4 * rows, LANES), F32),
@@ -449,17 +449,22 @@
             jax.ShapeDtypeStruct((rows, size), BF16),
         ],
         compiler_params=params(),
-        cost_estimate=cost(5),
+        cost_estimate=cost(),
         name="panel_bases",
-    )(flags, *slabs, inverse)
+    )(flags, *slabs, inverse, after)
 
 
 def trailing_kernel(flags_ref, x_ref, qh_ref, ql_ref, inv_ref, h0_ref, h1_ref, *refs):
-    factor_ref, out_ref, x_slabs, w_slabs, out_slabs, x_sems, w_sems, out_sems = refs[-8:]
+    factor_ref, out_ref, q_ref, x_slabs, w_slabs, out_slabs, q_sems, x_sems, w_sems, out_sems = refs[-10:]
     count, rows = x_slabs.shape[0], x_slabs.shape[1]
     halves = x_ref.shape[2]
     first = flags_ref[0] * x_ref.shape[1] // 2
-    fetched = fetch(x_ref, first, x_slabs, x_sems)
+    fetched = [
+        pltpu.make_async_copy(ref, q_ref.at[i], q_sems.at[i]) for i, ref in enumerate((qh_ref, ql_ref))
+    ]
+    for copy in fetched:
+        copy.start()
+    fetched += fetch(x_ref, first, x_slabs, x_sems)
     columns = []
     for i in range(count):
         at = [(2 * i + p) * LANES for p in range(2)]
@@ -478,7 +483,7 @@
     step = rows // chunks
     for chunk in range(chunks):
         here = pl.ds(chunk * step, step)
-        term = dot3((qh_ref[here, :], ql_ref[here, :]), right)
+        term = dot3((q_ref[0, here, :], q_ref[1, here, :]), right)
         for i in range(count):
             out_slabs[i, here, :] = x_slabs[i, here, :] - term[:, i * LANES:(i + 1) * LANES]
             target = out_ref.at[here, first + i // halves, i % halves]
@@ -499,16 +504,18 @@
     extra = len(outs)
     return pl.pallas_call(
         trailing_kernel,
-        in_specs=[smem_spec(), hbm] + [vmem_spec()] * 5 + [hbm] * extra + [any_spec()] * len(after),
+        in_specs=[smem_spec(), hbm] + [any_spec()] * 2 + [vmem_spec()] * 3 + [hbm] * extra + [any_spec()] * len(after),
         out_specs=[hbm, hbm],
         out_shape=[
             jax.ShapeDtypeStruct((size, panels, halves, LANES), F32),
             jax.ShapeDtypeStruct(x.shape, F32),
         ],
         scratch_shapes=[
+            pltpu.VMEM((2, rows, size), BF16),
             pltpu.VMEM((count, rows, LANES), F32),
             pltpu.VMEM((count, size, LANES), F32),
             pltpu.VMEM((count, rows, LANES), F32),
+            pltpu.SemaphoreType.DMA((2,)),
             pltpu.SemaphoreType.DMA((count,)),
             pltpu.SemaphoreType.DMA((count,)),
             pltpu.SemaphoreType.DMA((chunks, count)),
@@ -572,46 +579,43 @@
         other = swap(own, "cols", cols_n, 1)
         gram, give = panel_gram(jnp.stack([side, core]), own, other)
         gram = add(gram, swap(give, "rows", rows_n, 1))
+        order = gram = add(gram, swap(gram, "rows", rows_n, bits[0]))
+        for bit in bits[1:]:
+            gram = add(gram, swap(gram, "rows", rows_n, bit))
 
         flags = jnp.stack([side, core, owner])
         sums, shares = [], []
         for half in range(halves):
-            piece = held(pieces[half], gram)
+            piece = held(pieces[half], order)
             twin = swap(piece, "cols", cols_n, 1)
             share = [slabs[half], other[half], piece, twin]
             give, keep = panel_products(flags, features, *share, gram)
+            if half == 0:
+                gram = join(gram, swap(gram, "rows", rows_n, 1), side)
+            order = give
             shares += share
             steps = sum_steps(keep, swap(give, "rows", rows_n, 1), row, rows_n)
             next(steps)
             sums.append(steps)
-            if half < halves - 1:
-                gram = add(gram, swap(gram, "rows", rows_n, bits[0]), give)
 
         lead, trail = sums
-        last = lead.send(give)
-        last = lead.send(last)
-        for bit in bits[1:]:
-            last = gram = add(gram, swap(gram, "rows", rows_n, bit), last)
-        last = trail.send(last)
-        gram = join(gram, swap(gram, "rows", rows_n, 1), side, last)
-        last = lead.send(gram)
-        arrived = spread(gram, col, cols_n)
-        last = trail.send(last)
-        gram = jnp.where(col < 2, gram, held(arrived, last))
-        state = first_stage(core, gram, swap(gram, "cols", cols_n, 1), last)
-        for k in range(1, STAGES - 1):
-            near = lead.send(state)
-            last = trail.send(near)
-            state = later_stage(k, state, last)
-        for _ in range(2 * len(bits) - 4):
-            near = lead.send(state)
-            last = trail.send(near)
-        inverse = later_stage(STAGES - 1, state, last)
-        far = trail.send(inverse)
+        arrived, last = spread(gram, col, cols_n), give
+        steps = 2 * len(bits) + 1
+        for k in range(steps):
+            last = near = lead.send(last)
+            if k == 0:
+                gram = jnp.where(col < 2, gram, held(arrived, last))
+                last = state = first_stage(core, gram, swap(gram, "cols", cols_n, 1), last)
+            elif k < STAGES:
+                last = state = later_stage(k, state, last)
+            if k == steps - 1:
+                basis, q_high, q_low = panel_bases(flags, shares, state, near)
+                last = q_high
+            last = far = trail.send(last)
 
         mine = [near, far]
         received = [swap(total, "rows", rows_n, 1) for total in mine]
-        basis, q_high, q_low = panel_bases(flags, shares, inverse)
+        inverse = state
         outs = finish(side, features, q_high, q_low, inverse, mine, ())
         factor, trailing = finish(1 - side, features, q_high, q_low, inverse, received, outs)
         basis = basis.reshape(rows, halves, 2, LANES).transpose(0, 2, 1, 3).reshape(rows, 2, width)

time: 145 us -> 137 us (0.945)
  starting transfers between devices: 40.3 us -> 31 us
  Pallas kernels: 50.2 us -> 56.6 us
  waiting for transfers between devices: 49.3 us -> 43.1 us
    ppermute x3, waiting for transfers between devices: 8.35 us -> 0.01 us  [spread(): lax.ppermute(value, 'cols', [(i, i + span) for i in range(min(span, cols...]
    ppermute x20, starting transfers between devices: 27 us -> 22.2 us  [swap(): return lax.ppermute(value, axis, [(i, i ^ bit) for i in range(size)])]
    ppermute x3, starting transfers between devices: 13.3 us -> 8.78 us  [spread(): lax.ppermute(value, 'cols', [(i, i + span) for i in range(min(span, cols...]
    pallas_call x2, Pallas kernels: 9.7 us -> 12.1 us  [finish(): pl.pallas_call(trailing_kernel, in_specs=[smem_spec(), hbm] + [any_spec()...]
    ppermute x20, waiting for transfers between devices: 40.9 us -> 43.1 us  [swap(): return lax.ppermute(value, axis, [(i, i ^ bit) for i in range(size)])]
    pallas_call x4, Pallas kernels: 1.92 us -> 3.56 us  [halve(): pl.pallas_call(halve_kernel, in_specs=[smem_spec()] + [vmem_spec()] * 2 +...]
    unnamed x22 -> x6, local copies, waits for them, and re-layouts: 3.11 us -> 3.67 us
  transfers between devices with their start and end apart: 23 -> 23, of which waited for: 13 -> 13; matrix products, arithmetic and copies ran while one was open for 0% -> 0% of each run, Pallas kernels for 26% -> 35%
where the time goes in v3:
time: 137 us; the launch traced here: 136 us
  Pallas kernels  56.6 us (41%)
  waiting for transfers between devices  43.1 us (31%)
  starting transfers between devices  31 us (23%)
  local copies, waits for them, and re-layouts  3.74 us (3%)
    ppermute x20, waiting for transfers between devices, swap(): return lax.ppermute(value, axis, [(i, i ^ bit) for i in range(size)])  43.1 us
    ppermute x20, starting transfers between devices, swap(): return lax.ppermute(value, axis, [(i, i ^ bit) for i in range(size)])  22.2 us
    pallas_call x4, Pallas kernels, stage_call(): pl.pallas_call(kernel, in_specs=[smem_spec()] * scalars + [vmem_spec()] *...  19.7 us
    pallas_call x2, Pallas kernels, finish(): pl.pallas_call(trailing_kernel, in_specs=[smem_spec(), hbm] + [any_spec()...  12.1 us
    pallas_call x2, Pallas kernels, panel_products(): pl.pallas_call(product_kernel, in_specs=[smem_spec(), pl.BlockSpec(memory...  10.1 us
    ppermute x3, starting transfers between devices, spread(): lax.ppermute(value, 'cols', [(i, i + span) for i in range(min(span, cols...  8.78 us
    pallas_call x1, Pallas kernels, panel_bases(): pl.pallas_call(basis_kernel, grid=(rows // step,), in_specs=[smem_spec()]...  5.46 us
    unnamed x6, local copies, waits for them, and re-layouts  3.67 us
  transfers between devices with their start and end apart: 23, of which 13 were waited for; matrix products, arithmetic and copies ran while one was open for 0% of the time, Pallas kernels for 35%

profile of v3, /device:TPU:0, one launch (start us, length us, event | category | flops | bytes accessed | tf_op | source)
XLA Modules:
  0.0 135.7 jit_solution(6845989279163067280)
XLA Ops:
  0.6 2.5 %own_panel.1 = (f32[1024,128]{1,0:T(8,128)}, f32[1024,128]{1,0:T(8,128)}, f32[2,1024,128]{2,1,0:T(8,128)}) custom-call(f32[1024,4,2,128]{3,2,1,0:T(2,128)} %bitcast.18), custom_call_target="tpu_custom_call" | custom-call | flops 2000000000 | bytes 1 | tf_op jit(solution)/shard_map/own_panel/pallas_call | solution.py:62
  3.7 4.4 %collective-permute-start.1 = (f32[1024,128]{1,0:T(8,128)}, f32[1024,128]{1,0:T(8,128)S(1)}, u32[]{:S(2)}, u32[]{:S(2)}) collective-permute-start(f32[1024,128]{1,0:T(8,128)} %get-tuple-element.27.own_ref.refs_0_), channel_id=1, source_target_pairs={{0,2},{1,3},{4,6},{5,7},{8,10},{9,11},{12,14},{13,15},{16,18},{17,... | collective-permute-start | bytes 1572872 | tf_op jit(solution)/shard_map/ppermute | solution.py:537
  8.2 2.1 %panel_gram.1 = (f32[320,128]{1,0:T(8,128)S(1)}, f32[320,128]{1,0:T(8,128)S(1)}) custom-call(s32[2]{0:T(128)S(1)} %pad_add_fusion.1.flags_ref, f32[2,1024,128]{2,1,0:T(8,128)} %get-tuple-element.28.a_ref, f32[2,1024,128]{2,1,0:T(8,128)S(1)} %collective-permute-done.b_ref), custom_call_target="tpu_custom_call" | custom-call | flops 1000000000 | bytes 1 | tf_op jit(solution)/shard_map/panel_gram/pallas_call | solution.py:184
  12.0 4.8 %collective-permute-done.2.got_ref = f32[320,128]{1,0:T(8,128)S(1)} collective-permute-done((f32[320,128]{1,0:T(8,128)S(1)}, f32[320,128]{1,0:T(8,128)S(1)}, u32[]{:S(2)}, u32[]{:S(2)}) %collective-permute-start.2) | collective-permute-done | bytes 163872 | tf_op jit(solution)/shard_map/ppermute | solution.py:531
  16.8 1.6 %collective-permute-start.3 = (f32[320,128]{1,0:T(8,128)S(1)}, f32[320,128]{1,0:T(8,128)S(1)}, u32[]{:S(2)}, u32[]{:S(2)}) collective-permute-start(f32[320,128]{1,0:T(8,128)S(1)} %add.36.mine_ref), channel_id=1, source_target_pairs={{0,8},{4,12},{8,0},{12,4},{16,24},{20,28},{24,16},{28,20},{1,9},{5... | collective-permute-start | bytes 491528 | tf_op jit(solution)/shard_map/ppermute | solution.py:531
  18.4 3.9 %collective-permute-done.3.got_ref = f32[320,128]{1,0:T(8,128)S(1)} collective-permute-done((f32[320,128]{1,0:T(8,128)S(1)}, f32[320,128]{1,0:T(8,128)S(1)}, u32[]{:S(2)}, u32[]{:S(2)}) %collective-permute-start.3) | collective-permute-done | bytes 163872 | tf_op jit(solution)/shard_map/ppermute | solution.py:531
  22.5 2.6 %collective-permute-start.5 = (f32[1024,128]{1,0:T(8,128)}, f32[1024,128]{1,0:T(8,128)S(1)}, u32[]{:S(2)}, u32[]{:S(2)}) collective-permute-start(f32[1024,128]{1,0:T(8,128)} %get-tuple-element.31.own_ref.refs_4_), channel_id=1, source_target_pairs={{0,2},{1,3},{4,6},{5,7},{8,10},{9,11},{12,14},{13,15},{16,18},{17,... | collective-permute-start | bytes 1572872 | tf_op jit(solution)/shard_map/ppermute | solution.py:537
  25.2 2.6 %collective-permute-start.6 = (f32[320,128]{1,0:T(8,128)S(1)}, f32[320,128]{1,0:T(8,128)S(1)}, u32[]{:S(2)}, u32[]{:S(2)}) collective-permute-start(f32[320,128]{1,0:T(8,128)S(1)} %add.37.refs_0_.mine_ref), channel_id=1, source_target_pairs={{0,16},{4,20},{8,24},{12,28},{16,0},{20,4},{24,8},{28,12},{1,17},{... | collective-permute-start | bytes 491528 | tf_op jit(solution)/shard_map/ppermute | solution.py:531
  27.8 8.1 %collective-permute-done.6.got_ref = f32[320,128]{1,0:T(8,128)S(1)} collective-permute-done((f32[320,128]{1,0:T(8,128)S(1)}, f32[320,128]{1,0:T(8,128)S(1)}, u32[]{:S(2)}, u32[]{:S(2)}) %collective-permute-start.6) | collective-permute-done | bytes 163872 | tf_op jit(solution)/shard_map/ppermute | solution.py:531
  35.9 5.0 %panel_products.2 = (f32[1024,128]{1,0:T(8,128)S(1)}, f32[1024,128]{1,0:T(8,128)S(1)}) custom-call(s32[3]{0:T(128)S(1)} %pad_add_fusion.flags_ref, f32[1024,4,2,128]{3,2,1,0:T(2,128)} %bitcast.19, f32[1024,128]{1,0:T(8,128)} %get-tuple-element.27.own_ref.refs_0_, f32[1024,128]{1,0:T(8,128)S(1)} %get-tuple-element.55.other_ref.refs_1_, ...), custom_call_target="tpu_custom_call" | custom-call | flops 4000000000 | bytes 1 | tf_op jit(solution)/shard_map/panel_products/pallas_call | solution.py:241
  43.2 5.0 %collective-permute-done.8.got_ref = f32[320,128]{1,0:T(8,128)S(1)} collective-permute-done((f32[320,128]{1,0:T(8,128)S(1)}, f32[320,128]{1,0:T(8,128)S(1)}, u32[]{:S(2)}, u32[]{:S(2)}) %collective-permute-start.8) | collective-permute-done | bytes 163872 | tf_op jit(solution)/shard_map/ppermute | solution.py:531
  48.2 1.7 %collective-permute-start.9 = (f32[640,128]{1,0:T(8,128)S(1)}, f32[640,128]{1,0:T(8,128)S(1)}, u32[]{:S(2)}, u32[]{:S(2)}) collective-permute-start(f32[640,128]{1,0:T(8,128)S(1)} %join.5.refs_0_), channel_id=1, source_target_pairs={{0,2},{1,3},{4,6},{5,7},{8,10},{9,11},{12,14},{13,15},{16,18},{17,... | collective-permute-start | bytes 983048 | tf_op jit(solution)/shard_map/ppermute | solution.py:537
  49.9 5.0 %panel_products.3 = (f32[1024,128]{1,0:T(8,128)S(1)}, f32[1024,128]{1,0:T(8,128)S(1)}) custom-call(s32[3]{0:T(128)S(1)} %pad_add_fusion.flags_ref, f32[1024,4,2,128]{3,2,1,0:T(2,128)} %bitcast.20, f32[1024,128]{1,0:T(8,128)} %get-tuple-element.31.own_ref.refs_4_, f32[1024,128]{1,0:T(8,128)S(1)} %get-tuple-element.54.other_ref.refs_5_, ...), custom_call_target="tpu_custom_call" | custom-call | flops 4000000000 | bytes 1 | tf_op jit(solution)/shard_map/panel_products/pallas_call | solution.py:241
  55.0 1.6 %collective-permute-start.13 = (f32[1024,128]{1,0:T(8,128)S(1)}, f32[1024,128]{1,0:T(8,128)S(1)}, u32[]{:S(2)}, u32[]{:S(2)}) collective-permute-start(f32[1024,128]{1,0:T(8,128)S(1)} %get-tuple-element.34.refs_0_), channel_id=1, source_target_pairs={{0,4},{4,0},{8,12},{12,8},{16,20},{20,16},{24,28},{28,24},{1,5},{5... | collective-permute-start | bytes 1572872 | tf_op jit(solution)/shard_map/ppermute | solution.py:531
  56.6 2.9 %collective-permute-done.10.got_ref = f32[1024,128]{1,0:T(8,128)} collective-permute-done((f32[1024,128]{1,0:T(8,128)S(1)}, f32[1024,128]{1,0:T(8,128)}, u32[]{:S(2)}, u32[]{:S(2)}) %collective-permute-start.10) | collective-permute-done | bytes 524320 | tf_op jit(solution)/shard_map/ppermute | solution.py:531
  59.5 1.8 %halve.4 = (f32[512,128]{1,0:T(8,128)S(1)}, f32[512,128]{1,0:T(8,128)}) custom-call(s32[1]{0:T(128)} %bitcast.7.flag_ref, f32[1024,128]{1,0:T(8,128)S(1)} %get-tuple-element.33.mine_ref, f32[1024,128]{1,0:T(8,128)} %collective-permute-done.10.got_ref, f32[1024,128]{1,0:T(8,128)S(1)} %get-tuple-element.34.refs_0_), custom_call_target="tpu_custom_call" | custom-call | flops 1 | bytes 1 | tf_op jit(solution)/shard_map/halve/pallas_call | solution.py:112
  63.0 5.4 %factor_0.1.refs_0_.in_ref = f32[10,128,128]{2,1,0:T(8,128)S(1)} custom-call(s32[1]{0:T(128)} %bitcast.3.core_ref, f32[640,128]{1,0:T(8,128)S(1)} %broadcast_select_fusion.mine_ref, f32[640,128]{1,0:T(8,128)S(1)} %collective-permute-done.11.twin_ref, f32[512,128]{1,0:T(8,128)S(1)} %get-tuple-element.35.refs_0_.mine_ref), custom_call_target="tpu_custom_call" | custom-call | flops 1 | bytes 1 | tf_op jit(solution)/shard_map/factor_0/pallas_call | solution.py:386
  68.5 1.7 %collective-permute-done.13.got_ref = f32[1024,128]{1,0:T(8,128)S(1)} collective-permute-done((f32[1024,128]{1,0:T(8,128)S(1)}, f32[1024,128]{1,0:T(8,128)S(1)}, u32[]{:S(2)}, u32[]{:S(2)}) %collective-permute-start.13) | collective-permute-done | bytes 524320 | tf_op jit(solution)/shard_map/ppermute | solution.py:531
  71.6 3.4 %collective-permute-start.14 = (f32[256,128]{1,0:T(8,128)S(1)}, f32[256,128]{1,0:T(8,128)S(1)}, u32[]{:S(2)}, u32[]{:S(2)}) collective-permute-start(f32[256,128]{1,0:T(8,128)S(1)} %get-tuple-element.40), channel_id=1, source_target_pairs={{0,16},{4,20},{8,24},{12,28},{16,0},{20,4},{24,8},{28,12},{1,17},{... | collective-permute-start | bytes 393224 | tf_op jit(solution)/shard_map/ppermute | solution.py:531
  75.1 4.9 %factor_1.1.refs_0_.in_ref = f32[10,128,128]{2,1,0:T(8,128)S(1)} custom-call(f32[10,128,128]{2,1,0:T(8,128)S(1)} %factor_0.1.refs_0_.in_ref, f32[256,128]{1,0:T(8,128)S(1)} %get-tuple-element.39.refs_0_.mine_ref), custom_call_target="tpu_custom_call" | custom-call | flops 1 | bytes 1 | tf_op jit(solution)/shard_map/factor_1/pallas_call | solution.py:386
  79.9 2.0 %collective-permute-done.15.got_ref = f32[512,128]{1,0:T(8,128)} collective-permute-done((f32[512,128]{1,0:T(8,128)}, f32[512,128]{1,0:T(8,128)}, u32[]{:S(2)}, u32[]{:S(2)}) %collective-permute-start.15) | collective-permute-done | bytes 262176 | tf_op jit(solution)/shard_map/ppermute | solution.py:531
  82.9 1.6 %collective-permute-start.17 = (f32[256,128]{1,0:T(8,128)S(1)}, f32[256,128]{1,0:T(8,128)S(1)}, u32[]{:S(2)}, u32[]{:S(2)}) collective-permute-start(f32[256,128]{1,0:T(8,128)S(1)} %get-tuple-element.43), channel_id=1, source_target_pairs={{0,16},{4,20},{8,24},{12,28},{16,0},{20,4},{24,8},{28,12},{1,17},{... | collective-permute-start | bytes 393224 | tf_op jit(solution)/shard_map/ppermute | solution.py:531
  86.0 5.3 %factor_2.1.refs_0_.in_ref = f32[10,128,128]{2,1,0:T(8,128)S(1)} custom-call(f32[10,128,128]{2,1,0:T(8,128)S(1)} %factor_1.1.refs_0_.in_ref, f32[256,128]{1,0:T(8,128)S(1)} %add.39.refs_0_.mine_ref), custom_call_target="tpu_custom_call" | custom-call | flops 1 | bytes 1 | tf_op jit(solution)/shard_map/factor_2/pallas_call | solution.py:386
  91.3 3.8 %collective-permute-done.17.got_ref = f32[256,128]{1,0:T(8,128)S(1)} collective-permute-done((f32[256,128]{1,0:T(8,128)S(1)}, f32[256,128]{1,0:T(8,128)S(1)}, u32[]{:S(2)}, u32[]{:S(2)}) %collective-permute-start.17) | collective-permute-done | bytes 131104 | tf_op jit(solution)/shard_map/ppermute | solution.py:531
  95.2 2.7 %collective-permute-done.16.got_ref = f32[256,128]{1,0:T(8,128)S(1)} collective-permute-done((f32[256,128]{1,0:T(8,128)S(1)}, f32[256,128]{1,0:T(8,128)S(1)}, u32[]{:S(2)}, u32[]{:S(2)}) %collective-permute-start.16) | collective-permute-done | bytes 131104 | tf_op jit(solution)/shard_map/ppermute | solution.py:531
  98.8 4.2 %factor_3.1.refs_0_.refs_8_.inv_ref = f32[10,128,128]{2,1,0:T(8,128)S(1)} custom-call(f32[10,128,128]{2,1,0:T(8,128)S(1)} %factor_2.1.refs_0_.in_ref, f32[512,128]{1,0:T(8,128)S(1)} %join.6.refs_0_.mine_ref), custom_call_target="tpu_custom_call" | custom-call | flops 1 | bytes 1 | tf_op jit(solution)/shard_map/factor_3/pallas_call | solution.py:386
  104.2 3.3 %collective-permute-done.18.got_ref = f32[512,128]{1,0:T(8,128)S(1)} collective-permute-done((f32[512,128]{1,0:T(8,128)S(1)}, f32[512,128]{1,0:T(8,128)S(1)}, u32[]{:S(2)}, u32[]{:S(2)}) %collective-permute-start.18) | collective-permute-done | bytes 262176 | tf_op jit(solution)/shard_map/ppermute | solution.py:531
  107.6 1.6 %collective-permute-start.20 = (f32[1024,128]{1,0:T(8,128)S(1)}, f32[1024,128]{1,0:T(8,128)}, u32[]{:S(2)}, u32[]{:S(2)}) collective-permute-start(f32[1024,128]{1,0:T(8,128)S(1)} %join.8.refs_9_.h0_ref), channel_id=1, source_target_pairs={{0,4},{4,0},{8,12},{12,8},{16,20},{20,16},{24,28},{28,24},{1,5},{5... | collective-permute-start | bytes 1572872 | tf_op jit(solution)/shard_map/ppermute | solution.py:531
  109.1 5.5 %panel_bases.1 = (f32[4096,128]{1,0:T(8,128)}, bf16[1024,512]{1,0:T(8,128)(2,1)}, bf16[1024,512]{1,0:T(8,128)(2,1)}) custom-call(s32[3]{0:T(128)S(1)} %pad_add_fusion.flags_ref, f32[1024,128]{1,0:T(8,128)} %get-tuple-element.27.own_ref.refs_0_, f32[1024,128]{1,0:T(8,128)S(1)} %get-tuple-element.55.other_ref.refs_1_, f32[1024,128]{1,0:T(8,128)S(1)} %held.3.got_ref.refs_2_, ...), custom_call_target="tpu_custom_call" | custom-call | flops 1 | bytes 1 | tf_op jit(solution)/shard_map/panel_bases/pallas_call | solution.py:441
  119.6 6.0 %finish.2 = (f32[512,4,2,128]{3,2,1,0:T(2,128)}, f32[1024,4,2,128]{3,2,1,0:T(2,128)}) custom-call(s32[1]{0:T(128)} %bitcast.2.flag_ref.flags_ref, f32[1024,4,2,128]{3,2,1,0:T(2,128)} %bitcast.21, bf16[1024,512]{1,0:T(8,128)(2,1)S(1)} %copy-done.1, bf16[1024,512]{1,0:T(8,128)(2,1)S(1)} %copy-done.2, f32[10,128,128]{2,1,0:T(8,128)S(1)} %factor_3.1.refs_0_.refs_8_.inv_ref, ...), custom_call_target="tpu_custom_call" | custom-call | flops 5000000000 | bytes 1 | tf_op jit(solution)/shard_map/finish/pallas_call | solution.py:505
  125.6 3.9 %collective-permute-done.22.h1_ref = f32[1024,128]{1,0:T(8,128)} collective-permute-done((f32[1024,128]{1,0:T(8,128)}, f32[1024,128]{1,0:T(8,128)}, u32[]{:S(2)}, u32[]{:S(2)}) %collective-permute-start.22) | collective-permute-done | bytes 524320 | tf_op jit(solution)/shard_map/ppermute | solution.py:531
  129.5 6.1 %finish.3 = (f32[512,4,2,128]{3,2,1,0:T(2,128)}, f32[1024,4,2,128]{3,2,1,0:T(2,128)}) custom-call(s32[1]{0:T(128)} %bitcast.flags_ref, f32[1024,4,2,128]{3,2,1,0:T(2,128)} %bitcast.22, bf16[1024,512]{1,0:T(8,128)(2,1)S(1)} %copy-done.1, bf16[1024,512]{1,0:T(8,128)(2,1)S(1)} %copy-done.2, ...), custom_call_target="tpu_custom_call", output_to_operand_aliasing={{0}: (7, {}), {1}: (8, {})} | custom-call | flops 5000000000 | bytes 1 | tf_op jit(solution)/shard_map/finish/pallas_call | solution.py:505
  (52 shorter events, 17.6 us)
Async XLA Ops:
  3.2 5.1 %collective-permute-start = (f32[2,1024,128]{2,1,0:T(8,128)}, f32[2,1024,128]{2,1,0:T(8,128)S(1)}, u32[]{:S(2)}, u32[]{:S(2)}) collective-permute-start(f32[2,1024,128]{2,1,0:T(8,128)} %get-tuple-element.28.a_ref), channel_id=1, source_target_pairs={{0,1},{1,0},{2,3},{3,2},{4,5},{5,4},{6,7},{7,6},{8,9},{9,8},{10,11... | collective-permute-start | bytes 3145736 | tf_op jit(solution)/shard_map/ppermute | solution.py:531
  3.7 18.7 %collective-permute-start.1 = (f32[1024,128]{1,0:T(8,128)}, f32[1024,128]{1,0:T(8,128)S(1)}, u32[]{:S(2)}, u32[]{:S(2)}) collective-permute-start(f32[1024,128]{1,0:T(8,128)} %get-tuple-element.27.own_ref.refs_0_), channel_id=1, source_target_pairs={{0,2},{1,3},{4,6},{5,7},{8,10},{9,11},{12,14},{13,15},{16,18},{17,... | collective-permute-start | bytes 1572872 | tf_op jit(solution)/shard_map/ppermute | solution.py:537
  10.4 6.4 %collective-permute-start.2 = (f32[320,128]{1,0:T(8,128)S(1)}, f32[320,128]{1,0:T(8,128)S(1)}, u32[]{:S(2)}, u32[]{:S(2)}) collective-permute-start(f32[320,128]{1,0:T(8,128)S(1)} %get-tuple-element.30), channel_id=1, source_target_pairs={{0,4},{4,0},{8,12},{12,8},{16,20},{20,16},{24,28},{28,24},{1,5},{5... | collective-permute-start | bytes 491528 | tf_op jit(solution)/shard_map/ppermute | solution.py:531
  16.8 5.5 %collective-permute-start.3 = (f32[320,128]{1,0:T(8,128)S(1)}, f32[320,128]{1,0:T(8,128)S(1)}, u32[]{:S(2)}, u32[]{:S(2)}) collective-permute-start(f32[320,128]{1,0:T(8,128)S(1)} %add.36.mine_ref), channel_id=1, source_target_pairs={{0,8},{4,12},{8,0},{12,4},{16,24},{20,28},{24,16},{28,20},{1,9},{5... | collective-permute-start | bytes 491528 | tf_op jit(solution)/shard_map/ppermute | solution.py:531
  22.4 13.5 %collective-permute-start.4 = (f32[1024,128]{1,0:T(8,128)S(1)}, f32[1024,128]{1,0:T(8,128)}, u32[]{:S(2)}, u32[]{:S(2)}) collective-permute-start(f32[1024,128]{1,0:T(8,128)S(1)} %held.3.got_ref.refs_2_), channel_id=1, source_target_pairs={{0,1},{1,0},{2,3},{3,2},{4,5},{5,4},{6,7},{7,6},{8,9},{9,8},{10,11... | collective-permute-start | bytes 1572872 | tf_op jit(solution)/shard_map/ppermute | solution.py:531
  22.5 18.5 %collective-permute-start.5 = (f32[1024,128]{1,0:T(8,128)}, f32[1024,128]{1,0:T(8,128)S(1)}, u32[]{:S(2)}, u32[]{:S(2)}) collective-permute-start(f32[1024,128]{1,0:T(8,128)} %get-tuple-element.31.own_ref.refs_4_), channel_id=1, source_target_pairs={{0,2},{1,3},{4,6},{5,7},{8,10},{9,11},{12,14},{13,15},{16,18},{17,... | collective-permute-start | bytes 1572872 | tf_op jit(solution)/shard_map/ppermute | solution.py:537
  25.2 10.7 %collective-permute-start.6 = (f32[320,128]{1,0:T(8,128)S(1)}, f32[320,128]{1,0:T(8,128)S(1)}, u32[]{:S(2)}, u32[]{:S(2)}) collective-permute-start(f32[320,128]{1,0:T(8,128)S(1)} %add.37.refs_0_.mine_ref), channel_id=1, source_target_pairs={{0,16},{4,20},{8,24},{12,28},{16,0},{20,4},{24,8},{28,12},{1,17},{... | collective-permute-start | bytes 491528 | tf_op jit(solution)/shard_map/ppermute | solution.py:531
  41.0 8.9 %collective-permute-start.7 = (f32[1024,128]{1,0:T(8,128)S(1)}, f32[1024,128]{1,0:T(8,128)}, u32[]{:S(2)}, u32[]{:S(2)}) collective-permute-start(f32[1024,128]{1,0:T(8,128)S(1)} %held.4.got_ref.refs_6_), channel_id=1, source_target_pairs={{0,1},{1,0},{2,3},{3,2},{4,5},{5,4},{6,7},{7,6},{8,9},{9,8},{10,11... | collective-permute-start | bytes 1572872 | tf_op jit(solution)/shard_map/ppermute | solution.py:531
  41.1 7.1 %collective-permute-start.8 = (f32[320,128]{1,0:T(8,128)S(1)}, f32[320,128]{1,0:T(8,128)S(1)}, u32[]{:S(2)}, u32[]{:S(2)}) collective-permute-start(f32[320,128]{1,0:T(8,128)S(1)} %add.38.refs_0_.mine_ref), channel_id=1, source_target_pairs={{0,4},{4,0},{8,12},{12,8},{16,20},{20,16},{24,28},{28,24},{1,5},{5... | collective-permute-start | bytes 491528 | tf_op jit(solution)/shard_map/ppermute | solution.py:531
  42.7 16.8 %collective-permute-start.10 = (f32[1024,128]{1,0:T(8,128)S(1)}, f32[1024,128]{1,0:T(8,128)}, u32[]{:S(2)}, u32[]{:S(2)}) collective-permute-start(f32[1024,128]{1,0:T(8,128)S(1)} %get-tuple-element.32.refs_0_), channel_id=1, source_target_pairs={{0,4},{4,0},{8,12},{12,8},{16,20},{20,16},{24,28},{28,24},{1,5},{5... | collective-permute-start | bytes 1572872 | tf_op jit(solution)/shard_map/ppermute | solution.py:531
  48.2 13.1 %collective-permute-start.9 = (f32[640,128]{1,0:T(8,128)S(1)}, f32[640,128]{1,0:T(8,128)S(1)}, u32[]{:S(2)}, u32[]{:S(2)}) collective-permute-start(f32[640,128]{1,0:T(8,128)S(1)} %join.5.refs_0_), channel_id=1, source_target_pairs={{0,2},{1,3},{4,6},{5,7},{8,10},{9,11},{12,14},{13,15},{16,18},{17,... | collective-permute-start | bytes 983048 | tf_op jit(solution)/shard_map/ppermute | solution.py:537
  55.0 15.2 %collective-permute-start.13 = (f32[1024,128]{1,0:T(8,128)S(1)}, f32[1024,128]{1,0:T(8,128)S(1)}, u32[]{:S(2)}, u32[]{:S(2)}) collective-permute-start(f32[1024,128]{1,0:T(8,128)S(1)} %get-tuple-element.34.refs_0_), channel_id=1, source_target_pairs={{0,4},{4,0},{8,12},{12,8},{16,20},{20,16},{24,28},{28,24},{1,5},{5... | collective-permute-start | bytes 1572872 | tf_op jit(solution)/shard_map/ppermute | solution.py:531
  61.3 1.7 %collective-permute-start.11 = (f32[640,128]{1,0:T(8,128)S(1)}, f32[640,128]{1,0:T(8,128)S(1)}, u32[]{:S(2)}, u32[]{:S(2)}) collective-permute-start(f32[640,128]{1,0:T(8,128)S(1)} %broadcast_select_fusion.mine_ref), channel_id=1, source_target_pairs={{0,1},{1,0},{2,3},{3,2},{4,5},{5,4},{6,7},{7,6},{8,9},{9,8},{10,11... | collective-permute-start | bytes 983048 | tf_op jit(solution)/shard_map/ppermute | solution.py:531
  61.4 10.2 %collective-permute-start.12 = (f32[512,128]{1,0:T(8,128)}, f32[512,128]{1,0:T(8,128)S(1)}, u32[]{:S(2)}, u32[]{:S(2)}) collective-permute-start(f32[512,128]{1,0:T(8,128)} %get-tuple-element.36), channel_id=1, source_target_pairs={{0,8},{4,12},{8,0},{12,4},{16,24},{20,28},{24,16},{28,20},{1,9},{5... | collective-permute-start | bytes 786440 | tf_op jit(solution)/shard_map/ppermute | solution.py:531
  70.9 11.0 %collective-permute-start.15 = (f32[512,128]{1,0:T(8,128)}, f32[512,128]{1,0:T(8,128)}, u32[]{:S(2)}, u32[]{:S(2)}) collective-permute-start(f32[512,128]{1,0:T(8,128)} %get-tuple-element.41), channel_id=1, source_target_pairs={{0,8},{4,12},{8,0},{12,4},{16,24},{20,28},{24,16},{28,20},{1,9},{5... | collective-permute-start | bytes 786440 | tf_op jit(solution)/shard_map/ppermute | solution.py:531
  71.6 12.9 %collective-permute-start.14 = (f32[256,128]{1,0:T(8,128)S(1)}, f32[256,128]{1,0:T(8,128)S(1)}, u32[]{:S(2)}, u32[]{:S(2)}) collective-permute-start(f32[256,128]{1,0:T(8,128)S(1)} %get-tuple-element.40), channel_id=1, source_target_pairs={{0,16},{4,20},{8,24},{12,28},{16,0},{20,4},{24,8},{28,12},{1,17},{... | collective-permute-start | bytes 393224 | tf_op jit(solution)/shard_map/ppermute | solution.py:531
  82.9 12.2 %collective-permute-start.17 = (f32[256,128]{1,0:T(8,128)S(1)}, f32[256,128]{1,0:T(8,128)S(1)}, u32[]{:S(2)}, u32[]{:S(2)}) collective-permute-start(f32[256,128]{1,0:T(8,128)S(1)} %get-tuple-element.43), channel_id=1, source_target_pairs={{0,16},{4,20},{8,24},{12,28},{16,0},{20,4},{24,8},{28,12},{1,17},{... | collective-permute-start | bytes 393224 | tf_op jit(solution)/shard_map/ppermute | solution.py:531
  84.5 13.3 %collective-permute-start.16 = (f32[256,128]{1,0:T(8,128)S(1)}, f32[256,128]{1,0:T(8,128)S(1)}, u32[]{:S(2)}, u32[]{:S(2)}) collective-permute-start(f32[256,128]{1,0:T(8,128)S(1)} %add.39.refs_0_.mine_ref), channel_id=1, source_target_pairs={{0,16},{4,20},{8,24},{12,28},{16,0},{20,4},{24,8},{28,12},{1,17},{... | collective-permute-start | bytes 393224 | tf_op jit(solution)/shard_map/ppermute | solution.py:531
  95.1 8.1 %collective-permute-start.19 = (f32[256,128]{1,0:T(8,128)S(1)}, f32[256,128]{1,0:T(8,128)S(1)}, u32[]{:S(2)}, u32[]{:S(2)}) collective-permute-start(f32[256,128]{1,0:T(8,128)S(1)} %add.40.refs_0_.mine_ref), channel_id=1, source_target_pairs={{0,16},{4,20},{8,24},{12,28},{16,0},{20,4},{24,8},{28,12},{1,17},{... | collective-permute-start | bytes 393224 | tf_op jit(solution)/shard_map/ppermute | solution.py:531
  97.9 9.6 %collective-permute-start.18 = (f32[512,128]{1,0:T(8,128)S(1)}, f32[512,128]{1,0:T(8,128)S(1)}, u32[]{:S(2)}, u32[]{:S(2)}) collective-permute-start(f32[512,128]{1,0:T(8,128)S(1)} %join.6.refs_0_.mine_ref), channel_id=1, source_target_pairs={{0,8},{4,12},{8,0},{12,4},{16,24},{20,28},{24,16},{28,20},{1,9},{5... | collective-permute-start | bytes 786440 | tf_op jit(solution)/shard_map/ppermute | solution.py:531
  103.2 11.4 %collective-permute-start.21 = (f32[512,128]{1,0:T(8,128)S(1)}, f32[512,128]{1,0:T(8,128)S(1)}, u32[]{:S(2)}, u32[]{:S(2)}) collective-permute-start(f32[512,128]{1,0:T(8,128)S(1)} %join.7.refs_0_.mine_ref), channel_id=1, source_target_pairs={{0,8},{4,12},{8,0},{12,4},{16,24},{20,28},{24,16},{28,20},{1,9},{5... | collective-permute-start | bytes 786440 | tf_op jit(solution)/shard_map/ppermute | solution.py:531
  107.6 18.0 %collective-permute-start.20 = (f32[1024,128]{1,0:T(8,128)S(1)}, f32[1024,128]{1,0:T(8,128)}, u32[]{:S(2)}, u32[]{:S(2)}) collective-permute-start(f32[1024,128]{1,0:T(8,128)S(1)} %join.8.refs_9_.h0_ref), channel_id=1, source_target_pairs={{0,4},{4,0},{8,12},{12,8},{16,20},{20,16},{24,28},{28,24},{1,5},{5... | collective-permute-start | bytes 1572872 | tf_op jit(solution)/shard_map/ppermute | solution.py:531
  114.6 1.2 copy-start
  116.7 12.8 %collective-permute-start.22 = (f32[1024,128]{1,0:T(8,128)}, f32[1024,128]{1,0:T(8,128)}, u32[]{:S(2)}, u32[]{:S(2)}) collective-permute-start(f32[1024,128]{1,0:T(8,128)} %join.9.h1_ref), channel_id=1, source_target_pairs={{0,4},{4,0},{8,12},{12,8},{16,20},{20,16},{24,28},{28,24},{1,5},{5... | collective-permute-start | bytes 1572872 | tf_op jit(solution)/shard_map/ppermute | solution.py:531
  117.2 1.2 copy-start.1
  118.4 1.2 copy-start.2

commit v4 on v3

--- a/solution.py
+++ b/solution.py
@@ -222,30 +222,46 @@
     return zero, one
 
 
-def product_kernel(flags_ref, x_ref, own_ref, other_ref, got_ref, twin_ref, *refs):
-    give_ref, keep_ref, far_ref, near_ref, sems = refs[-5:]
+def product_kernel(half, flags_ref, x_ref, own_ref, other_ref, got_ref, twin_ref, *refs):
+    give_ref, keep_ref, pair_ref, far_ref, near_ref, pair_sems, sems = refs[-7:]
+
+    def load(*sources):
+        for i, source in enumerate(sources):
+            pltpu.make_async_copy(source, pair_ref.at[i], pair_sems.at[i]).start()
+
+    @pl.when(flags_ref[2] == 1)
+    def _():
+        load(own_ref, other_ref.at[half])
+
+    @pl.when(flags_ref[2] != 1)
+    def _():
+        load(got_ref, twin_ref)
+
     panels = x_ref.shape[1] // 2
     far = fetch(x_ref, (1 - flags_ref[0]) * panels, far_ref, sems.at[0])
     near = fetch(x_ref, flags_ref[0] * panels, near_ref, sems.at[1])
-    zero, one = choose(flags_ref, own_ref[...], other_ref[...], got_ref[...], twin_ref[...])
+    for i in range(2):
+        pltpu.make_async_copy(own_ref, pair_ref.at[i], pair_sems.at[i]).wait()
+    zero, one = pair_ref[flags_ref[1]], pair_ref[1 - flags_ref[1]]
     left = split(jnp.concatenate([zero, one], axis=1).T)
     times_columns(left, far, far_ref, give_ref)
     times_columns(left, near, near_ref, keep_ref)
 
 
-def panel_products(flags, features, own, other, got, twin, *after):
+def panel_products(half, flags, features, own, other, got, twin, *after):
     rows, panels, _, width = features.shape
     count = panels * width // LANES // 2
     x = features.reshape(rows, panels, width // LANES, LANES)
     out = jax.ShapeDtypeStruct((count * 2 * LANES, LANES), F32)
     return pl.pallas_call(
-        product_kernel,
+        functools.partial(product_kernel, half),
         in_specs=[smem_spec(), pl.BlockSpec(memory_space=pltpu.HBM)]
-        + [vmem_spec()] * 4 + [any_spec()] * len(after),
+        + [any_spec()] * (4 + len(after)),
         out_specs=[vmem_spec()] * 2,
         out_shape=[out, out],
-        scratch_shapes=[pltpu.VMEM((count, rows, LANES), F32)] * 2
-        + [pltpu.SemaphoreType.DMA((2, count))],
+        scratch_shapes=[pltpu.VMEM((2, rows, LANES), F32)]
+        + [pltpu.VMEM((count, rows, LANES), F32)] * 2
+        + [pltpu.SemaphoreType.DMA((2,)), pltpu.SemaphoreType.DMA((2, count))],
         compiler_params=params(),
         cost_estimate=cost(4),
         name="panel_products",
@@ -579,20 +595,20 @@
         other = swap(own, "cols", cols_n, 1)
         gram, give = panel_gram(jnp.stack([side, core]), own, other)
         gram = add(gram, swap(give, "rows", rows_n, 1))
-        order = gram = add(gram, swap(gram, "rows", rows_n, bits[0]))
-        for bit in bits[1:]:
+        order = (gram,)
+        for bit in bits:
             gram = add(gram, swap(gram, "rows", rows_n, bit))
+        gram = join(gram, swap(gram, "rows", rows_n, 1), side)
 
         flags = jnp.stack([side, core, owner])
         sums, shares = [], []
         for half in range(halves):
-            piece = held(pieces[half], order)
+            piece = held(pieces[half], *order)
             twin = swap(piece, "cols", cols_n, 1)
             share = [slabs[half], other[half], piece, twin]
-            give, keep = panel_products(flags, features, *share, gram)
-            if half == 0:
-                gram = join(gram, swap(gram, "rows", rows_n, 1), side)
-            order = give
+            give, keep = panel_products(
+                half, flags, features, slabs[half], other, piece, twin, gram)
+            order = (give,)
             shares += share
             steps = sum_steps(keep, swap(give, "rows", rows_n, 1), row, rows_n)
             next(steps)

time: 137 us -> 151 us (1.10)
  waiting for transfers between devices: 43.1 us -> 50.9 us
  starting transfers between devices: 31 us -> 37.8 us
  Pallas kernels: 56.6 us -> 51 us
  local copies, waits for them, and re-layouts: 3.74 us -> 8.83 us
    ppermute x3, waiting for transfers between devices: 0.01 us -> 5.66 us  [spread(): lax.ppermute(value, 'cols', [(i, i + span) for i in range(min(span, cols...]
    unnamed x6 -> x26, local copies, waits for them, and re-layouts: 3.67 us -> 8.76 us
    ppermute x3, starting transfers between devices: 8.78 us -> 13.3 us  [spread(): lax.ppermute(value, 'cols', [(i, i + span) for i in range(min(span, cols...]
    ppermute x20, starting transfers between devices: 22.2 us -> 24.5 us  [swap(): return lax.ppermute(value, axis, [(i, i ^ bit) for i in range(size)])]
    ppermute x20, waiting for transfers between devices: 43.1 us -> 45.2 us  [swap(): return lax.ppermute(value, axis, [(i, i ^ bit) for i in range(size)])]
    pallas_call x2, Pallas kernels: 12.1 us -> 10 us  [finish(): pl.pallas_call(trailing_kernel, in_specs=[smem_spec(), hbm] + [any_spec()...]
  transfers between devices with their start and end apart: 23 -> 23, of which waited for: 13 -> 12; matrix products, arithmetic and copies ran while one was open for 0% -> 0% of each run, Pallas kernels for 35% -> 29%
where the time goes in v4:
time: 151 us; the launch traced here: 150 us
  Pallas kernels  51 us (34%)
  waiting for transfers between devices  50.9 us (34%)
  starting transfers between devices  37.8 us (25%)
  local copies, waits for them, and re-layouts  8.83 us (6%)
    ppermute x20, waiting for transfers between devices, swap(): return lax.ppermute(value, axis, [(i, i ^ bit) for i in range(size)])  45.2 us
    ppermute x20, starting transfers between devices, swap(): return lax.ppermute(value, axis, [(i, i ^ bit) for i in range(size)])  24.5 us
    pallas_call x4, Pallas kernels, stage_call(): pl.pallas_call(kernel, in_specs=[smem_spec()] * scalars + [vmem_spec()] *...  19.8 us
    ppermute x3, starting transfers between devices, spread(): lax.ppermute(value, 'cols', [(i, i + span) for i in range(min(span, cols...  13.3 us
    pallas_call x2, Pallas kernels, finish(): pl.pallas_call(trailing_kernel, in_specs=[smem_spec(), hbm] + [any_spec()...  10 us
    unnamed x26, local copies, waits for them, and re-layouts  8.76 us
    pallas_call x2, Pallas kernels, panel_products(): pl.pallas_call(functools.partial(product_kernel, half), in_specs=[smem_sp...  8.62 us
    ppermute x3, waiting for transfers between devices, spread(): lax.ppermute(value, 'cols', [(i, i + span) for i in range(min(span, cols...  5.66 us
  transfers between devices with their start and end apart: 23, of which 12 were waited for; matrix products, arithmetic and copies ran while one was open for 0% of the time, Pallas kernels for 29%

profile of v4, /device:TPU:0, one launch (start us, length us, event | category | flops | bytes accessed | tf_op | source)
XLA Modules:
  0.0 149.8 jit_solution(17479782165942292994)
XLA Ops:
  0.6 2.1 %own_panel.1 = (f32[1024,128]{1,0:T(8,128)S(1)}, f32[1024,128]{1,0:T(8,128)}, f32[2,1024,128]{2,1,0:T(8,128)S(1)}) custom-call(f32[1024,4,2,128]{3,2,1,0:T(2,128)} %bitcast.18), custom_call_target="tpu_custom_call" | custom-call | flops 2000000000 | bytes 1 | tf_op jit(solution)/shard_map/own_panel/pallas_call | solution.py:62
  4.2 4.5 %collective-permute-start.1 = (f32[1024,128]{1,0:T(8,128)S(1)}, f32[1024,128]{1,0:T(8,128)S(1)}, u32[]{:S(2)}, u32[]{:S(2)}) collective-permute-start(f32[1024,128]{1,0:T(8,128)S(1)} %get-tuple-element.27.own_ref.refs_0_), channel_id=1, source_target_pairs={{0,2},{1,3},{4,6},{5,7},{8,10},{9,11},{12,14},{13,15},{16,18},{17,... | collective-permute-start | bytes 1572872 | tf_op jit(solution)/shard_map/ppermute | solution.py:553
  13.1 4.7 %collective-permute-done.2.got_ref = f32[320,128]{1,0:T(8,128)S(1)} collective-permute-done((f32[320,128]{1,0:T(8,128)S(1)}, f32[320,128]{1,0:T(8,128)S(1)}, u32[]{:S(2)}, u32[]{:S(2)}) %collective-permute-start.2) | collective-permute-done | bytes 163872 | tf_op jit(solution)/shard_map/ppermute | solution.py:547
  17.8 2.6 %collective-permute-done.1.value_ref = f32[1024,128]{1,0:T(8,128)S(1)} collective-permute-done((f32[1024,128]{1,0:T(8,128)S(1)}, f32[1024,128]{1,0:T(8,128)S(1)}, u32[]{:S(2)}, u32[]{:S(2)}) %collective-permute-start.1) | collective-permute-done | bytes 524320 | tf_op jit(solution)/shard_map/ppermute | solution.py:553
  22.0 5.0 %collective-permute-done.5.got_ref = f32[320,128]{1,0:T(8,128)S(1)} collective-permute-done((f32[320,128]{1,0:T(8,128)S(1)}, f32[320,128]{1,0:T(8,128)S(1)}, u32[]{:S(2)}, u32[]{:S(2)}) %collective-permute-start.5) | collective-permute-done | bytes 163872 | tf_op jit(solution)/shard_map/ppermute | solution.py:547
  27.1 2.7 %collective-permute-start.6 = (f32[320,128]{1,0:T(8,128)S(1)}, f32[320,128]{1,0:T(8,128)S(1)}, u32[]{:S(2)}, u32[]{:S(2)}) collective-permute-start(f32[320,128]{1,0:T(8,128)S(1)} %add.37.mine_ref), channel_id=1, source_target_pairs={{0,16},{4,20},{8,24},{12,28},{16,0},{20,4},{24,8},{28,12},{1,17},{... | collective-permute-start | bytes 491528 | tf_op jit(solution)/shard_map/ppermute | solution.py:547
  29.7 7.6 %collective-permute-done.6.got_ref = f32[320,128]{1,0:T(8,128)S(1)} collective-permute-done((f32[320,128]{1,0:T(8,128)S(1)}, f32[320,128]{1,0:T(8,128)S(1)}, u32[]{:S(2)}, u32[]{:S(2)}) %collective-permute-start.6) | collective-permute-done | bytes 163872 | tf_op jit(solution)/shard_map/ppermute | solution.py:547
  37.4 1.6 %collective-permute-start.7 = (f32[320,128]{1,0:T(8,128)S(1)}, f32[320,128]{1,0:T(8,128)S(1)}, u32[]{:S(2)}, u32[]{:S(2)}) collective-permute-start(f32[320,128]{1,0:T(8,128)S(1)} %add.38.mine_ref), channel_id=1, source_target_pairs={{0,4},{4,0},{8,12},{12,8},{16,20},{20,16},{24,28},{28,24},{1,5},{5... | collective-permute-start | bytes 491528 | tf_op jit(solution)/shard_map/ppermute | solution.py:547
  39.0 4.4 %collective-permute-start.4 = (f32[1024,128]{1,0:T(8,128)}, f32[1024,128]{1,0:T(8,128)S(1)}, u32[]{:S(2)}, u32[]{:S(2)}) collective-permute-start(f32[1024,128]{1,0:T(8,128)} %get-tuple-element.31.own_ref.refs_4_), channel_id=1, source_target_pairs={{0,2},{1,3},{4,6},{5,7},{8,10},{9,11},{12,14},{13,15},{16,18},{17,... | collective-permute-start | bytes 1572872 | tf_op jit(solution)/shard_map/ppermute | solution.py:553
  46.4 4.2 %panel_products.2 = (f32[1024,128]{1,0:T(8,128)S(1)}, f32[1024,128]{1,0:T(8,128)S(1)}) custom-call(s32[3]{0:T(128)S(1)} %pad_add_fusion.flags_ref, f32[1024,4,2,128]{3,2,1,0:T(2,128)} %bitcast.19, f32[1024,128]{1,0:T(8,128)S(1)} %copy-done.5, f32[2,1024,128]{2,1,0:T(8,128)S(1)} %collective-permute-done.b_ref.other_ref, f32[1024,128]{1,0:T(8,128)S(1)} %held.3.got_ref.refs_2_, ...), custom_call_target="tpu_custom_call" | custom-call | flops 4000000000 | bytes 1 | tf_op jit(solution)/shard_map/panel_products/pallas_call | solution.py:256
  50.6 3.1 %collective-permute-done.4.value_ref = f32[1024,128]{1,0:T(8,128)S(1)} collective-permute-done((f32[1024,128]{1,0:T(8,128)}, f32[1024,128]{1,0:T(8,128)S(1)}, u32[]{:S(2)}, u32[]{:S(2)}) %collective-permute-start.4) | collective-permute-done | bytes 524320 | tf_op jit(solution)/shard_map/ppermute | solution.py:553
  54.2 4.4 %collective-permute-start.9 = (f32[640,128]{1,0:T(8,128)S(1)}, f32[640,128]{1,0:T(8,128)S(1)}, u32[]{:S(2)}, u32[]{:S(2)}) collective-permute-start(f32[640,128]{1,0:T(8,128)S(1)} %join.5.refs_0_), channel_id=1, source_target_pairs={{0,2},{1,3},{4,6},{5,7},{8,10},{9,11},{12,14},{13,15},{16,18},{17,... | collective-permute-start | bytes 983048 | tf_op jit(solution)/shard_map/ppermute | solution.py:553
  58.7 4.4 %panel_products.3 = (f32[1024,128]{1,0:T(8,128)S(1)}, f32[1024,128]{1,0:T(8,128)S(1)}) custom-call(s32[3]{0:T(128)S(1)} %pad_add_fusion.flags_ref, f32[1024,4,2,128]{3,2,1,0:T(2,128)} %bitcast.20, f32[1024,128]{1,0:T(8,128)} %get-tuple-element.31.own_ref.refs_4_, f32[2,1024,128]{2,1,0:T(8,128)S(1)} %collective-permute-done.b_ref.other_ref, ...), custom_call_target="tpu_custom_call" | custom-call | flops 4000000000 | bytes 1 | tf_op jit(solution)/shard_map/panel_products/pallas_call | solution.py:256
  64.6 3.9 %collective-permute-done.10.got_ref = f32[1024,128]{1,0:T(8,128)} collective-permute-done((f32[1024,128]{1,0:T(8,128)S(1)}, f32[1024,128]{1,0:T(8,128)}, u32[]{:S(2)}, u32[]{:S(2)}) %collective-permute-start.10) | collective-permute-done | bytes 524320 | tf_op jit(solution)/shard_map/ppermute | solution.py:547
  68.5 1.8 %halve.4 = (f32[512,128]{1,0:T(8,128)S(1)}, f32[512,128]{1,0:T(8,128)}) custom-call(s32[1]{0:T(128)} %bitcast.7.flag_ref, f32[1024,128]{1,0:T(8,128)S(1)} %copy-done.3, f32[1024,128]{1,0:T(8,128)} %collective-permute-done.10.got_ref, f32[1024,128]{1,0:T(8,128)S(1)} %get-tuple-element.34.refs_0_), custom_call_target="tpu_custom_call" | custom-call | flops 1 | bytes 1 | tf_op jit(solution)/shard_map/halve/pallas_call | solution.py:112
  70.5 1.8 %collective-permute-start.12 = (f32[512,128]{1,0:T(8,128)}, f32[512,128]{1,0:T(8,128)S(1)}, u32[]{:S(2)}, u32[]{:S(2)}) collective-permute-start(f32[512,128]{1,0:T(8,128)} %get-tuple-element.36), channel_id=1, source_target_pairs={{0,8},{4,12},{8,0},{12,4},{16,24},{20,28},{24,16},{28,20},{1,9},{5... | collective-permute-start | bytes 786440 | tf_op jit(solution)/shard_map/ppermute | solution.py:547
  72.2 5.4 %factor_0.1.refs_0_.in_ref = f32[10,128,128]{2,1,0:T(8,128)S(1)} custom-call(s32[1]{0:T(128)} %bitcast.3.core_ref, f32[640,128]{1,0:T(8,128)S(1)} %broadcast_select_fusion.mine_ref, f32[640,128]{1,0:T(8,128)S(1)} %collective-permute-done.11.twin_ref, f32[512,128]{1,0:T(8,128)S(1)} %get-tuple-element.35.refs_0_.mine_ref), custom_call_target="tpu_custom_call" | custom-call | flops 1 | bytes 1 | tf_op jit(solution)/shard_map/factor_0/pallas_call | solution.py:402
  80.0 1.7 %collective-permute-start.15 = (f32[512,128]{1,0:T(8,128)}, f32[512,128]{1,0:T(8,128)}, u32[]{:S(2)}, u32[]{:S(2)}) collective-permute-start(f32[512,128]{1,0:T(8,128)} %get-tuple-element.41), channel_id=1, source_target_pairs={{0,8},{4,12},{8,0},{12,4},{16,24},{20,28},{24,16},{28,20},{1,9},{5... | collective-permute-start | bytes 786440 | tf_op jit(solution)/shard_map/ppermute | solution.py:547
  81.8 3.4 %collective-permute-start.14 = (f32[256,128]{1,0:T(8,128)S(1)}, f32[256,128]{1,0:T(8,128)S(1)}, u32[]{:S(2)}, u32[]{:S(2)}) collective-permute-start(f32[256,128]{1,0:T(8,128)S(1)} %get-tuple-element.40), channel_id=1, source_target_pairs={{0,16},{4,20},{8,24},{12,28},{16,0},{20,4},{24,8},{28,12},{1,17},{... | collective-permute-start | bytes 393224 | tf_op jit(solution)/shard_map/ppermute | solution.py:547
  85.2 4.9 %factor_1.1.refs_0_.in_ref = f32[10,128,128]{2,1,0:T(8,128)S(1)} custom-call(f32[10,128,128]{2,1,0:T(8,128)S(1)} %factor_0.1.refs_0_.in_ref, f32[256,128]{1,0:T(8,128)S(1)} %get-tuple-element.39.refs_0_.mine_ref), custom_call_target="tpu_custom_call" | custom-call | flops 1 | bytes 1 | tf_op jit(solution)/shard_map/factor_1/pallas_call | solution.py:402
  92.1 2.7 %collective-permute-start.17 = (f32[256,128]{1,0:T(8,128)S(1)}, f32[256,128]{1,0:T(8,128)S(1)}, u32[]{:S(2)}, u32[]{:S(2)}) collective-permute-start(f32[256,128]{1,0:T(8,128)S(1)} %get-tuple-element.43), channel_id=1, source_target_pairs={{0,16},{4,20},{8,24},{12,28},{16,0},{20,4},{24,8},{28,12},{1,17},{... | collective-permute-start | bytes 393224 | tf_op jit(solution)/shard_map/ppermute | solution.py:547
  95.2 5.3 %factor_2.1.refs_0_.in_ref = f32[10,128,128]{2,1,0:T(8,128)S(1)} custom-call(f32[10,128,128]{2,1,0:T(8,128)S(1)} %factor_1.1.refs_0_.in_ref, f32[256,128]{1,0:T(8,128)S(1)} %add.39.refs_0_.mine_ref), custom_call_target="tpu_custom_call" | custom-call | flops 1 | bytes 1 | tf_op jit(solution)/shard_map/factor_2/pallas_call | solution.py:402
  100.5 4.3 %collective-permute-done.17.got_ref = f32[256,128]{1,0:T(8,128)S(1)} collective-permute-done((f32[256,128]{1,0:T(8,128)S(1)}, f32[256,128]{1,0:T(8,128)S(1)}, u32[]{:S(2)}, u32[]{:S(2)}) %collective-permute-start.17) | collective-permute-done | bytes 131104 | tf_op jit(solution)/shard_map/ppermute | solution.py:547
  104.9 2.7 %collective-permute-done.16.got_ref = f32[256,128]{1,0:T(8,128)S(1)} collective-permute-done((f32[256,128]{1,0:T(8,128)S(1)}, f32[256,128]{1,0:T(8,128)S(1)}, u32[]{:S(2)}, u32[]{:S(2)}) %collective-permute-start.16) | collective-permute-done | bytes 131104 | tf_op jit(solution)/shard_map/ppermute | solution.py:547
  107.7 4.2 %factor_3.1.refs_0_.refs_8_.inv_ref = f32[10,128,128]{2,1,0:T(8,128)S(1)} custom-call(f32[10,128,128]{2,1,0:T(8,128)S(1)} %factor_2.1.refs_0_.in_ref, f32[512,128]{1,0:T(8,128)S(1)} %join.6.refs_0_.mine_ref), custom_call_target="tpu_custom_call" | custom-call | flops 1 | bytes 1 | tf_op jit(solution)/shard_map/factor_3/pallas_call | solution.py:402
  111.8 2.0 %collective-permute-start.18 = (f32[512,128]{1,0:T(8,128)S(1)}, f32[512,128]{1,0:T(8,128)S(1)}, u32[]{:S(2)}, u32[]{:S(2)}) collective-permute-start(f32[512,128]{1,0:T(8,128)S(1)} %join.6.refs_0_.mine_ref), channel_id=1, source_target_pairs={{0,8},{4,12},{8,0},{12,4},{16,24},{20,28},{24,16},{28,20},{1,9},{5... | collective-permute-start | bytes 786440 | tf_op jit(solution)/shard_map/ppermute | solution.py:547
  114.1 7.0 %collective-permute-done.18.got_ref = f32[512,128]{1,0:T(8,128)S(1)} collective-permute-done((f32[512,128]{1,0:T(8,128)S(1)}, f32[512,128]{1,0:T(8,128)S(1)}, u32[]{:S(2)}, u32[]{:S(2)}) %collective-permute-start.18) | collective-permute-done | bytes 262176 | tf_op jit(solution)/shard_map/ppermute | solution.py:547
  121.7 5.2 %panel_bases.1 = (f32[4096,128]{1,0:T(8,128)}, bf16[1024,512]{1,0:T(8,128)(2,1)}, bf16[1024,512]{1,0:T(8,128)(2,1)}) custom-call(s32[3]{0:T(128)S(1)} %pad_add_fusion.flags_ref, f32[1024,128]{1,0:T(8,128)S(1)} %copy-done.6, f32[1024,128]{1,0:T(8,128)S(1)} %get-tuple-element.55.refs_1_, f32[1024,128]{1,0:T(8,128)S(1)} %held.3.got_ref.refs_2_, ...), custom_call_target="tpu_custom_call" | custom-call | flops 1 | bytes 1 | tf_op jit(solution)/shard_map/panel_bases/pallas_call | solution.py:457
  128.2 1.6 %collective-permute-start.22 = (f32[1024,128]{1,0:T(8,128)S(1)}, f32[1024,128]{1,0:T(8,128)S(1)}, u32[]{:S(2)}, u32[]{:S(2)}) collective-permute-start(f32[1024,128]{1,0:T(8,128)S(1)} %join.9.h1_ref), channel_id=1, source_target_pairs={{0,4},{4,0},{8,12},{12,8},{16,20},{20,16},{24,28},{28,24},{1,5},{5... | collective-permute-start | bytes 1572872 | tf_op jit(solution)/shard_map/ppermute | solution.py:547
  132.2 5.0 %finish.2 = (f32[512,4,2,128]{3,2,1,0:T(2,128)}, f32[1024,4,2,128]{3,2,1,0:T(2,128)}) custom-call(s32[1]{0:T(128)} %bitcast.2.flag_ref.flags_ref, f32[1024,4,2,128]{3,2,1,0:T(2,128)} %bitcast.21, bf16[1024,512]{1,0:T(8,128)(2,1)S(1)} %copy-done.1, bf16[1024,512]{1,0:T(8,128)(2,1)S(1)} %copy-done.12, f32[10,128,128]{2,1,0:T(8,128)S(1)} %factor_3.1.refs_0_.refs_8_.inv_ref, ...), custom_call_target="tpu_custom_call" | custom-call | flops 5000000000 | bytes 1 | tf_op jit(solution)/shard_map/finish/pallas_call | solution.py:521
  137.2 7.3 %collective-permute-done.22.h1_ref = f32[1024,128]{1,0:T(8,128)S(1)} collective-permute-done((f32[1024,128]{1,0:T(8,128)S(1)}, f32[1024,128]{1,0:T(8,128)S(1)}, u32[]{:S(2)}, u32[]{:S(2)}) %collective-permute-start.22) | collective-permute-done | bytes 524320 | tf_op jit(solution)/shard_map/ppermute | solution.py:547
  144.6 5.0 %finish.3 = (f32[512,4,2,128]{3,2,1,0:T(2,128)}, f32[1024,4,2,128]{3,2,1,0:T(2,128)}) custom-call(s32[1]{0:T(128)} %bitcast.flags_ref, f32[1024,4,2,128]{3,2,1,0:T(2,128)} %bitcast.22, bf16[1024,512]{1,0:T(8,128)(2,1)S(1)} %copy-done.1, bf16[1024,512]{1,0:T(8,128)(2,1)S(1)} %copy-done.12, ...), custom_call_target="tpu_custom_call", output_to_operand_aliasing={{0}: (7, {}), {1}: (8, {})} | custom-call | flops 5000000000 | bytes 1 | tf_op jit(solution)/shard_map/finish/pallas_call | solution.py:521
  (72 shorter events, 22.0 us)
Async XLA Ops:
  2.7 27.0 %copy-start.4 = (f32[1024,128]{1,0:T(8,128)}, f32[1024,128]{1,0:T(8,128)S(1)}, u32[]{:S(2)}) copy-start(f32[1024,128]{1,0:T(8,128)S(1)} %get-tuple-element.27.own_ref.refs_0_) | copy-start | bytes 1572868
  2.7 6.1 %collective-permute-start = (f32[2,1024,128]{2,1,0:T(8,128)S(1)}, f32[2,1024,128]{2,1,0:T(8,128)S(1)}, u32[]{:S(2)}, u32[]{:S(2)}) collective-permute-start(f32[2,1024,128]{2,1,0:T(8,128)S(1)} %get-tuple-element.28.a_ref), channel_id=1, source_target_pairs={{0,1},{1,0},{2,3},{3,2},{4,5},{5,4},{6,7},{7,6},{8,9},{9,8},{10,11... | collective-permute-start | bytes 3145736 | tf_op jit(solution)/shard_map/ppermute | solution.py:547
  4.2 16.2 %collective-permute-start.1 = (f32[1024,128]{1,0:T(8,128)S(1)}, f32[1024,128]{1,0:T(8,128)S(1)}, u32[]{:S(2)}, u32[]{:S(2)}) collective-permute-start(f32[1024,128]{1,0:T(8,128)S(1)} %get-tuple-element.27.own_ref.refs_0_), channel_id=1, source_target_pairs={{0,2},{1,3},{4,6},{5,7},{8,10},{9,11},{12,14},{13,15},{16,18},{17,... | collective-permute-start | bytes 1572872 | tf_op jit(solution)/shard_map/ppermute | solution.py:553
  8.8 1.2 copy-start.11
  11.5 6.3 %collective-permute-start.2 = (f32[320,128]{1,0:T(8,128)S(1)}, f32[320,128]{1,0:T(8,128)S(1)}, u32[]{:S(2)}, u32[]{:S(2)}) collective-permute-start(f32[320,128]{1,0:T(8,128)S(1)} %get-tuple-element.30), channel_id=1, source_target_pairs={{0,4},{4,0},{8,12},{12,8},{16,20},{20,16},{24,28},{28,24},{1,5},{5... | collective-permute-start | bytes 491528 | tf_op jit(solution)/shard_map/ppermute | solution.py:547
  20.4 23.1 %collective-permute-start.3 = (f32[1024,128]{1,0:T(8,128)S(1)}, f32[1024,128]{1,0:T(8,128)S(1)}, u32[]{:S(2)}, u32[]{:S(2)}) collective-permute-start(f32[1024,128]{1,0:T(8,128)S(1)} %held.3.got_ref.refs_2_), channel_id=1, source_target_pairs={{0,1},{1,0},{2,3},{3,2},{4,5},{5,4},{6,7},{7,6},{8,9},{9,8},{10,11... | collective-permute-start | bytes 1572872 | tf_op jit(solution)/shard_map/ppermute | solution.py:547
  20.4 6.6 %collective-permute-start.5 = (f32[320,128]{1,0:T(8,128)S(1)}, f32[320,128]{1,0:T(8,128)S(1)}, u32[]{:S(2)}, u32[]{:S(2)}) collective-permute-start(f32[320,128]{1,0:T(8,128)S(1)} %add.36.refs_0_.mine_ref), channel_id=1, source_target_pairs={{0,8},{4,12},{8,0},{12,4},{16,24},{20,28},{24,16},{28,20},{1,9},{5... | collective-permute-start | bytes 491528 | tf_op jit(solution)/shard_map/ppermute | solution.py:547
  27.1 10.3 %collective-permute-start.6 = (f32[320,128]{1,0:T(8,128)S(1)}, f32[320,128]{1,0:T(8,128)S(1)}, u32[]{:S(2)}, u32[]{:S(2)}) collective-permute-start(f32[320,128]{1,0:T(8,128)S(1)} %add.37.mine_ref), channel_id=1, source_target_pairs={{0,16},{4,20},{8,24},{12,28},{16,0},{20,4},{24,8},{28,12},{1,17},{... | collective-permute-start | bytes 491528 | tf_op jit(solution)/shard_map/ppermute | solution.py:547
  37.4 6.1 %collective-permute-start.7 = (f32[320,128]{1,0:T(8,128)S(1)}, f32[320,128]{1,0:T(8,128)S(1)}, u32[]{:S(2)}, u32[]{:S(2)}) collective-permute-start(f32[320,128]{1,0:T(8,128)S(1)} %add.38.mine_ref), channel_id=1, source_target_pairs={{0,4},{4,0},{8,12},{12,8},{16,20},{20,16},{24,28},{28,24},{1,5},{5... | collective-permute-start | bytes 491528 | tf_op jit(solution)/shard_map/ppermute | solution.py:547
  39.0 14.7 %collective-permute-start.4 = (f32[1024,128]{1,0:T(8,128)}, f32[1024,128]{1,0:T(8,128)S(1)}, u32[]{:S(2)}, u32[]{:S(2)}) collective-permute-start(f32[1024,128]{1,0:T(8,128)} %get-tuple-element.31.own_ref.refs_4_), channel_id=1, source_target_pairs={{0,2},{1,3},{4,6},{5,7},{8,10},{9,11},{12,14},{13,15},{16,18},{17,... | collective-permute-start | bytes 1572872 | tf_op jit(solution)/shard_map/ppermute | solution.py:553
  50.6 3.1 %copy-start.2 = (f32[1024,128]{1,0:T(8,128)}, f32[1024,128]{1,0:T(8,128)S(1)}, u32[]{:S(2)}) copy-start(f32[1024,128]{1,0:T(8,128)S(1)} %get-tuple-element.33.mine_ref) | copy-start | bytes 1572868
  53.7 4.9 %collective-permute-start.8 = (f32[1024,128]{1,0:T(8,128)S(1)}, f32[1024,128]{1,0:T(8,128)}, u32[]{:S(2)}, u32[]{:S(2)}) collective-permute-start(f32[1024,128]{1,0:T(8,128)S(1)} %held.4.got_ref.refs_6_), channel_id=1, source_target_pairs={{0,1},{1,0},{2,3},{3,2},{4,5},{5,4},{6,7},{7,6},{8,9},{9,8},{10,11... | collective-permute-start | bytes 1572872 | tf_op jit(solution)/shard_map/ppermute | solution.py:547
  53.7 14.8 %collective-permute-start.10 = (f32[1024,128]{1,0:T(8,128)S(1)}, f32[1024,128]{1,0:T(8,128)}, u32[]{:S(2)}, u32[]{:S(2)}) collective-permute-start(f32[1024,128]{1,0:T(8,128)S(1)} %get-tuple-element.32.refs_0_), channel_id=1, source_target_pairs={{0,4},{4,0},{8,12},{12,8},{16,20},{20,16},{24,28},{28,24},{1,5},{5... | collective-permute-start | bytes 1572872 | tf_op jit(solution)/shard_map/ppermute | solution.py:547
  54.2 14.3 %copy-start.3 = (f32[1024,128]{1,0:T(8,128)S(1)}, f32[1024,128]{1,0:T(8,128)}, u32[]{:S(2)}) copy-start(f32[1024,128]{1,0:T(8,128)} %copy-done.2) | copy-start | bytes 1572868
  54.2 16.1 %collective-permute-start.9 = (f32[640,128]{1,0:T(8,128)S(1)}, f32[640,128]{1,0:T(8,128)S(1)}, u32[]{:S(2)}, u32[]{:S(2)}) collective-permute-start(f32[640,128]{1,0:T(8,128)S(1)} %join.5.refs_0_), channel_id=1, source_target_pairs={{0,2},{1,3},{4,6},{5,7},{8,10},{9,11},{12,14},{13,15},{16,18},{17,... | collective-permute-start | bytes 983048 | tf_op jit(solution)/shard_map/ppermute | solution.py:553
  63.1 16.2 %collective-permute-start.13 = (f32[1024,128]{1,0:T(8,128)S(1)}, f32[1024,128]{1,0:T(8,128)S(1)}, u32[]{:S(2)}, u32[]{:S(2)}) collective-permute-start(f32[1024,128]{1,0:T(8,128)S(1)} %get-tuple-element.34.refs_0_), channel_id=1, source_target_pairs={{0,4},{4,0},{8,12},{12,8},{16,20},{20,16},{24,28},{28,24},{1,5},{5... | collective-permute-start | bytes 1572872 | tf_op jit(solution)/shard_map/ppermute | solution.py:547
  70.4 1.9 %collective-permute-start.11 = (f32[640,128]{1,0:T(8,128)S(1)}, f32[640,128]{1,0:T(8,128)S(1)}, u32[]{:S(2)}, u32[]{:S(2)}) collective-permute-start(f32[640,128]{1,0:T(8,128)S(1)} %broadcast_select_fusion.mine_ref), channel_id=1, source_target_pairs={{0,1},{1,0},{2,3},{3,2},{4,5},{5,4},{6,7},{7,6},{8,9},{9,8},{10,11... | collective-permute-start | bytes 983048 | tf_op jit(solution)/shard_map/ppermute | solution.py:547
  70.5 11.3 %collective-permute-start.12 = (f32[512,128]{1,0:T(8,128)}, f32[512,128]{1,0:T(8,128)S(1)}, u32[]{:S(2)}, u32[]{:S(2)}) collective-permute-start(f32[512,128]{1,0:T(8,128)} %get-tuple-element.36), channel_id=1, source_target_pairs={{0,8},{4,12},{8,0},{12,4},{16,24},{20,28},{24,16},{28,20},{1,9},{5... | collective-permute-start | bytes 786440 | tf_op jit(solution)/shard_map/ppermute | solution.py:547
  80.0 11.1 %collective-permute-start.15 = (f32[512,128]{1,0:T(8,128)}, f32[512,128]{1,0:T(8,128)}, u32[]{:S(2)}, u32[]{:S(2)}) collective-permute-start(f32[512,128]{1,0:T(8,128)} %get-tuple-element.41), channel_id=1, source_target_pairs={{0,8},{4,12},{8,0},{12,4},{16,24},{20,28},{24,16},{28,20},{1,9},{5... | collective-permute-start | bytes 786440 | tf_op jit(solution)/shard_map/ppermute | solution.py:547
  81.8 13.0 %collective-permute-start.14 = (f32[256,128]{1,0:T(8,128)S(1)}, f32[256,128]{1,0:T(8,128)S(1)}, u32[]{:S(2)}, u32[]{:S(2)}) collective-permute-start(f32[256,128]{1,0:T(8,128)S(1)} %get-tuple-element.40), channel_id=1, source_target_pairs={{0,16},{4,20},{8,24},{12,28},{16,0},{20,4},{24,8},{28,12},{1,17},{... | collective-permute-start | bytes 393224 | tf_op jit(solution)/shard_map/ppermute | solution.py:547
  92.1 12.7 %collective-permute-start.17 = (f32[256,128]{1,0:T(8,128)S(1)}, f32[256,128]{1,0:T(8,128)S(1)}, u32[]{:S(2)}, u32[]{:S(2)}) collective-permute-start(f32[256,128]{1,0:T(8,128)S(1)} %get-tuple-element.43), channel_id=1, source_target_pairs={{0,16},{4,20},{8,24},{12,28},{16,0},{20,4},{24,8},{28,12},{1,17},{... | collective-permute-start | bytes 393224 | tf_op jit(solution)/shard_map/ppermute | solution.py:547
  94.8 12.8 %collective-permute-start.16 = (f32[256,128]{1,0:T(8,128)S(1)}, f32[256,128]{1,0:T(8,128)S(1)}, u32[]{:S(2)}, u32[]{:S(2)}) collective-permute-start(f32[256,128]{1,0:T(8,128)S(1)} %add.39.refs_0_.mine_ref), channel_id=1, source_target_pairs={{0,16},{4,20},{8,24},{12,28},{16,0},{20,4},{24,8},{28,12},{1,17},{... | collective-permute-start | bytes 393224 | tf_op jit(solution)/shard_map/ppermute | solution.py:547
  100.5 21.2 %copy-start.6 = (f32[1024,128]{1,0:T(8,128)S(1)}, f32[1024,128]{1,0:T(8,128)}, u32[]{:S(2)}) copy-start(f32[1024,128]{1,0:T(8,128)} %copy-done.4) | copy-start | bytes 1572868
  100.5 21.2 %copy-start.9 = (f32[1024,128]{1,0:T(8,128)S(1)}, f32[1024,128]{1,0:T(8,128)}, u32[]{:S(2)}) copy-start(f32[1024,128]{1,0:T(8,128)} %copy-done.7) | copy-start | bytes 1572868
  104.8 9.0 %collective-permute-start.19 = (f32[256,128]{1,0:T(8,128)S(1)}, f32[256,128]{1,0:T(8,128)S(1)}, u32[]{:S(2)}, u32[]{:S(2)}) collective-permute-start(f32[256,128]{1,0:T(8,128)S(1)} %add.40.refs_0_.mine_ref), channel_id=1, source_target_pairs={{0,16},{4,20},{8,24},{12,28},{16,0},{20,4},{24,8},{28,12},{1,17},{... | collective-permute-start | bytes 393224 | tf_op jit(solution)/shard_map/ppermute | solution.py:547
  111.8 9.2 %collective-permute-start.18 = (f32[512,128]{1,0:T(8,128)S(1)}, f32[512,128]{1,0:T(8,128)S(1)}, u32[]{:S(2)}, u32[]{:S(2)}) collective-permute-start(f32[512,128]{1,0:T(8,128)S(1)} %join.6.refs_0_.mine_ref), channel_id=1, source_target_pairs={{0,8},{4,12},{8,0},{12,4},{16,24},{20,28},{24,16},{28,20},{1,9},{5... | collective-permute-start | bytes 786440 | tf_op jit(solution)/shard_map/ppermute | solution.py:547
  113.9 13.0 %collective-permute-start.21 = (f32[512,128]{1,0:T(8,128)S(1)}, f32[512,128]{1,0:T(8,128)S(1)}, u32[]{:S(2)}, u32[]{:S(2)}) collective-permute-start(f32[512,128]{1,0:T(8,128)S(1)} %join.7.refs_0_.mine_ref), channel_id=1, source_target_pairs={{0,8},{4,12},{8,0},{12,4},{16,24},{20,28},{24,16},{28,20},{1,9},{5... | collective-permute-start | bytes 786440 | tf_op jit(solution)/shard_map/ppermute | solution.py:547
  121.1 16.2 %collective-permute-start.20 = (f32[1024,128]{1,0:T(8,128)S(1)}, f32[1024,128]{1,0:T(8,128)S(1)}, u32[]{:S(2)}, u32[]{:S(2)}) collective-permute-start(f32[1024,128]{1,0:T(8,128)S(1)} %join.8.refs_9_.h0_ref), channel_id=1, source_target_pairs={{0,4},{4,0},{8,12},{12,8},{16,20},{20,16},{24,28},{28,24},{1,5},{5... | collective-permute-start | bytes 1572872 | tf_op jit(solution)/shard_map/ppermute | solution.py:547
  126.9 1.2 copy-start
  128.2 16.4 %collective-permute-start.22 = (f32[1024,128]{1,0:T(8,128)S(1)}, f32[1024,128]{1,0:T(8,128)S(1)}, u32[]{:S(2)}, u32[]{:S(2)}) collective-permute-start(f32[1024,128]{1,0:T(8,128)S(1)} %join.9.h1_ref), channel_id=1, source_target_pairs={{0,4},{4,0},{8,12},{12,8},{16,20},{20,16},{24,28},{28,24},{1,5},{5... | collective-permute-start | bytes 1572872 | tf_op jit(solution)/shard_map/ppermute | solution.py:547
  129.8 1.2 copy-start.1
  131.0 1.2 copy-start.12
  (4 other events, 3.8 us)

commit v5 on v3

--- a/solution.py
+++ b/solution.py
@@ -579,20 +579,19 @@
         other = swap(own, "cols", cols_n, 1)
         gram, give = panel_gram(jnp.stack([side, core]), own, other)
         gram = add(gram, swap(give, "rows", rows_n, 1))
-        order = gram = add(gram, swap(gram, "rows", rows_n, bits[0]))
-        for bit in bits[1:]:
+        order = (gram,)
+        for bit in bits:
             gram = add(gram, swap(gram, "rows", rows_n, bit))
+        gram = join(gram, swap(gram, "rows", rows_n, 1), side)
 
         flags = jnp.stack([side, core, owner])
         sums, shares = [], []
         for half in range(halves):
-            piece = held(pieces[half], order)
+            piece = held(pieces[half], *order)
             twin = swap(piece, "cols", cols_n, 1)
             share = [slabs[half], other[half], piece, twin]
             give, keep = panel_products(flags, features, *share, gram)
-            if half == 0:
-                gram = join(gram, swap(gram, "rows", rows_n, 1), side)
-            order = give
+            order = (give,)
             shares += share
             steps = sum_steps(keep, swap(give, "rows", rows_n, 1), row, rows_n)
             next(steps)

time: 137 us -> 137 us (level); the launches traced: 136 us -> 134 us
  waiting for transfers between devices: 43.1 us -> 38.2 us
  starting transfers between devices: 31 us -> 35.6 us
  Pallas kernels: 56.6 us -> 53.4 us
  local copies, waits for them, and re-layouts: 3.74 us -> 5.56 us
    ppermute x20, waiting for transfers between devices: 43.1 us -> 36 us  [swap(): return lax.ppermute(value, axis, [(i, i ^ bit) for i in range(size)])]
    ppermute x3, starting transfers between devices: 8.78 us -> 12.2 us  [spread(): lax.ppermute(value, 'cols', [(i, i + span) for i in range(min(span, cols...]
    ppermute x3, waiting for transfers between devices: 0.01 us -> 2.18 us  [spread(): lax.ppermute(value, 'cols', [(i, i + span) for i in range(min(span, cols...]
    unnamed x6 -> x16, local copies, waits for them, and re-layouts: 3.67 us -> 5.49 us
  transfers between devices with their start and end apart: 23 -> 23, of which waited for: 13 -> 13; matrix products, arithmetic and copies ran while one was open for 0% -> 0% of each run, Pallas kernels for 35% -> 34%
where the time goes in v5:
time: 137 us; the launch traced here: 134 us
  Pallas kernels  53.4 us (39%)
  waiting for transfers between devices  38.2 us (28%)
  starting transfers between devices  35.6 us (26%)
  local copies, waits for them, and re-layouts  5.56 us (4%)
    ppermute x20, waiting for transfers between devices, swap(): return lax.ppermute(value, axis, [(i, i ^ bit) for i in range(size)])  36 us
    ppermute x20, starting transfers between devices, swap(): return lax.ppermute(value, axis, [(i, i ^ bit) for i in range(size)])  23.4 us
    pallas_call x4, Pallas kernels, stage_call(): pl.pallas_call(kernel, in_specs=[smem_spec()] * scalars + [vmem_spec()] *...  19.8 us
    ppermute x3, starting transfers between devices, spread(): lax.ppermute(value, 'cols', [(i, i + span) for i in range(min(span, cols...  12.2 us
    pallas_call x2, Pallas kernels, finish(): pl.pallas_call(trailing_kernel, in_specs=[smem_spec(), hbm] + [any_spec()...  11.1 us
    pallas_call x2, Pallas kernels, panel_products(): pl.pallas_call(product_kernel, in_specs=[smem_spec(), pl.BlockSpec(memory...  9.99 us
    unnamed x16, local copies, waits for them, and re-layouts  5.49 us
    pallas_call x1, Pallas kernels, panel_bases(): pl.pallas_call(basis_kernel, grid=(rows // step,), in_specs=[smem_spec()]...  5.34 us
  transfers between devices with their start and end apart: 23, of which 13 were waited for; matrix products, arithmetic and copies ran while one was open for 0% of the time, Pallas kernels for 34%

profile of v5, /device:TPU:0, one launch (start us, length us, event | category | flops | bytes accessed | tf_op | source)
XLA Modules:
  0.0 134.1 jit_solution(8111395811822074569)
XLA Ops:
  0.6 2.0 %own_panel.1 = (f32[1024,128]{1,0:T(8,128)S(1)}, f32[1024,128]{1,0:T(8,128)}, f32[2,1024,128]{2,1,0:T(8,128)S(1)}) custom-call(f32[1024,4,2,128]{3,2,1,0:T(2,128)} %bitcast.18), custom_call_target="tpu_custom_call" | custom-call | flops 2000000000 | bytes 1 | tf_op jit(solution)/shard_map/own_panel/pallas_call | solution.py:62
  3.2 4.4 %collective-permute-start.1 = (f32[1024,128]{1,0:T(8,128)S(1)}, f32[1024,128]{1,0:T(8,128)S(1)}, u32[]{:S(2)}, u32[]{:S(2)}) collective-permute-start(f32[1024,128]{1,0:T(8,128)S(1)} %get-tuple-element.27.own_ref.refs_0_), channel_id=1, source_target_pairs={{0,2},{1,3},{4,6},{5,7},{8,10},{9,11},{12,14},{13,15},{16,18},{17,... | collective-permute-start | bytes 1572872 | tf_op jit(solution)/shard_map/ppermute | solution.py:537
  9.2 1.6 %collective-permute-start.2 = (f32[320,128]{1,0:T(8,128)S(1)}, f32[320,128]{1,0:T(8,128)S(1)}, u32[]{:S(2)}, u32[]{:S(2)}) collective-permute-start(f32[320,128]{1,0:T(8,128)S(1)} %get-tuple-element.30), channel_id=1, source_target_pairs={{0,4},{4,0},{8,12},{12,8},{16,20},{20,16},{24,28},{28,24},{1,5},{5... | collective-permute-start | bytes 491528 | tf_op jit(solution)/shard_map/ppermute | solution.py:531
  10.8 4.8 %collective-permute-done.2.got_ref = f32[320,128]{1,0:T(8,128)S(1)} collective-permute-done((f32[320,128]{1,0:T(8,128)S(1)}, f32[320,128]{1,0:T(8,128)S(1)}, u32[]{:S(2)}, u32[]{:S(2)}) %collective-permute-start.2) | collective-permute-done | bytes 163872 | tf_op jit(solution)/shard_map/ppermute | solution.py:531
  15.6 1.6 %collective-permute-start.5 = (f32[320,128]{1,0:T(8,128)S(1)}, f32[320,128]{1,0:T(8,128)S(1)}, u32[]{:S(2)}, u32[]{:S(2)}) collective-permute-start(f32[320,128]{1,0:T(8,128)S(1)} %add.36.refs_0_.mine_ref), channel_id=1, source_target_pairs={{0,8},{4,12},{8,0},{12,4},{16,24},{20,28},{24,16},{28,20},{1,9},{5... | collective-permute-start | bytes 491528 | tf_op jit(solution)/shard_map/ppermute | solution.py:531
  17.2 2.2 %collective-permute-done.1.value_ref = f32[1024,128]{1,0:T(8,128)S(1)} collective-permute-done((f32[1024,128]{1,0:T(8,128)S(1)}, f32[1024,128]{1,0:T(8,128)S(1)}, u32[]{:S(2)}, u32[]{:S(2)}) %collective-permute-start.1) | collective-permute-done | bytes 524320 | tf_op jit(solution)/shard_map/ppermute | solution.py:537
  19.4 1.7 %collective-permute-done.5.got_ref = f32[320,128]{1,0:T(8,128)S(1)} collective-permute-done((f32[320,128]{1,0:T(8,128)S(1)}, f32[320,128]{1,0:T(8,128)S(1)}, u32[]{:S(2)}, u32[]{:S(2)}) %collective-permute-start.5) | collective-permute-done | bytes 163872 | tf_op jit(solution)/shard_map/ppermute | solution.py:531
  21.2 2.7 %collective-permute-start.6 = (f32[320,128]{1,0:T(8,128)S(1)}, f32[320,128]{1,0:T(8,128)S(1)}, u32[]{:S(2)}, u32[]{:S(2)}) collective-permute-start(f32[320,128]{1,0:T(8,128)S(1)} %add.37.mine_ref), channel_id=1, source_target_pairs={{0,16},{4,20},{8,24},{12,28},{16,0},{20,4},{24,8},{28,12},{1,17},{... | collective-permute-start | bytes 491528 | tf_op jit(solution)/shard_map/ppermute | solution.py:531
  23.8 2.7 %collective-permute-start.4 = (f32[1024,128]{1,0:T(8,128)}, f32[1024,128]{1,0:T(8,128)S(1)}, u32[]{:S(2)}, u32[]{:S(2)}) collective-permute-start(f32[1024,128]{1,0:T(8,128)} %get-tuple-element.31.own_ref.refs_4_), channel_id=1, source_target_pairs={{0,2},{1,3},{4,6},{5,7},{8,10},{9,11},{12,14},{13,15},{16,18},{17,... | collective-permute-start | bytes 1572872 | tf_op jit(solution)/shard_map/ppermute | solution.py:537
  26.6 3.9 %collective-permute-done.6.got_ref = f32[320,128]{1,0:T(8,128)S(1)} collective-permute-done((f32[320,128]{1,0:T(8,128)S(1)}, f32[320,128]{1,0:T(8,128)S(1)}, u32[]{:S(2)}, u32[]{:S(2)}) %collective-permute-start.6) | collective-permute-done | bytes 163872 | tf_op jit(solution)/shard_map/ppermute | solution.py:531
  32.2 3.7 %collective-permute-done.7.got_ref = f32[320,128]{1,0:T(8,128)S(1)} collective-permute-done((f32[320,128]{1,0:T(8,128)S(1)}, f32[320,128]{1,0:T(8,128)S(1)}, u32[]{:S(2)}, u32[]{:S(2)}) %collective-permute-start.7) | collective-permute-done | bytes 163872 | tf_op jit(solution)/shard_map/ppermute | solution.py:531
  37.0 4.9 %panel_products.2 = (f32[1024,128]{1,0:T(8,128)S(1)}, f32[1024,128]{1,0:T(8,128)S(1)}) custom-call(s32[3]{0:T(128)S(1)} %pad_add_fusion.flags_ref, f32[1024,4,2,128]{3,2,1,0:T(2,128)} %bitcast.19, f32[1024,128]{1,0:T(8,128)S(1)} %copy-done.5, f32[1024,128]{1,0:T(8,128)S(1)} %get-tuple-element.55.other_ref.refs_1_, f32[1024,128]{1,0:T(8,128)S(1)} %held.3.got_ref.refs_2_, ...), custom_call_target="tpu_custom_call" | custom-call | flops 4000000000 | bytes 1 | tf_op jit(solution)/shard_map/panel_products/pallas_call | solution.py:241
  44.2 5.1 %collective-permute-start.9 = (f32[640,128]{1,0:T(8,128)S(1)}, f32[640,128]{1,0:T(8,128)S(1)}, u32[]{:S(2)}, u32[]{:S(2)}) collective-permute-start(f32[640,128]{1,0:T(8,128)S(1)} %join.5.refs_0_), channel_id=1, source_target_pairs={{0,2},{1,3},{4,6},{5,7},{8,10},{9,11},{12,14},{13,15},{16,18},{17,... | collective-permute-start | bytes 983048 | tf_op jit(solution)/shard_map/ppermute | solution.py:537
  49.4 5.1 %panel_products.3 = (f32[1024,128]{1,0:T(8,128)S(1)}, f32[1024,128]{1,0:T(8,128)S(1)}) custom-call(s32[3]{0:T(128)S(1)} %pad_add_fusion.flags_ref, f32[1024,4,2,128]{3,2,1,0:T(2,128)} %bitcast.20, f32[1024,128]{1,0:T(8,128)} %get-tuple-element.31.own_ref.refs_4_, f32[1024,128]{1,0:T(8,128)S(1)} %get-tuple-element.54.other_ref.refs_5_, ...), custom_call_target="tpu_custom_call" | custom-call | flops 4000000000 | bytes 1 | tf_op jit(solution)/shard_map/panel_products/pallas_call | solution.py:241
  55.0 2.1 %collective-permute-done.10.got_ref = f32[1024,128]{1,0:T(8,128)} collective-permute-done((f32[1024,128]{1,0:T(8,128)S(1)}, f32[1024,128]{1,0:T(8,128)}, u32[]{:S(2)}, u32[]{:S(2)}) %collective-permute-start.10) | collective-permute-done | bytes 524320 | tf_op jit(solution)/shard_map/ppermute | solution.py:531
  57.2 1.8 %halve.4 = (f32[512,128]{1,0:T(8,128)S(1)}, f32[512,128]{1,0:T(8,128)}) custom-call(s32[1]{0:T(128)} %bitcast.7.flag_ref, f32[1024,128]{1,0:T(8,128)S(1)} %copy-done.3, f32[1024,128]{1,0:T(8,128)} %collective-permute-done.10.got_ref, f32[1024,128]{1,0:T(8,128)S(1)} %get-tuple-element.34.refs_0_), custom_call_target="tpu_custom_call" | custom-call | flops 1 | bytes 1 | tf_op jit(solution)/shard_map/halve/pallas_call | solution.py:112
  60.7 5.4 %factor_0.1.refs_0_.in_ref = f32[10,128,128]{2,1,0:T(8,128)S(1)} custom-call(s32[1]{0:T(128)} %bitcast.3.core_ref, f32[640,128]{1,0:T(8,128)S(1)} %broadcast_select_fusion.mine_ref, f32[640,128]{1,0:T(8,128)S(1)} %collective-permute-done.11.twin_ref, f32[512,128]{1,0:T(8,128)S(1)} %get-tuple-element.35.refs_0_.mine_ref), custom_call_target="tpu_custom_call" | custom-call | flops 1 | bytes 1 | tf_op jit(solution)/shard_map/factor_0/pallas_call | solution.py:386
  66.2 2.1 %collective-permute-done.13.got_ref = f32[1024,128]{1,0:T(8,128)S(1)} collective-permute-done((f32[1024,128]{1,0:T(8,128)S(1)}, f32[1024,128]{1,0:T(8,128)S(1)}, u32[]{:S(2)}, u32[]{:S(2)}) %collective-permute-start.13) | collective-permute-done | bytes 524320 | tf_op jit(solution)/shard_map/ppermute | solution.py:531
  70.2 3.4 %collective-permute-start.14 = (f32[256,128]{1,0:T(8,128)S(1)}, f32[256,128]{1,0:T(8,128)S(1)}, u32[]{:S(2)}, u32[]{:S(2)}) collective-permute-start(f32[256,128]{1,0:T(8,128)S(1)} %get-tuple-element.40), channel_id=1, source_target_pairs={{0,16},{4,20},{8,24},{12,28},{16,0},{20,4},{24,8},{28,12},{1,17},{... | collective-permute-start | bytes 393224 | tf_op jit(solution)/shard_map/ppermute | solution.py:531
  73.6 4.9 %factor_1.1.refs_0_.in_ref = f32[10,128,128]{2,1,0:T(8,128)S(1)} custom-call(f32[10,128,128]{2,1,0:T(8,128)S(1)} %factor_0.1.refs_0_.in_ref, f32[256,128]{1,0:T(8,128)S(1)} %get-tuple-element.39.refs_0_.mine_ref), custom_call_target="tpu_custom_call" | custom-call | flops 1 | bytes 1 | tf_op jit(solution)/shard_map/factor_1/pallas_call | solution.py:386
  80.5 2.1 %collective-permute-start.17 = (f32[256,128]{1,0:T(8,128)S(1)}, f32[256,128]{1,0:T(8,128)S(1)}, u32[]{:S(2)}, u32[]{:S(2)}) collective-permute-start(f32[256,128]{1,0:T(8,128)S(1)} %get-tuple-element.43), channel_id=1, source_target_pairs={{0,16},{4,20},{8,24},{12,28},{16,0},{20,4},{24,8},{28,12},{1,17},{... | collective-permute-start | bytes 393224 | tf_op jit(solution)/shard_map/ppermute | solution.py:531
  83.6 5.3 %factor_2.1.refs_0_.in_ref = f32[10,128,128]{2,1,0:T(8,128)S(1)} custom-call(f32[10,128,128]{2,1,0:T(8,128)S(1)} %factor_1.1.refs_0_.in_ref, f32[256,128]{1,0:T(8,128)S(1)} %add.39.refs_0_.mine_ref), custom_call_target="tpu_custom_call" | custom-call | flops 1 | bytes 1 | tf_op jit(solution)/shard_map/factor_2/pallas_call | solution.py:386
  88.9 4.0 %collective-permute-done.17.got_ref = f32[256,128]{1,0:T(8,128)S(1)} collective-permute-done((f32[256,128]{1,0:T(8,128)S(1)}, f32[256,128]{1,0:T(8,128)S(1)}, u32[]{:S(2)}, u32[]{:S(2)}) %collective-permute-start.17) | collective-permute-done | bytes 131104 | tf_op jit(solution)/shard_map/ppermute | solution.py:531
  93.0 2.7 %collective-permute-done.16.got_ref = f32[256,128]{1,0:T(8,128)S(1)} collective-permute-done((f32[256,128]{1,0:T(8,128)S(1)}, f32[256,128]{1,0:T(8,128)S(1)}, u32[]{:S(2)}, u32[]{:S(2)}) %collective-permute-start.16) | collective-permute-done | bytes 131104 | tf_op jit(solution)/shard_map/ppermute | solution.py:531
  95.7 1.7 %collective-permute-start.18 = (f32[512,128]{1,0:T(8,128)S(1)}, f32[512,128]{1,0:T(8,128)S(1)}, u32[]{:S(2)}, u32[]{:S(2)}) collective-permute-start(f32[512,128]{1,0:T(8,128)S(1)} %join.6.refs_0_.mine_ref), channel_id=1, source_target_pairs={{0,8},{4,12},{8,0},{12,4},{16,24},{20,28},{24,16},{28,20},{1,9},{5... | collective-permute-start | bytes 786440 | tf_op jit(solution)/shard_map/ppermute | solution.py:531
  97.4 4.2 %factor_3.1.refs_0_.refs_8_.inv_ref = f32[10,128,128]{2,1,0:T(8,128)S(1)} custom-call(f32[10,128,128]{2,1,0:T(8,128)S(1)} %factor_2.1.refs_0_.in_ref, f32[512,128]{1,0:T(8,128)S(1)} %join.6.refs_0_.mine_ref), custom_call_target="tpu_custom_call" | custom-call | flops 1 | bytes 1 | tf_op jit(solution)/shard_map/factor_3/pallas_call | solution.py:386
  102.1 3.4 %collective-permute-done.18.got_ref = f32[512,128]{1,0:T(8,128)S(1)} collective-permute-done((f32[512,128]{1,0:T(8,128)S(1)}, f32[512,128]{1,0:T(8,128)S(1)}, u32[]{:S(2)}, u32[]{:S(2)}) %collective-permute-start.18) | collective-permute-done | bytes 262176 | tf_op jit(solution)/shard_map/ppermute | solution.py:531
  105.5 2.2 %collective-permute-start.20 = (f32[1024,128]{1,0:T(8,128)S(1)}, f32[1024,128]{1,0:T(8,128)}, u32[]{:S(2)}, u32[]{:S(2)}) collective-permute-start(f32[1024,128]{1,0:T(8,128)S(1)} %join.8.refs_9_.h0_ref), channel_id=1, source_target_pairs={{0,4},{4,0},{8,12},{12,8},{16,20},{20,16},{24,28},{28,24},{1,5},{5... | collective-permute-start | bytes 1572872 | tf_op jit(solution)/shard_map/ppermute | solution.py:531
  107.7 5.3 %panel_bases.1 = (f32[4096,128]{1,0:T(8,128)}, bf16[1024,512]{1,0:T(8,128)(2,1)}, bf16[1024,512]{1,0:T(8,128)(2,1)}) custom-call(s32[3]{0:T(128)S(1)} %pad_add_fusion.flags_ref, f32[1024,128]{1,0:T(8,128)S(1)} %copy-done.6, f32[1024,128]{1,0:T(8,128)S(1)} %get-tuple-element.55.other_ref.refs_1_, f32[1024,128]{1,0:T(8,128)S(1)} %held.3.got_ref.refs_2_, ...), custom_call_target="tpu_custom_call" | custom-call | flops 1 | bytes 1 | tf_op jit(solution)/shard_map/panel_bases/pallas_call | solution.py:441
  116.9 5.0 %finish.2 = (f32[512,4,2,128]{3,2,1,0:T(2,128)}, f32[1024,4,2,128]{3,2,1,0:T(2,128)}) custom-call(s32[1]{0:T(128)} %bitcast.2.flag_ref.flags_ref, f32[1024,4,2,128]{3,2,1,0:T(2,128)} %bitcast.21, bf16[1024,512]{1,0:T(8,128)(2,1)S(1)} %copy-done.1, bf16[1024,512]{1,0:T(8,128)(2,1)S(1)} %copy-done.7, f32[10,128,128]{2,1,0:T(8,128)S(1)} %factor_3.1.refs_0_.refs_8_.inv_ref, ...), custom_call_target="tpu_custom_call" | custom-call | flops 5000000000 | bytes 1 | tf_op jit(solution)/shard_map/finish/pallas_call | solution.py:505
  121.9 5.9 %collective-permute-done.22.h1_ref = f32[1024,128]{1,0:T(8,128)S(1)} collective-permute-done((f32[1024,128]{1,0:T(8,128)S(1)}, f32[1024,128]{1,0:T(8,128)S(1)}, u32[]{:S(2)}, u32[]{:S(2)}) %collective-permute-start.22) | collective-permute-done | bytes 524320 | tf_op jit(solution)/shard_map/ppermute | solution.py:531
  127.9 6.1 %finish.3 = (f32[512,4,2,128]{3,2,1,0:T(2,128)}, f32[1024,4,2,128]{3,2,1,0:T(2,128)}) custom-call(s32[1]{0:T(128)} %bitcast.flags_ref, f32[1024,4,2,128]{3,2,1,0:T(2,128)} %bitcast.22, bf16[1024,512]{1,0:T(8,128)(2,1)S(1)} %copy-done.1, bf16[1024,512]{1,0:T(8,128)(2,1)S(1)} %copy-done.7, ...), custom_call_target="tpu_custom_call", output_to_operand_aliasing={{0}: (7, {}), {1}: (8, {})} | custom-call | flops 5000000000 | bytes 1 | tf_op jit(solution)/shard_map/finish/pallas_call | solution.py:505
  (62 shorter events, 18.8 us)
Async XLA Ops:
  2.7 21.2 %copy-start.4 = (f32[1024,128]{1,0:T(8,128)}, f32[1024,128]{1,0:T(8,128)S(1)}, u32[]{:S(2)}) copy-start(f32[1024,128]{1,0:T(8,128)S(1)} %get-tuple-element.27.own_ref.refs_0_) | copy-start | bytes 1572868
  2.7 5.1 %collective-permute-start = (f32[2,1024,128]{2,1,0:T(8,128)S(1)}, f32[2,1024,128]{2,1,0:T(8,128)S(1)}, u32[]{:S(2)}, u32[]{:S(2)}) collective-permute-start(f32[2,1024,128]{2,1,0:T(8,128)S(1)} %get-tuple-element.28.a_ref), channel_id=1, source_target_pairs={{0,1},{1,0},{2,3},{3,2},{4,5},{5,4},{6,7},{7,6},{8,9},{9,8},{10,11... | collective-permute-start | bytes 3145736 | tf_op jit(solution)/shard_map/ppermute | solution.py:531
  3.2 16.2 %collective-permute-start.1 = (f32[1024,128]{1,0:T(8,128)S(1)}, f32[1024,128]{1,0:T(8,128)S(1)}, u32[]{:S(2)}, u32[]{:S(2)}) collective-permute-start(f32[1024,128]{1,0:T(8,128)S(1)} %get-tuple-element.27.own_ref.refs_0_), channel_id=1, source_target_pairs={{0,2},{1,3},{4,6},{5,7},{8,10},{9,11},{12,14},{13,15},{16,18},{17,... | collective-permute-start | bytes 1572872 | tf_op jit(solution)/shard_map/ppermute | solution.py:537
  9.2 6.4 %collective-permute-start.2 = (f32[320,128]{1,0:T(8,128)S(1)}, f32[320,128]{1,0:T(8,128)S(1)}, u32[]{:S(2)}, u32[]{:S(2)}) collective-permute-start(f32[320,128]{1,0:T(8,128)S(1)} %get-tuple-element.30), channel_id=1, source_target_pairs={{0,4},{4,0},{8,12},{12,8},{16,20},{20,16},{24,28},{28,24},{1,5},{5... | collective-permute-start | bytes 491528 | tf_op jit(solution)/shard_map/ppermute | solution.py:531
  15.6 5.5 %collective-permute-start.5 = (f32[320,128]{1,0:T(8,128)S(1)}, f32[320,128]{1,0:T(8,128)S(1)}, u32[]{:S(2)}, u32[]{:S(2)}) collective-permute-start(f32[320,128]{1,0:T(8,128)S(1)} %add.36.refs_0_.mine_ref), channel_id=1, source_target_pairs={{0,8},{4,12},{8,0},{12,4},{16,24},{20,28},{24,16},{28,20},{1,9},{5... | collective-permute-start | bytes 491528 | tf_op jit(solution)/shard_map/ppermute | solution.py:531
  19.4 16.6 %collective-permute-start.3 = (f32[1024,128]{1,0:T(8,128)S(1)}, f32[1024,128]{1,0:T(8,128)}, u32[]{:S(2)}, u32[]{:S(2)}) collective-permute-start(f32[1024,128]{1,0:T(8,128)S(1)} %held.3.got_ref.refs_2_), channel_id=1, source_target_pairs={{0,1},{1,0},{2,3},{3,2},{4,5},{5,4},{6,7},{7,6},{8,9},{9,8},{10,11... | collective-permute-start | bytes 1572872 | tf_op jit(solution)/shard_map/ppermute | solution.py:531
  21.2 9.4 %collective-permute-start.6 = (f32[320,128]{1,0:T(8,128)S(1)}, f32[320,128]{1,0:T(8,128)S(1)}, u32[]{:S(2)}, u32[]{:S(2)}) collective-permute-start(f32[320,128]{1,0:T(8,128)S(1)} %add.37.mine_ref), channel_id=1, source_target_pairs={{0,16},{4,20},{8,24},{12,28},{16,0},{20,4},{24,8},{28,12},{1,17},{... | collective-permute-start | bytes 491528 | tf_op jit(solution)/shard_map/ppermute | solution.py:531
  23.8 18.1 %collective-permute-start.4 = (f32[1024,128]{1,0:T(8,128)}, f32[1024,128]{1,0:T(8,128)S(1)}, u32[]{:S(2)}, u32[]{:S(2)}) collective-permute-start(f32[1024,128]{1,0:T(8,128)} %get-tuple-element.31.own_ref.refs_4_), channel_id=1, source_target_pairs={{0,2},{1,3},{4,6},{5,7},{8,10},{9,11},{12,14},{13,15},{16,18},{17,... | collective-permute-start | bytes 1572872 | tf_op jit(solution)/shard_map/ppermute | solution.py:537
  30.6 5.4 %collective-permute-start.7 = (f32[320,128]{1,0:T(8,128)S(1)}, f32[320,128]{1,0:T(8,128)S(1)}, u32[]{:S(2)}, u32[]{:S(2)}) collective-permute-start(f32[320,128]{1,0:T(8,128)S(1)} %add.38.mine_ref), channel_id=1, source_target_pairs={{0,4},{4,0},{8,12},{12,8},{16,20},{20,16},{24,28},{28,24},{1,5},{5... | collective-permute-start | bytes 491528 | tf_op jit(solution)/shard_map/ppermute | solution.py:531
  36.0 1.0 copy-start.5
  41.9 0.8 copy-start.2
  42.7 6.6 %collective-permute-start.8 = (f32[1024,128]{1,0:T(8,128)S(1)}, f32[1024,128]{1,0:T(8,128)}, u32[]{:S(2)}, u32[]{:S(2)}) collective-permute-start(f32[1024,128]{1,0:T(8,128)S(1)} %held.4.got_ref.refs_6_), channel_id=1, source_target_pairs={{0,1},{1,0},{2,3},{3,2},{4,5},{5,4},{6,7},{7,6},{8,9},{9,8},{10,11... | collective-permute-start | bytes 1572872 | tf_op jit(solution)/shard_map/ppermute | solution.py:531
  42.7 14.4 %collective-permute-start.10 = (f32[1024,128]{1,0:T(8,128)S(1)}, f32[1024,128]{1,0:T(8,128)}, u32[]{:S(2)}, u32[]{:S(2)}) collective-permute-start(f32[1024,128]{1,0:T(8,128)S(1)} %get-tuple-element.32.refs_0_), channel_id=1, source_target_pairs={{0,4},{4,0},{8,12},{12,8},{16,20},{20,16},{24,28},{28,24},{1,5},{5... | collective-permute-start | bytes 1572872 | tf_op jit(solution)/shard_map/ppermute | solution.py:531
  44.2 14.7 %collective-permute-start.9 = (f32[640,128]{1,0:T(8,128)S(1)}, f32[640,128]{1,0:T(8,128)S(1)}, u32[]{:S(2)}, u32[]{:S(2)}) collective-permute-start(f32[640,128]{1,0:T(8,128)S(1)} %join.5.refs_0_), channel_id=1, source_target_pairs={{0,2},{1,3},{4,6},{5,7},{8,10},{9,11},{12,14},{13,15},{16,18},{17,... | collective-permute-start | bytes 983048 | tf_op jit(solution)/shard_map/ppermute | solution.py:537
  49.3 7.8 %copy-start.3 = (f32[1024,128]{1,0:T(8,128)S(1)}, f32[1024,128]{1,0:T(8,128)}, u32[]{:S(2)}) copy-start(f32[1024,128]{1,0:T(8,128)} %copy-done.2) | copy-start | bytes 1572868
  54.5 13.8 %collective-permute-start.13 = (f32[1024,128]{1,0:T(8,128)S(1)}, f32[1024,128]{1,0:T(8,128)S(1)}, u32[]{:S(2)}, u32[]{:S(2)}) collective-permute-start(f32[1024,128]{1,0:T(8,128)S(1)} %get-tuple-element.34.refs_0_), channel_id=1, source_target_pairs={{0,4},{4,0},{8,12},{12,8},{16,20},{20,16},{24,28},{28,24},{1,5},{5... | collective-permute-start | bytes 1572872 | tf_op jit(solution)/shard_map/ppermute | solution.py:531
  59.0 1.7 %collective-permute-start.11 = (f32[640,128]{1,0:T(8,128)S(1)}, f32[640,128]{1,0:T(8,128)S(1)}, u32[]{:S(2)}, u32[]{:S(2)}) collective-permute-start(f32[640,128]{1,0:T(8,128)S(1)} %broadcast_select_fusion.mine_ref), channel_id=1, source_target_pairs={{0,1},{1,0},{2,3},{3,2},{4,5},{5,4},{6,7},{7,6},{8,9},{9,8},{10,11... | collective-permute-start | bytes 983048 | tf_op jit(solution)/shard_map/ppermute | solution.py:531
  59.1 11.0 %collective-permute-start.12 = (f32[512,128]{1,0:T(8,128)}, f32[512,128]{1,0:T(8,128)S(1)}, u32[]{:S(2)}, u32[]{:S(2)}) collective-permute-start(f32[512,128]{1,0:T(8,128)} %get-tuple-element.36), channel_id=1, source_target_pairs={{0,8},{4,12},{8,0},{12,4},{16,24},{20,28},{24,16},{28,20},{1,9},{5... | collective-permute-start | bytes 786440 | tf_op jit(solution)/shard_map/ppermute | solution.py:531
  69.1 10.4 %collective-permute-start.15 = (f32[512,128]{1,0:T(8,128)}, f32[512,128]{1,0:T(8,128)}, u32[]{:S(2)}, u32[]{:S(2)}) collective-permute-start(f32[512,128]{1,0:T(8,128)} %get-tuple-element.41), channel_id=1, source_target_pairs={{0,8},{4,12},{8,0},{12,4},{16,24},{20,28},{24,16},{28,20},{1,9},{5... | collective-permute-start | bytes 786440 | tf_op jit(solution)/shard_map/ppermute | solution.py:531
  70.2 12.4 %collective-permute-start.14 = (f32[256,128]{1,0:T(8,128)S(1)}, f32[256,128]{1,0:T(8,128)S(1)}, u32[]{:S(2)}, u32[]{:S(2)}) collective-permute-start(f32[256,128]{1,0:T(8,128)S(1)} %get-tuple-element.40), channel_id=1, source_target_pairs={{0,16},{4,20},{8,24},{12,28},{16,0},{20,4},{24,8},{28,12},{1,17},{... | collective-permute-start | bytes 393224 | tf_op jit(solution)/shard_map/ppermute | solution.py:531
  78.5 29.3 %copy-start.6 = (f32[1024,128]{1,0:T(8,128)S(1)}, f32[1024,128]{1,0:T(8,128)}, u32[]{:S(2)}) copy-start(f32[1024,128]{1,0:T(8,128)} %copy-done.4) | copy-start | bytes 1572868
  80.5 12.4 %collective-permute-start.17 = (f32[256,128]{1,0:T(8,128)S(1)}, f32[256,128]{1,0:T(8,128)S(1)}, u32[]{:S(2)}, u32[]{:S(2)}) collective-permute-start(f32[256,128]{1,0:T(8,128)S(1)} %get-tuple-element.43), channel_id=1, source_target_pairs={{0,16},{4,20},{8,24},{12,28},{16,0},{20,4},{24,8},{28,12},{1,17},{... | collective-permute-start | bytes 393224 | tf_op jit(solution)/shard_map/ppermute | solution.py:531
  82.6 13.1 %collective-permute-start.16 = (f32[256,128]{1,0:T(8,128)S(1)}, f32[256,128]{1,0:T(8,128)S(1)}, u32[]{:S(2)}, u32[]{:S(2)}) collective-permute-start(f32[256,128]{1,0:T(8,128)S(1)} %add.39.refs_0_.mine_ref), channel_id=1, source_target_pairs={{0,16},{4,20},{8,24},{12,28},{16,0},{20,4},{24,8},{28,12},{1,17},{... | collective-permute-start | bytes 393224 | tf_op jit(solution)/shard_map/ppermute | solution.py:531
  92.9 8.7 %collective-permute-start.19 = (f32[256,128]{1,0:T(8,128)S(1)}, f32[256,128]{1,0:T(8,128)S(1)}, u32[]{:S(2)}, u32[]{:S(2)}) collective-permute-start(f32[256,128]{1,0:T(8,128)S(1)} %add.40.refs_0_.mine_ref), channel_id=1, source_target_pairs={{0,16},{4,20},{8,24},{12,28},{16,0},{20,4},{24,8},{28,12},{1,17},{... | collective-permute-start | bytes 393224 | tf_op jit(solution)/shard_map/ppermute | solution.py:531
  95.7 9.8 %collective-permute-start.18 = (f32[512,128]{1,0:T(8,128)S(1)}, f32[512,128]{1,0:T(8,128)S(1)}, u32[]{:S(2)}, u32[]{:S(2)}) collective-permute-start(f32[512,128]{1,0:T(8,128)S(1)} %join.6.refs_0_.mine_ref), channel_id=1, source_target_pairs={{0,8},{4,12},{8,0},{12,4},{16,24},{20,28},{24,16},{28,20},{1,9},{5... | collective-permute-start | bytes 786440 | tf_op jit(solution)/shard_map/ppermute | solution.py:531
  101.6 11.4 %collective-permute-start.21 = (f32[512,128]{1,0:T(8,128)S(1)}, f32[512,128]{1,0:T(8,128)S(1)}, u32[]{:S(2)}, u32[]{:S(2)}) collective-permute-start(f32[512,128]{1,0:T(8,128)S(1)} %join.7.refs_0_.mine_ref), channel_id=1, source_target_pairs={{0,8},{4,12},{8,0},{12,4},{16,24},{20,28},{24,16},{28,20},{1,9},{5... | collective-permute-start | bytes 786440 | tf_op jit(solution)/shard_map/ppermute | solution.py:531
  105.5 16.4 %collective-permute-start.20 = (f32[1024,128]{1,0:T(8,128)S(1)}, f32[1024,128]{1,0:T(8,128)}, u32[]{:S(2)}, u32[]{:S(2)}) collective-permute-start(f32[1024,128]{1,0:T(8,128)S(1)} %join.8.refs_9_.h0_ref), channel_id=1, source_target_pairs={{0,4},{4,0},{8,12},{12,8},{16,20},{20,16},{24,28},{28,24},{1,5},{5... | collective-permute-start | bytes 1572872 | tf_op jit(solution)/shard_map/ppermute | solution.py:531
  113.1 1.2 copy-start
  114.4 13.5 %collective-permute-start.22 = (f32[1024,128]{1,0:T(8,128)S(1)}, f32[1024,128]{1,0:T(8,128)S(1)}, u32[]{:S(2)}, u32[]{:S(2)}) collective-permute-start(f32[1024,128]{1,0:T(8,128)S(1)} %join.9.h1_ref), channel_id=1, source_target_pairs={{0,4},{4,0},{8,12},{12,8},{16,20},{20,16},{24,28},{28,24},{1,5},{5... | collective-permute-start | bytes 1572872 | tf_op jit(solution)/shard_map/ppermute | solution.py:531
  114.5 1.2 copy-start.1
  115.7 1.2 copy-start.7
